TPU v7x, 32 devices: a whole 2x2x4 slice. The times are simulated.
32 devices in a mesh: groups: 2 (over y), row: 4 (over z), col: 4 (over x, core).
Axes of the slice: x: 2, y: 2, z: 4, core: 2. Of those that a mesh axis runs over, the one named last changes fastest.
Arguments:
- features: bfloat16 [4096, 256], P(('groups', 'row', 'col')), parts along dimension 0, may hold values from -6 to 6
- w_self: bfloat16 [256, 256], replicated, may hold values from -0.375 to 0.375
- w_neigh: bfloat16 [256, 256], replicated, may hold values from -0.375 to 0.375
- layer_bias: float32 [256], replicated, may hold values from -4 to 4
- tile_vals: bfloat16 [8, 4, 8, 128, 128], P(('groups', 'row'), 'col'), parts along dimension 0, may hold values from 0 to 2
- tile_dst: int32 [8, 4, 8], P(('groups', 'row'), 'col'), parts along dimension 0, may hold values from 0 to 3, as said below
- tile_src: int32 [8, 4, 8], P(('groups', 'row'), 'col'), parts along dimension 0, may hold values from 0 to 3
- tile_count: int32 [8, 4], P(('groups', 'row'), 'col'), parts along dimension 0, may hold values from 2 to 8, as said below
- degree: int32 [4096], P(('groups', 'row', 'col')), parts along dimension 0, may hold values from 8 to 32
- target_ids: int32 [512], P('groups'), parts along dimension 0, may hold values from 0 to 2047, as said below
- cotangent: bfloat16 [4096, 256], P(('groups', 'row', 'col')), parts along dimension 0, may hold values from -6 to 6
Outputs:
- hidden: bfloat16 [4096, 256], P(('groups', 'row', 'col')), parts along dimension 0
- grad_features: bfloat16 [4096, 256], P(('groups', 'row', 'col')), parts along dimension 0
- grad_self: float32 [512, 256], P('groups'), parts along dimension 0
- grad_neigh: float32 [512, 256], P('groups'), parts along dimension 0
- grad_bias: float32 [512], P('groups'), parts along dimension 0
There are 2 independent parts, one for each index of `groups`. A program takes and returns all parts, laid end to end along the dimension named above; an argument that names none is the same for every part. Nothing has to cross between parts.
Inputs may be any that keep to these rules, and one draw needn't show every extreme that they name: Within one grid cell the 8 pairs (tile_dst, tile_src) are all different. Slots at or beyond tile_count of their cell are not part of the graph; some cell uses all 8 slots. `target_ids`: distinct node numbers.
All inputs are finite; a program needn't handle non-finite values.
Results may differ from a plain program's by a relative error of at most 0.0055.
Values may be sent and summed in bfloat16 or wider, within the bound.
No kernel may reach another device: no remote copies, remote signals or barrier semaphores. Data moves between devices by JAX's collectives and lax.ppermute only.
A program may use at most 64 MiB of HBM per device.

v0:
```python
import math

import jax
import jax.numpy as jnp
from jax import lax
from jax.sharding import PartitionSpec as P


def gelu_value(inputs):
    return 0.5 * inputs * (1.0 + jax.scipy.special.erf(inputs * 0.7071067811865476))


def gelu_slope(inputs):
    return (
        0.5 * (1.0 + jax.scipy.special.erf(inputs * 0.7071067811865476))
        + inputs * jnp.exp(-0.5 * inputs * inputs) * 0.3989422804014327
    )


def tile_sum(values, take_index, put_index, usable, source, out_tiles, transpose, first_tile):
    slot_count, tile_width = (values.shape[0], values.shape[1])
    columns = source.shape[1]
    blocks = source.reshape(-1, tile_width, columns)
    group_size = math.gcd(slot_count, 16)
    pattern = "kji,kjf->kif" if transpose else "kij,kjf->kif"

    def advance(running, offset):
        tile_block = lax.dynamic_slice_in_dim(values, offset, group_size, 0)
        taken = lax.dynamic_slice_in_dim(take_index, offset, group_size, 0)
        placed = lax.dynamic_slice_in_dim(put_index, offset, group_size, 0) - first_tile
        allowed = lax.dynamic_slice_in_dim(usable, offset, group_size, 0)
        inside = allowed & (placed >= 0) & (placed < out_tiles)
        chosen = blocks[taken]
        product = jnp.einsum(pattern, tile_block, chosen, preferred_element_type=jnp.float32)
        product = product * inside.astype(jnp.float32)[:, None, None]
        where_to = jnp.where(inside, placed, 0)
        running = running.at[where_to].add(product)
        return (running, None)

    offsets = jnp.arange(0, slot_count, group_size, dtype=jnp.int32)
    running, _ = lax.scan(
        advance, jnp.zeros((out_tiles, tile_width, columns), jnp.float32), offsets
    )
    return running.reshape(out_tiles * tile_width, columns)


def per_device(
    features,
    w_self,
    w_neigh,
    layer_bias,
    tile_vals,
    tile_dst,
    tile_src,
    tile_count,
    degree,
    target_ids,
    cotangent,
):
    row_count = lax.axis_size("row")
    col_count = lax.axis_size("col")
    node_rows = features.shape[0]
    tile_width = tile_vals.shape[-1]
    cell_tiles = tile_vals[0, 0]
    cell_dst = tile_dst[0, 0]
    cell_src = tile_src[0, 0]
    usable = jnp.arange(cell_tiles.shape[0], dtype=jnp.int32) < tile_count[0, 0]
    source = lax.all_gather(features, "row", axis=0, tiled=True)
    partial_value = tile_sum(
        cell_tiles,
        cell_src,
        cell_dst,
        usable,
        source,
        col_count * node_rows // tile_width,
        False,
        0,
    )
    agg_sum = lax.psum_scatter(partial_value, "col", scatter_dimension=0, tiled=True)
    inv_degree = 1.0 / degree.astype(jnp.float32)
    aggregate = (agg_sum * inv_degree[:, None]).astype(jnp.bfloat16)
    before = (
        jnp.dot(features, w_self, preferred_element_type=jnp.float32)
        + jnp.dot(aggregate, w_neigh, preferred_element_type=jnp.float32)
        + layer_bias
    )
    hidden = gelu_value(before).astype(jnp.bfloat16)
    first_node = (lax.axis_index("row") * col_count + lax.axis_index("col")) * node_rows
    node_ids = first_node + jnp.arange(node_rows, dtype=jnp.int32)
    target = jnp.any(node_ids[:, None] == target_ids[None, :], axis=1).astype(jnp.float32)
    slope_grad = (cotangent.astype(jnp.float32) * target[:, None] * gelu_slope(before)).astype(
        jnp.bfloat16
    )
    grad_scale = 1.0 / math.sqrt(node_rows * row_count * col_count)
    contract_rows = (((0,), (0,)), ((), ()))
    self_term = lax.dot_general(
        features, slope_grad, contract_rows, preferred_element_type=jnp.float32
    )
    neigh_term = lax.dot_general(
        aggregate, slope_grad, contract_rows, preferred_element_type=jnp.float32
    )
    bias_term = jnp.sum(slope_grad.astype(jnp.float32), axis=0)
    self_sum, neigh_sum, bias_sum = lax.psum((self_term, neigh_term, bias_term), ("row", "col"))
    contract_out = (((1,), (1,)), ((), ()))
    message = (
        lax.dot_general(slope_grad, w_neigh, contract_out, preferred_element_type=jnp.float32)
        * inv_degree[:, None]
    ).astype(jnp.bfloat16)
    message_slab = lax.all_gather(message, "col", axis=0, tiled=True)
    back_part = tile_sum(
        cell_tiles,
        cell_dst,
        cell_src,
        usable,
        message_slab,
        row_count * node_rows // tile_width,
        True,
        0,
    )
    neighbour_grad = lax.psum_scatter(
        back_part.astype(jnp.bfloat16).astype(jnp.float32).astype(jnp.bfloat16),
        "row",
        scatter_dimension=0,
        tiled=True,
    ).astype(jnp.float32)
    direct = lax.dot_general(slope_grad, w_self, contract_out, preferred_element_type=jnp.float32)
    grad_features = (direct + neighbour_grad).astype(jnp.bfloat16)
    return (
        hidden,
        grad_features,
        self_sum * grad_scale,
        neigh_sum * grad_scale,
        bias_sum * grad_scale,
    )


def solution(mesh):
    in_specs = (
        P(("groups", "row", "col"), None),
        P(),
        P(),
        P(),
        P(("groups", "row"), "col", None, None, None),
        P(("groups", "row"), "col", None),
        P(("groups", "row"), "col", None),
        P(("groups", "row"), "col"),
        P(("groups", "row", "col")),
        P("groups"),
        P(("groups", "row", "col"), None),
    )
    out_specs = (
        P(("groups", "row", "col"), None),
        P(("groups", "row", "col"), None),
        P("groups", None),
        P("groups", None),
        P("groups"),
    )
    return jax.shard_map(
        per_device, mesh=mesh, in_specs=in_specs, out_specs=out_specs, check_vma=False
    )
```

profile of v0, /device:TPU:0, one launch (start us, length us, event | category | flops | bytes accessed | tf_op | source)
XLA Modules:
  0.0 183.5 jit_solution(7378907591326688978)
XLA Ops:
  7.2 0.0 copy-start
  7.2 0.0 reduce-scatter.3.cloned.1.call-start
  7.9 0.0 copy-start.8
  7.9 0.6 copy-done.8
  8.6 0.0 copy-start.9
  8.6 0.7 copy-done.9
  9.3 15.8 %all_gather.6 = bf16[512,256]{1,0:T(8,128)(2,1)S(1)} all-gather(bf16[128,256]{1,0:T(8,128)(2,1)} %param.11), channel_id=1, replica_groups=mesh['groups'=2,'row'=4,'col'=4] {'row'}, dimensions={0}, use_global_device_ids=true | all-gather | bytes 327680 | tf_op jit(solution)/shard_map/all_gather | solution.py:68
  25.1 0.6 gather_fusion
  25.7 0.0 copy-done
  25.7 0.3 fusion.1
  26.0 0.3 copy.29
  26.4 1.3 scatter_fusion
  27.7 0.0 copy-start.1
  27.8 0.0 copy-start.2
  27.8 0.0 copy-start.3
  27.8 0.8 copy-done.1
  28.5 0.0 reduce-scatter.3.cloned.1.call-update
  28.6 0.0 all-reduce.3.cloned.1.call-start
  28.6 0.0 copy-start.7
  28.6 0.7 copy-done.7
  29.3 0.2 compare_reduce_fusion
  29.5 0.0 copy-start.12
  29.5 0.6 copy-done.12
  30.2 0.0 copy-done.2
  30.2 0.0 copy-done.3
  30.2 0.0 copy-start.5
  30.2 0.0 copy-start.10
  30.2 0.0 copy-start.11
  30.2 0.2 fusion.21
  30.4 21.6 %reduce-scatter.3.cloned.1.call-done = f32[128,256]{1,0:T(8,128)} async-done(((f32[512,256]{1,0:T(8,128)}), f32[128,256]{1,0:T(8,128)}) %reduce-scatter.3.cloned.1.call-update) | async-done | bytes 131088 | tf_op jit(solution)/shard_map/reduce_scatter | solution.py:79
  51.9 0.0 copy-done.5
  51.9 0.0 copy-done.10
  51.9 0.0 copy-done.11
  51.9 1.8 convert_reduce_fusion
  53.8 0.2 fusion.4
  54.0 0.9 convolution_bitcast_fusion
  54.9 5.8 %all_gather.7 = bf16[512,256]{1,0:T(8,128)(2,1)S(1)} all-gather(bf16[128,256]{1,0:T(8,128)(2,1)S(1)} %fusion.4), channel_id=1, replica_groups=mesh['groups'=2,'row'=4,'col'=4] {'col'}, dimensions={0}, use_global_device_ids=true | all-gather | bytes 327680 | tf_op jit(solution)/shard_map/all_gather | solution.py:109
  60.6 0.0 copy-start.6
  60.6 0.6 gather_fusion.1
  61.2 0.3 copy-done.6
  61.6 1.0 fusion.19
  62.5 0.0 all-reduce.3.cloned.1.call-update
  62.5 0.0 reduce-scatter.5.cloned.1.call-start
  62.6 0.3 fusion
  62.9 0.3 copy.31
  63.3 1.3 scatter_fusion.1
  64.6 0.7 convert_element_type.67
  65.4 32.9 %psum.23 = f32[256]{0:T(256)S(1)} all-reduce(f32[256]{0:T(256)S(1)} %get-tuple-element.64), channel_id=1, replica_groups=mesh['groups'=2,'row'=4,'col'=4] {'row','col'}, use_global_device_ids=true, to_apply=%region_8.9 | all-reduce | flops 256 | bytes 2048 | tf_op jit(solution)/shard_map/psum | solution.py:103
  98.3 0.0 reduce-scatter.5.cloned.1.call-update
  98.3 0.6 broadcast_multiply_fusion.2
  98.9 53.9 %all-reduce.3.cloned.1.call-done = (f32[256,256]{0,1:T(8,128)}, f32[256,256]{0,1:T(8,128)}) async-done(((f32[256,256]{0,1:T(8,128)}, f32[256,256]{0,1:T(8,128)}), (f32[256,256]{0,1:T(8,128)}, f32[256,256]{0,1:T(8,128)})) %all-reduce.3.cloned.1.call-update) | async-done | bytes 524304 | tf_op jit(solution)/shard_map/psum | solution.py:103
  152.8 1.0 broadcast_multiply_fusion.1
  153.8 0.0 copy-start.4
  153.8 0.8 copy.33
  154.6 0.1 copy-done.4
  154.8 0.8 copy.34
  155.6 19.7 %reduce-scatter.5.cloned.1.call-done = bf16[128,256]{1,0:T(8,128)(2,1)} async-done(((bf16[512,256]{1,0:T(8,128)(2,1)}), bf16[128,256]{1,0:T(8,128)(2,1)}) %reduce-scatter.5.cloned.1.call-update) | async-done | bytes 65552 | tf_op jit(solution)/shard_map/reduce_scatter | solution.py:120
  175.3 1.7 fusion.3
  (11 shorter events, 0.1 us)
Async XLA Ops:
  7.2 18.5 %copy-start = (bf16[1,1,8,128,128]{4,3,2,1,0:T(8,128)(2,1)S(1)}, bf16[1,1,8,128,128]{4,3,2,1,0:T(8,128)(2,1)}, u32[]{:S(2)}) copy-start(bf16[1,1,8,128,128]{4,3,2,1,0:T(8,128)(2,1)} %param.15) | copy-start | bytes 786436
  7.2 44.7 %reduce-scatter.3.cloned.1.call-start = ((), (), s32[]{:S(2)}) async-start(), calls=%async_computation.2 | async-start | bytes 655360 | tf_op jit(solution)/shard_map/reduce_scatter | solution.py:79
  7.9 0.7 copy-start.8
  8.6 0.7 copy-start.9
  27.7 0.8 copy-start.1
  27.8 2.4 %copy-start.2 = (bf16[128,256]{1,0:T(8,128)(2,1)S(1)}, bf16[128,256]{1,0:T(8,128)(2,1)}, u32[]{:S(2)}) copy-start(bf16[128,256]{1,0:T(8,128)(2,1)} %param.11) | copy-start | bytes 196612
  27.8 2.4 %copy-start.3 = (bf16[256,256]{1,0:T(8,128)(2,1)S(1)}, bf16[256,256]{1,0:T(8,128)(2,1)}, u32[]{:S(2)}) copy-start(bf16[256,256]{1,0:T(8,128)(2,1)} %param.12) | copy-start | bytes 393220
  28.6 124.3 %all-reduce.3.cloned.1.call-start = ((), (), s32[]{:S(2)}) async-start(), calls=%async_computation.4 | async-start | bytes 1048576 | tf_op jit(solution)/shard_map/psum | solution.py:103
  28.6 0.7 copy-start.7
  29.5 0.7 copy-start.12
  30.2 21.8 %copy-start.5 = (bf16[256,256]{1,0:T(8,128)(2,1)S(1)}, bf16[256,256]{1,0:T(8,128)(2,1)}, u32[]{:S(2)}) copy-start(bf16[256,256]{1,0:T(8,128)(2,1)} %param.13) | copy-start | bytes 393220
  30.2 21.7 %copy-start.10 = (bf16[128,256]{1,0:T(8,128)(2,1)S(1)}, bf16[128,256]{1,0:T(8,128)(2,1)}, u32[]{:S(2)}) copy-start(bf16[128,256]{1,0:T(8,128)(2,1)} %param.21) | copy-start | bytes 196612
  30.2 21.7 %copy-start.11 = (f32[256]{0:T(256)S(1)}, f32[256]{0:T(256)}, u32[]{:S(2)}) copy-start(f32[256]{0:T(256)} %param.14) | copy-start | bytes 3076
  60.6 0.9 copy-start.6
  62.5 112.8 %reduce-scatter.5.cloned.1.call-start = ((), (), s32[]{:S(2)}) async-start(), calls=%async_computation.3 | async-start | bytes 327680 | tf_op jit(solution)/shard_map/reduce_scatter | solution.py:120
  153.8 1.0 copy-start.4
Sparse Core Ops, SparseCore 0:
  28.7 23.2 reduce-scatter.2
  62.7 90.1 all-reduce.2
  155.2 20.1 reduce-scatter.4
where the time goes:
time: 184 us
  waiting for transfers between devices  95.3 us (52%)
  blocking collectives  54.5 us (30%)
  between operations  14.7 us (8%)
  local copies, waits for them, and re-layouts  7.4 us (4%)
  matrix products  6.39 us (3%)
  other arithmetic  5.12 us (3%)
    psum x1, waiting for transfers between devices, per_device(): lax.psum((self_term, neigh_term, bias_term), ('row', 'col'))  53.9 us
    psum x1, blocking collectives, per_device(): lax.psum((self_term, neigh_term, bias_term), ('row', 'col'))  32.9 us
    reduce_scatter x1, waiting for transfers between devices, per_device(): lax.psum_scatter(partial_value, 'col', scatter_dimension=0, tiled=True)  21.6 us
    reduce_scatter x1, waiting for transfers between devices, per_device(): lax.psum_scatter(back_part.astype(jnp.bfloat16).astype(jnp.float32).astyp...  19.7 us
    all_gather x1, blocking collectives, per_device(): source = lax.all_gather(features, 'row', axis=0, tiled=True)  15.8 us
    all_gather x1, blocking collectives, per_device(): message_slab = lax.all_gather(message, 'col', axis=0, tiled=True)  5.77 us
    unnamed x28, local copies, waits for them, and re-layouts  5.51 us
  transfers between devices with their start and end apart: 3, of which 3 were waited for; matrix products, arithmetic and copies ran while one was open for 3% of the time, Pallas kernels for 0%

commit v1 on v0

--- a/solution.py
+++ b/solution.py
@@ -5,6 +5,9 @@
 from jax import lax
 from jax.sharding import PartitionSpec as P
 
+F32 = jnp.float32
+BF16 = jnp.bfloat16
+
 
 def gelu_value(inputs):
     return 0.5 * inputs * (1.0 + jax.scipy.special.erf(inputs * 0.7071067811865476))
@@ -15,6 +18,113 @@
         0.5 * (1.0 + jax.scipy.special.erf(inputs * 0.7071067811865476))
         + inputs * jnp.exp(-0.5 * inputs * inputs) * 0.3989422804014327
     )
+
+
+def dot(left, right, dims=((1,), (0,))):
+    return lax.dot_general(left, right, (dims, ((), ())), preferred_element_type=F32)
+
+
+def shift(block, axis, step):
+    size = lax.axis_size(axis)
+    return lax.ppermute(block, axis, [(i, (i + step) % size) for i in range(size)])
+
+
+def gather_parts(block, axis):
+    size = lax.axis_size(axis)
+    return [block] + [shift(block, axis, -step) for step in range(1, size)]
+
+
+def swap_parts(parts, axis):
+    return [parts[0]] + [shift(parts[j], axis, j) for j in range(1, len(parts))]
+
+
+def compact_device(
+    features,
+    w_self,
+    w_neigh,
+    layer_bias,
+    tile_vals,
+    tile_dst,
+    tile_src,
+    tile_count,
+    degree,
+    target_ids,
+    cotangent,
+):
+    rows = lax.axis_size("row")
+    cols = lax.axis_size("col")
+    row = lax.axis_index("row")
+    col = lax.axis_index("col")
+    nodes, width = features.shape
+    slots = target_ids.shape[0]
+    share = slots // cols
+    tiles = tile_vals[0, 0]
+
+    feature_parts = gather_parts(features, "row")
+
+    ids = lax.dynamic_slice_in_dim(jnp.concatenate([target_ids, target_ids]), col * share, slots, 0)
+    place = jnp.arange(cols * nodes, dtype=jnp.int32)
+    slab = (row * cols + (col + place // nodes) % cols) * nodes + place % nodes
+    pick_slab = (ids[:, None] == slab[None, :]).astype(BF16)
+    pick_own = pick_slab[:, :nodes]
+
+    degree_wide = jnp.broadcast_to(degree.astype(BF16)[:, None], (nodes, 128))
+    known = dot(pick_own, jnp.concatenate([features, cotangent, degree_wide], axis=1)).astype(BF16)
+    known = sum(swap_parts([known[j * share : (j + 1) * share] for j in range(cols)], "col"))
+    feature_slots = known[:, :width]
+    cotangent_slots = known[:, width : 2 * width]
+    degree_slots = known[:, 2 * width :]
+
+    usable = jnp.arange(tiles.shape[0], dtype=jnp.int32) < tile_count[0, 0]
+    src = (tile_src[0, 0] - row) % rows
+    dst = (tile_dst[0, 0] - col) % cols
+    src = jnp.where(usable, src, rows)
+    adjacency = jnp.zeros((rows, cols, nodes, nodes), BF16).at[src, dst].set(tiles, mode="drop")
+    adjacency = adjacency.reshape(rows, cols * nodes, nodes)
+    picked = [dot(pick_slab, adjacency[s]).astype(BF16) for s in range(rows)]
+    own_columns = sum(swap_parts(picked, "row"))
+
+    slab_features = jnp.concatenate(feature_parts, axis=0)
+    part = dot(jnp.concatenate(picked, axis=1), slab_features)
+    part_low = part.astype(BF16)
+    agg_parts = swap_parts(
+        [part[:share]] + [part_low[j * share : (j + 1) * share] for j in range(1, cols)], "col"
+    )
+    agg_sum = sum(piece.astype(F32) for piece in agg_parts)
+    degree_one = degree_slots[:, :1].astype(F32)
+    inverse = jnp.where(degree_one > 0, 1.0 / jnp.maximum(degree_one, 1.0), 0.0)
+    aggregate = (agg_sum * inverse).astype(BF16)
+    before = dot(feature_slots, w_self) + dot(aggregate, w_neigh) + layer_bias
+    slope = (cotangent_slots.astype(F32) * gelu_slope(before)).astype(BF16)
+
+    fixed = jnp.concatenate([feature_slots, degree_slots], axis=1)
+    fixed = sum(gather_parts(fixed, "row"))
+    found = jnp.concatenate([slope, aggregate], axis=1)
+    found = sum(gather_parts(found, "row"))
+    everything = jnp.concatenate(
+        gather_parts(jnp.concatenate([found, fixed], axis=1), "col"), axis=0
+    )
+    slope_all = everything[:, :width]
+    terms = dot(everything[:, width : 3 * width], slope_all, ((0,), (0,)))
+    scale = 1.0 / math.sqrt(nodes * rows * cols)
+    grad_neigh = terms[:width] * scale
+    grad_self = terms[width:] * scale
+    grad_bias = jnp.sum(slope_all.astype(F32), axis=0) * scale
+    degree_all = everything[:, 3 * width : 3 * width + 1].astype(F32)
+    message = (dot(slope_all, w_neigh, ((1,), (1,))) / degree_all).astype(BF16)
+    own_slope = dot(pick_own, slope_all, ((0,), (0,))).astype(BF16)
+    grad_features = dot(own_slope, w_self, ((1,), (1,))) + dot(own_columns, message, ((0,), (0,)))
+
+    dense = sum(dot(adjacency[s], feature_parts[s]) for s in range(rows))
+    dense_low = dense.astype(BF16)
+    dense_parts = swap_parts(
+        [dense[:nodes]] + [dense_low[j * nodes : (j + 1) * nodes] for j in range(1, cols)], "col"
+    )
+    own_sum = sum(piece.astype(F32) for piece in dense_parts)
+    own_aggregate = (own_sum * (1.0 / degree.astype(F32))[:, None]).astype(BF16)
+    own_before = dot(features, w_self) + dot(own_aggregate, w_neigh) + layer_bias
+    hidden = gelu_value(own_before).astype(BF16)
+    return (hidden, grad_features.astype(BF16), grad_self, grad_neigh, grad_bias)
 
 
 def tile_sum(values, take_index, put_index, usable, source, out_tiles, transpose, first_tile):
@@ -44,7 +154,7 @@
     return running.reshape(out_tiles * tile_width, columns)
 
 
-def per_device(
+def dense_device(
     features,
     w_self,
     w_neigh,
@@ -155,6 +265,8 @@
         P("groups", None),
         P("groups"),
     )
+    parts = mesh.shape["row"] * mesh.shape["col"]
+    per_device = compact_device if parts <= 16 else dense_device
     return jax.shard_map(
         per_device, mesh=mesh, in_specs=in_specs, out_specs=out_specs, check_vma=False
     )

time: 184 us -> 52 us (0.28)
  waiting for transfers between devices: 95.3 us -> 13.5 us
  blocking collectives: 54.5 us -> 0 us
  starting transfers between devices: 0.12 us -> 23.5 us
  between operations: 14.7 us -> 1.67 us
  other arithmetic: 5.12 us -> 2.05 us
  local copies, waits for them, and re-layouts: 7.4 us -> 5.22 us
    psum x1 -> x0, waiting for transfers between devices: 53.9 us -> none  [per_device(): lax.psum((self_term, neigh_term, bias_term), ('row', 'col'))]
    reduce_scatter x2 -> x0, waiting for transfers between devices: 41.3 us -> none  [the longest x1 21.6 us: per_device(): lax.psum_scatter(partial_value, 'col', scatter_dimension=0, tiled=True)]
    psum x1 -> x0, blocking collectives: 32.9 us -> none  [per_device(): lax.psum((self_term, neigh_term, bias_term), ('row', 'col'))]
    ppermute x0 -> x24, starting transfers between devices: none -> 23.5 us  [shift(): lax.ppermute(block, axis, [(i, (i + step) % size) for i in range(size)])]
    all_gather x2 -> x0, blocking collectives: 21.6 us -> none  [the longest x1 15.8 us: per_device(): source = lax.all_gather(features, 'row', axis=0, tiled=True)]
    ppermute x0 -> x24, waiting for transfers between devices: none -> 13.5 us  [shift(): lax.ppermute(block, axis, [(i, (i + step) % size) for i in range(size)])]
    scatter-add x2 -> x0, other arithmetic: 2.62 us -> none  [advance(): running = running.at[where_to].add(product)]
    unnamed x28 -> x20, local copies, waits for them, and re-layouts: 5.51 us -> 4.01 us
  transfers between devices with their start and end apart: 3 -> 24, of which waited for: 3 -> 9; matrix products, arithmetic and copies ran while one was open for 3% -> 15% of each run, Pallas kernels for 0% -> 0%
where the time goes in v1:
time: 52 us; the launch traced here: 51.5 us
  starting transfers between devices  23.5 us (45%)
  waiting for transfers between devices  13.5 us (26%)
  matrix products  5.55 us (11%)
  local copies, waits for them, and re-layouts  5.22 us (10%)
  other arithmetic  2.05 us (4%)
  between operations  1.67 us (3%)
    ppermute x24, starting transfers between devices, shift(): lax.ppermute(block, axis, [(i, (i + step) % size) for i in range(size)])  23.5 us
    ppermute x24, waiting for transfers between devices, shift(): lax.ppermute(block, axis, [(i, (i + step) % size) for i in range(size)])  13.5 us
    dot_general x17, matrix products, dot(): lax.dot_general(left, right, (dims, ((), ())), preferred_element_type=F32)  5.55 us
    unnamed x20, local copies, waits for them, and re-layouts  4.01 us
  transfers between devices with their start and end apart: 24, of which 9 were waited for; matrix products, arithmetic and copies ran while one was open for 15% of the time, Pallas kernels for 0%

profile of v1, /device:TPU:0, one launch (start us, length us, event | category | flops | bytes accessed | tf_op | source)
XLA Modules:
  0.0 51.5 jit_solution(16223926599332408997)
XLA Ops:
  0.6 3.1 %collective-permute-start.2 = (bf16[128,256]{1,0:T(8,128)(2,1)}, bf16[128,256]{1,0:T(8,128)(2,1)S(1)}, u32[]{:S(2)}, u32[]{:S(2)}) collective-permute-start(bf16[128,256]{1,0:T(8,128)(2,1)} %param.11), channel_id=1, source_target_pairs={{0,4},{4,8},{8,12},{12,0},{1,5},{5,9},{9,13},{13,1},{2,6},{6,10},{... | collective-permute-start | bytes 196616 | tf_op jit(solution)/shard_map/ppermute | solution.py:29
  3.7 2.1 %collective-permute-start = (bf16[128,256]{1,0:T(8,128)(2,1)}, bf16[128,256]{1,0:T(8,128)(2,1)S(1)}, u32[]{:S(2)}, u32[]{:S(2)}) collective-permute-start(bf16[128,256]{1,0:T(8,128)(2,1)} %param.11), channel_id=1, source_target_pairs={{0,12},{4,0},{8,4},{12,8},{1,13},{5,1},{9,5},{13,9},{2,14},{6,2},{... | collective-permute-start | bytes 196616 | tf_op jit(solution)/shard_map/ppermute | solution.py:29
  5.8 0.9 %collective-permute-start.1 = (bf16[128,256]{1,0:T(8,128)(2,1)}, bf16[128,256]{1,0:T(8,128)(2,1)S(1)}, u32[]{:S(2)}, u32[]{:S(2)}) collective-permute-start(bf16[128,256]{1,0:T(8,128)(2,1)} %param.11), channel_id=1, source_target_pairs={{0,8},{4,12},{8,0},{12,4},{1,9},{5,13},{9,1},{13,5},{2,10},{6,14},... | collective-permute-start | bytes 196616 | tf_op jit(solution)/shard_map/ppermute | solution.py:29
  6.8 0.7 %copy-done.9 = s32[128]{0:T(128)S(1)} copy-done((s32[128]{0:T(128)S(1)}, s32[128]{0:T(128)}, u32[]{:S(2)}) %copy-start.9) | copy-done | bytes 536
  7.4 0.7 %copy-done.5 = s32[256]{0:T(256)S(1)} copy-done((s32[256]{0:T(256)S(1)}, s32[256]{0:T(256)}, u32[]{:S(2)}) %copy-start.5) | copy-done | bytes 1048
  8.1 0.1 dynamic_slice.3
  8.2 0.1 broadcast_compare_fusion
  8.4 0.1 broadcast_in_dim.7
  8.4 0.6 %copy-done.3 = bf16[128,256]{1,0:T(8,128)(2,1)S(1)} copy-done((bf16[128,256]{1,0:T(8,128)(2,1)S(1)}, bf16[128,256]{1,0:T(8,128)(2,1)}, u32[]{:S(2)}) %copy-start.3) | copy-done | bytes 65560
  9.0 0.0 copy-done.8
  9.1 0.2 convolution_convert_fusion
  9.3 0.1 collective-permute-start.8
  9.5 1.5 %collective-permute-start.7 = (bf16[64,640]{1,0:T(8,128)(2,1)S(1)}, bf16[64,640]{1,0:T(8,128)(2,1)S(1)}, u32[]{:S(2)}, u32[]{:S(2)}) collective-permute-start(bf16[64,640]{1,0:T(8,128)(2,1)S(1)} %get-tuple-element.15), channel_id=1, source_target_pairs={{0,2},{1,3},{2,0},{3,1},{4,6},{5,7},{6,4},{7,5},{8,10},{9,11},{10,... | collective-permute-start | bytes 245768 | tf_op jit(solution)/shard_map/ppermute | solution.py:29
  11.6 0.6 %copy-done.6 = s32[1,1,8]{2,1,0:T(1,128)S(1)} copy-done((s32[1,1,8]{2,1,0:T(1,128)S(1)}, s32[1,1,8]{2,1,0:T(1,128)}, u32[]{:S(2)}) %copy-start.6) | copy-done | bytes 56
  12.3 0.0 copy-done.7
  12.3 0.1 broadcast_in_dim.6
  12.4 0.8 %copy-done.2 = bf16[1,1,8,128,128]{4,3,2,1,0:T(8,128)(2,1)S(1)} copy-done((bf16[1,1,8,128,128]{4,3,2,1,0:T(8,128)(2,1)S(1)}, bf16[1,1,8,128,128]{4,3,2,1,0:T(8,128)(2,1)}, u32[]{:S(2)}) %copy-start.2) | copy-done | bytes 262168
  13.3 0.9 %scatter_fusion = bf16[4,4,128,128]{3,2,1,0:T(8,128)(2,1)S(1)} fusion(bf16[4,4,128,128]{3,2,1,0:T(8,128)(2,1)S(1)} %broadcast_in_dim.6, s32[8]{0:T(128)S(1)} %fusion.85, bf16[8,128,128]{2,1,0:T(8,128)(2,1)S(1)} %bitcast.48), kind=kCustom, calls=%fused_computation | custom fusion | bytes 786496 | tf_op jit(solution)/shard_map/scatter | solution.py:82
  14.2 0.2 fusion.97
  14.4 0.3 convolution_convert_fusion.5
  14.7 0.2 fusion.96
  14.9 0.3 convolution_convert_fusion.2
  15.2 0.3 convolution_convert_fusion.3
  15.5 0.3 convolution_convert_fusion.4
  15.9 0.2 collective-permute-start.6
  16.1 0.2 convolution_add_fusion.1
  16.3 1.4 %collective-permute-start.23 = (bf16[256,128]{0,1:T(8,128)(2,1)S(1)}, bf16[256,128]{0,1:T(8,128)(2,1)S(1)}, u32[]{:S(2)}, u32[]{:S(2)}) collective-permute-start(bf16[256,128]{0,1:T(8,128)(2,1)S(1)} %convolution_convert_fusion.2), channel_id=1, source_target_pairs={{0,12},{4,0},{8,4},{12,8},{1,13},{5,1},{9,5},{13,9},{2,14},{6,2},{... | collective-permute-start | bytes 196616 | tf_op jit(solution)/shard_map/ppermute | solution.py:29
  17.7 0.2 fusion.98
  17.9 1.7 %collective-permute-start.22 = (bf16[256,128]{0,1:T(8,128)(2,1)S(1)}, bf16[256,128]{0,1:T(8,128)(2,1)S(1)}, u32[]{:S(2)}, u32[]{:S(2)}) collective-permute-start(bf16[256,128]{0,1:T(8,128)(2,1)S(1)} %convolution_convert_fusion.3), channel_id=1, source_target_pairs={{0,8},{4,12},{8,0},{12,4},{1,9},{5,13},{9,1},{13,5},{2,10},{6,14},... | collective-permute-start | bytes 196616 | tf_op jit(solution)/shard_map/ppermute | solution.py:29
  19.7 0.2 fusion.94
  19.9 0.3 fusion.95
  20.2 1.1 %collective-permute-start.11 = (bf16[64,256]{1,0:T(8,128)(2,1)S(1)}, bf16[64,256]{1,0:T(8,128)(2,1)S(1)}, u32[]{:S(2)}, u32[]{:S(2)}) collective-permute-start(bf16[64,256]{1,0:T(8,128)(2,1)S(1)} %get-tuple-element.20), channel_id=1, source_target_pairs={{0,3},{1,0},{2,1},{3,2},{4,7},{5,4},{6,5},{7,6},{8,11},{9,8},{10,9... | collective-permute-start | bytes 98312 | tf_op jit(solution)/shard_map/ppermute | solution.py:29
  21.3 0.6 %collective-permute-start.10 = (bf16[64,256]{1,0:T(8,128)(2,1)S(1)}, bf16[64,256]{1,0:T(8,128)(2,1)S(1)}, u32[]{:S(2)}, u32[]{:S(2)}) collective-permute-start(bf16[64,256]{1,0:T(8,128)(2,1)S(1)} %get-tuple-element.21), channel_id=1, source_target_pairs={{0,2},{1,3},{2,0},{3,1},{4,6},{5,7},{6,4},{7,5},{8,10},{9,11},{10,... | collective-permute-start | bytes 98312 | tf_op jit(solution)/shard_map/ppermute | solution.py:29
  21.9 0.1 fusion.69
  22.0 0.8 %collective-permute-done.11 = bf16[64,256]{1,0:T(8,128)(2,1)S(1)} collective-permute-done((bf16[64,256]{1,0:T(8,128)(2,1)S(1)}, bf16[64,256]{1,0:T(8,128)(2,1)S(1)}, u32[]{:S(2)}, u32[]{:S(2)}) %collective-permute-start.11) | collective-permute-done | bytes 32800 | tf_op jit(solution)/shard_map/ppermute | solution.py:29
  22.9 1.1 %collective-permute-start.17 = (bf16[64,384]{1,0:T(8,128)(2,1)S(1)}, bf16[64,384]{1,0:T(8,128)(2,1)S(1)}, u32[]{:S(2)}, u32[]{:S(2)}) collective-permute-start(bf16[64,384]{1,0:T(8,128)(2,1)S(1)} %pad_maximum_fusion.11), channel_id=1, source_target_pairs={{0,4},{4,8},{8,12},{12,0},{1,5},{5,9},{9,13},{13,1},{2,6},{6,10},{... | collective-permute-start | bytes 147464 | tf_op jit(solution)/shard_map/ppermute | solution.py:29
  24.0 1.5 %collective-permute-done.10 = bf16[64,256]{1,0:T(8,128)(2,1)S(1)} collective-permute-done((bf16[64,256]{1,0:T(8,128)(2,1)S(1)}, bf16[64,256]{1,0:T(8,128)(2,1)S(1)}, u32[]{:S(2)}, u32[]{:S(2)}) %collective-permute-start.10) | collective-permute-done | bytes 32800 | tf_op jit(solution)/shard_map/ppermute | solution.py:29
  25.5 1.2 %collective-permute-start.16 = (bf16[64,384]{1,0:T(8,128)(2,1)S(1)}, bf16[64,384]{1,0:T(8,128)(2,1)S(1)}, u32[]{:S(2)}, u32[]{:S(2)}) collective-permute-start(bf16[64,384]{1,0:T(8,128)(2,1)S(1)} %pad_maximum_fusion.11), channel_id=1, source_target_pairs={{0,8},{4,12},{8,0},{12,4},{1,9},{5,13},{9,1},{13,5},{2,10},{6,14},... | collective-permute-start | bytes 147464 | tf_op jit(solution)/shard_map/ppermute | solution.py:29
  26.8 2.2 %collective-permute-start.15 = (bf16[64,384]{1,0:T(8,128)(2,1)S(1)}, bf16[64,384]{1,0:T(8,128)(2,1)S(1)}, u32[]{:S(2)}, u32[]{:S(2)}) collective-permute-start(bf16[64,384]{1,0:T(8,128)(2,1)S(1)} %pad_maximum_fusion.11), channel_id=1, source_target_pairs={{0,12},{4,0},{8,4},{12,8},{1,13},{5,1},{9,5},{13,9},{2,14},{6,2},{... | collective-permute-start | bytes 147464 | tf_op jit(solution)/shard_map/ppermute | solution.py:29
  28.9 0.1 fusion.62
  29.0 0.1 fusion.99
  29.2 0.5 %copy-done.4 = f32[256]{0:T(256)S(1)} copy-done((f32[256]{0:T(256)S(1)}, f32[256]{0:T(256)}, u32[]{:S(2)}) %copy-start.4) | copy-done | bytes 1048
  29.7 0.2 fusion.57
  29.9 0.1 collective-permute-start.14
  30.0 1.6 %collective-permute-done.16 = bf16[64,384]{1,0:T(8,128)(2,1)S(1)} collective-permute-done((bf16[64,384]{1,0:T(8,128)(2,1)S(1)}, bf16[64,384]{1,0:T(8,128)(2,1)S(1)}, u32[]{:S(2)}, u32[]{:S(2)}) %collective-permute-start.16) | collective-permute-done | bytes 49184 | tf_op jit(solution)/shard_map/ppermute | solution.py:29
  31.6 0.7 %collective-permute-start.13 = (bf16[64,512]{1,0:T(8,128)(2,1)S(1)}, bf16[64,512]{1,0:T(8,128)(2,1)S(1)}, u32[]{:S(2)}, u32[]{:S(2)}) collective-permute-start(bf16[64,512]{1,0:T(8,128)(2,1)S(1)} %pad_maximum_fusion.10), channel_id=1, source_target_pairs={{0,8},{4,12},{8,0},{12,4},{1,9},{5,13},{9,1},{13,5},{2,10},{6,14},... | collective-permute-start | bytes 196616 | tf_op jit(solution)/shard_map/ppermute | solution.py:29
  32.3 2.9 %collective-permute-start.12 = (bf16[64,512]{1,0:T(8,128)(2,1)S(1)}, bf16[64,512]{1,0:T(8,128)(2,1)S(1)}, u32[]{:S(2)}, u32[]{:S(2)}) collective-permute-start(bf16[64,512]{1,0:T(8,128)(2,1)S(1)} %pad_maximum_fusion.10), channel_id=1, source_target_pairs={{0,12},{4,0},{8,4},{12,8},{1,13},{5,1},{9,5},{13,9},{2,14},{6,2},{... | collective-permute-start | bytes 196616 | tf_op jit(solution)/shard_map/ppermute | solution.py:29
  35.2 0.9 %collective-permute-done.14 = bf16[64,512]{1,0:T(8,128)(2,1)S(1)} collective-permute-done((bf16[64,512]{1,0:T(8,128)(2,1)S(1)}, bf16[64,512]{1,0:T(8,128)(2,1)S(1)}, u32[]{:S(2)}, u32[]{:S(2)}) %collective-permute-start.14) | collective-permute-done | bytes 65568 | tf_op jit(solution)/shard_map/ppermute | solution.py:29
  36.2 2.0 %collective-permute-done.13 = bf16[64,512]{1,0:T(8,128)(2,1)S(1)} collective-permute-done((bf16[64,512]{1,0:T(8,128)(2,1)S(1)}, bf16[64,512]{1,0:T(8,128)(2,1)S(1)}, u32[]{:S(2)}, u32[]{:S(2)}) %collective-permute-start.13) | collective-permute-done | bytes 65568 | tf_op jit(solution)/shard_map/ppermute | solution.py:29
  38.2 0.6 %collective-permute-start.4 = (bf16[128,256]{1,0:T(8,128)(2,1)S(1)}, bf16[128,256]{1,0:T(8,128)(2,1)S(1)}, u32[]{:S(2)}, u32[]{:S(2)}) collective-permute-start(bf16[128,256]{1,0:T(8,128)(2,1)S(1)} %get-tuple-element.18), channel_id=1, source_target_pairs={{0,2},{1,3},{2,0},{3,1},{4,6},{5,7},{6,4},{7,5},{8,10},{9,11},{10,... | collective-permute-start | bytes 196616 | tf_op jit(solution)/shard_map/ppermute | solution.py:29
  38.9 1.6 %collective-permute-start.20 = (bf16[64,896]{1,0:T(8,128)(2,1)S(1)}, bf16[64,896]{1,0:T(8,128)(2,1)S(1)}, u32[]{:S(2)}, u32[]{:S(2)}) collective-permute-start(bf16[64,896]{1,0:T(8,128)(2,1)S(1)} %pad_maximum_fusion.9), channel_id=1, source_target_pairs={{0,1},{1,2},{2,3},{3,0},{4,5},{5,6},{6,7},{7,4},{8,9},{9,10},{10,1... | collective-permute-start | bytes 344072 | tf_op jit(solution)/shard_map/ppermute | solution.py:29
  40.4 2.7 %collective-permute-done.4 = bf16[128,256]{1,0:T(8,128)(2,1)S(1)} collective-permute-done((bf16[128,256]{1,0:T(8,128)(2,1)S(1)}, bf16[128,256]{1,0:T(8,128)(2,1)S(1)}, u32[]{:S(2)}, u32[]{:S(2)}) %collective-permute-start.4) | collective-permute-done | bytes 65568 | tf_op jit(solution)/shard_map/ppermute | solution.py:29
  43.1 0.0 collective-permute-done.3
  43.1 0.9 %multiply_convert_fusion = bf16[128,256]{1,0:T(8,128)(2,1)} fusion(f32[128,256]{1,0:T(8,128)S(1)} %fusion.96, bf16[256,256]{1,0:T(8,128)(2,1)S(1)} %copy-done.1, f32[512,256]{1,0:T(8,128)S(1)} %get-tuple-element.23, bf16[128,256]{1,0:T(8,128)(2,1)S(1)} %collective-permute-done.5, bf16[128,256]{1,0:T(8,128)(2,1)S(1)} %collective-permute-done.4, ...), kind=kOutput, calls=%fused_computation.70 | convolution fusion | flops 17268736 | bytes 656896 | tf_op jit(solution)/shard_map/dot_general | solution.py:24
  44.0 0.4 collective-permute-done.20
  44.4 0.4 collective-permute-start.21
  44.8 3.1 %collective-permute-done.19 = bf16[64,896]{1,0:T(8,128)(2,1)S(1)} collective-permute-done((bf16[64,896]{1,0:T(8,128)(2,1)S(1)}, bf16[64,896]{1,0:T(8,128)(2,1)S(1)}, u32[]{:S(2)}, u32[]{:S(2)}) %collective-permute-start.19) | collective-permute-done | bytes 114720 | tf_op jit(solution)/shard_map/ppermute | solution.py:29
  48.0 0.3 fusion.7
  48.3 0.3 fusion.12
  48.6 0.8 %slice_multiply_fusion = (f32[256,256]{1,0:T(8,128)}, f32[256,256]{1,0:T(8,128)}) fusion(f32[512,256]{1,0:T(8,128)S(1)} %fusion.12), kind=kLoop, calls=%fused_computation.24 | loop fusion | flops 131072 | bytes 1048576 | tf_op jit(solution)/shard_map/mul | solution.py:110
  49.4 0.6 %broadcast_multiply_fusion = f32[256]{0:T(256)} fusion(f32[256]{0:T(256)S(1)} %get-tuple-element.5), kind=kLoop, calls=%fused_computation.137 | loop fusion | flops 256 | bytes 2048 | tf_op jit(solution)/shard_map/mul | solution.py:112
  50.0 0.1 convert_reduce_fusion.1
  50.1 0.3 collective-permute-done.21
  50.4 1.0 %fusion.5 = bf16[128,256]{1,0:T(8,128)(2,1)} fusion(f32[128,256]{1,0:T(8,128)S(1)} %fusion.7, bf16[256,256]{1,0:T(8,128)(2,1)S(1)} %get-tuple-element.6, bf16[256,256]{1,0:T(8,128)(2,1)S(1)} %copy-done.1, f32[256]{0:T(256)S(1)} %convert_reduce_fusion.1, bf16[256,128]{0,1:T(8,128)(2,1)S(1)} %collective-permute-done.23, ...), kind=kOutput, calls=%fused_computation.11 | convolution fusion | flops 50626560 | bytes 721920 | tf_op jit(solution)/shard_map/dot_general | solution.py:24
  (49 shorter events, 0.4 us)
Async XLA Ops:
  0.6 14.1 %copy-start = (bf16[256,256]{1,0:T(8,128)(2,1)S(1)}, bf16[256,256]{1,0:T(8,128)(2,1)}, u32[]{:S(2)}) copy-start(bf16[256,256]{1,0:T(8,128)(2,1)} %param.12) | copy-start | bytes 393220
  0.6 15.6 %collective-permute-start.2 = (bf16[128,256]{1,0:T(8,128)(2,1)}, bf16[128,256]{1,0:T(8,128)(2,1)S(1)}, u32[]{:S(2)}, u32[]{:S(2)}) collective-permute-start(bf16[128,256]{1,0:T(8,128)(2,1)} %param.11), channel_id=1, source_target_pairs={{0,4},{4,8},{8,12},{12,0},{1,5},{5,9},{9,13},{13,1},{2,6},{6,10},{... | collective-permute-start | bytes 196616 | tf_op jit(solution)/shard_map/ppermute | solution.py:29
  3.7 12.1 %collective-permute-start = (bf16[128,256]{1,0:T(8,128)(2,1)}, bf16[128,256]{1,0:T(8,128)(2,1)S(1)}, u32[]{:S(2)}, u32[]{:S(2)}) collective-permute-start(bf16[128,256]{1,0:T(8,128)(2,1)} %param.11), channel_id=1, source_target_pairs={{0,12},{4,0},{8,4},{12,8},{1,13},{5,1},{9,5},{13,9},{2,14},{6,2},{... | collective-permute-start | bytes 196616 | tf_op jit(solution)/shard_map/ppermute | solution.py:29
  5.8 12.1 %collective-permute-start.1 = (bf16[128,256]{1,0:T(8,128)(2,1)}, bf16[128,256]{1,0:T(8,128)(2,1)S(1)}, u32[]{:S(2)}, u32[]{:S(2)}) collective-permute-start(bf16[128,256]{1,0:T(8,128)(2,1)} %param.11), channel_id=1, source_target_pairs={{0,8},{4,12},{8,0},{12,4},{1,9},{5,13},{9,1},{13,5},{2,10},{6,14},... | collective-permute-start | bytes 196616 | tf_op jit(solution)/shard_map/ppermute | solution.py:29
  6.8 0.7 %copy-start.9 = (s32[128]{0:T(128)S(1)}, s32[128]{0:T(128)}, u32[]{:S(2)}) copy-start(s32[128]{0:T(128)} %param.19) | copy-start | bytes 1540
  7.4 0.7 %copy-start.5 = (s32[256]{0:T(256)S(1)}, s32[256]{0:T(256)}, u32[]{:S(2)}) copy-start(s32[256]{0:T(256)} %param.20) | copy-start | bytes 3076
  8.2 0.8 %copy-start.3 = (bf16[128,256]{1,0:T(8,128)(2,1)S(1)}, bf16[128,256]{1,0:T(8,128)(2,1)}, u32[]{:S(2)}) copy-start(bf16[128,256]{1,0:T(8,128)(2,1)} %param.11) | copy-start | bytes 196612
  8.2 0.9 %copy-start.8 = (bf16[128,256]{1,0:T(8,128)(2,1)S(1)}, bf16[128,256]{1,0:T(8,128)(2,1)}, u32[]{:S(2)}) copy-start(bf16[128,256]{1,0:T(8,128)(2,1)} %param.21) | copy-start | bytes 196612
  9.3 10.9 %collective-permute-start.8 = (bf16[64,640]{1,0:T(8,128)(2,1)S(1)}, bf16[64,640]{1,0:T(8,128)(2,1)S(1)}, u32[]{:S(2)}, u32[]{:S(2)}) collective-permute-start(bf16[64,640]{1,0:T(8,128)(2,1)S(1)} %get-tuple-element.14), channel_id=1, source_target_pairs={{0,3},{1,0},{2,1},{3,2},{4,7},{5,4},{6,5},{7,6},{8,11},{9,8},{10,9... | collective-permute-start | bytes 245768 | tf_op jit(solution)/shard_map/ppermute | solution.py:29
  9.5 11.8 %collective-permute-start.7 = (bf16[64,640]{1,0:T(8,128)(2,1)S(1)}, bf16[64,640]{1,0:T(8,128)(2,1)S(1)}, u32[]{:S(2)}, u32[]{:S(2)}) collective-permute-start(bf16[64,640]{1,0:T(8,128)(2,1)S(1)} %get-tuple-element.15), channel_id=1, source_target_pairs={{0,2},{1,3},{2,0},{3,1},{4,6},{5,7},{6,4},{7,5},{8,10},{9,11},{10,... | collective-permute-start | bytes 245768 | tf_op jit(solution)/shard_map/ppermute | solution.py:29
  11.6 0.7 %copy-start.6 = (s32[1,1,8]{2,1,0:T(1,128)S(1)}, s32[1,1,8]{2,1,0:T(1,128)}, u32[]{:S(2)}) copy-start(s32[1,1,8]{2,1,0:T(1,128)} %param.16) | copy-start | bytes 100
  11.6 0.7 %copy-start.7 = (s32[1,1,8]{2,1,0:T(1,128)S(1)}, s32[1,1,8]{2,1,0:T(1,128)}, u32[]{:S(2)}) copy-start(s32[1,1,8]{2,1,0:T(1,128)} %param.17) | copy-start | bytes 100
  12.3 1.0 %copy-start.2 = (bf16[1,1,8,128,128]{4,3,2,1,0:T(8,128)(2,1)S(1)}, bf16[1,1,8,128,128]{4,3,2,1,0:T(8,128)(2,1)}, u32[]{:S(2)}) copy-start(bf16[1,1,8,128,128]{4,3,2,1,0:T(8,128)(2,1)} %param.15) | copy-start | bytes 786436
  15.9 6.0 %collective-permute-start.6 = (bf16[64,640]{1,0:T(8,128)(2,1)S(1)}, bf16[64,640]{1,0:T(8,128)(2,1)S(1)}, u32[]{:S(2)}, u32[]{:S(2)}) collective-permute-start(bf16[64,640]{1,0:T(8,128)(2,1)S(1)} %get-tuple-element.13), channel_id=1, source_target_pairs={{0,1},{1,2},{2,3},{3,0},{4,5},{5,6},{6,7},{7,4},{8,9},{9,10},{10,1... | collective-permute-start | bytes 245768 | tf_op jit(solution)/shard_map/ppermute | solution.py:29
  16.3 33.8 %collective-permute-start.23 = (bf16[256,128]{0,1:T(8,128)(2,1)S(1)}, bf16[256,128]{0,1:T(8,128)(2,1)S(1)}, u32[]{:S(2)}, u32[]{:S(2)}) collective-permute-start(bf16[256,128]{0,1:T(8,128)(2,1)S(1)} %convolution_convert_fusion.2), channel_id=1, source_target_pairs={{0,12},{4,0},{8,4},{12,8},{1,13},{5,1},{9,5},{13,9},{2,14},{6,2},{... | collective-permute-start | bytes 196616 | tf_op jit(solution)/shard_map/ppermute | solution.py:29
  17.9 32.2 %collective-permute-start.22 = (bf16[256,128]{0,1:T(8,128)(2,1)S(1)}, bf16[256,128]{0,1:T(8,128)(2,1)S(1)}, u32[]{:S(2)}, u32[]{:S(2)}) collective-permute-start(bf16[256,128]{0,1:T(8,128)(2,1)S(1)} %convolution_convert_fusion.3), channel_id=1, source_target_pairs={{0,8},{4,12},{8,0},{12,4},{1,9},{5,13},{9,1},{13,5},{2,10},{6,14},... | collective-permute-start | bytes 196616 | tf_op jit(solution)/shard_map/ppermute | solution.py:29
  20.2 2.7 %collective-permute-start.11 = (bf16[64,256]{1,0:T(8,128)(2,1)S(1)}, bf16[64,256]{1,0:T(8,128)(2,1)S(1)}, u32[]{:S(2)}, u32[]{:S(2)}) collective-permute-start(bf16[64,256]{1,0:T(8,128)(2,1)S(1)} %get-tuple-element.20), channel_id=1, source_target_pairs={{0,3},{1,0},{2,1},{3,2},{4,7},{5,4},{6,5},{7,6},{8,11},{9,8},{10,9... | collective-permute-start | bytes 98312 | tf_op jit(solution)/shard_map/ppermute | solution.py:29
  21.3 4.2 %collective-permute-start.10 = (bf16[64,256]{1,0:T(8,128)(2,1)S(1)}, bf16[64,256]{1,0:T(8,128)(2,1)S(1)}, u32[]{:S(2)}, u32[]{:S(2)}) collective-permute-start(bf16[64,256]{1,0:T(8,128)(2,1)S(1)} %get-tuple-element.21), channel_id=1, source_target_pairs={{0,2},{1,3},{2,0},{3,1},{4,6},{5,7},{6,4},{7,5},{8,10},{9,11},{10,... | collective-permute-start | bytes 98312 | tf_op jit(solution)/shard_map/ppermute | solution.py:29
  21.8 4.9 %collective-permute-start.9 = (bf16[64,256]{1,0:T(8,128)(2,1)S(1)}, bf16[64,256]{1,0:T(8,128)(2,1)S(1)}, u32[]{:S(2)}, u32[]{:S(2)}) collective-permute-start(bf16[64,256]{1,0:T(8,128)(2,1)S(1)} %get-tuple-element.19), channel_id=1, source_target_pairs={{0,1},{1,2},{2,3},{3,0},{4,5},{5,6},{6,7},{7,4},{8,9},{9,10},{10,1... | collective-permute-start | bytes 98312 | tf_op jit(solution)/shard_map/ppermute | solution.py:29
  22.0 7.0 %copy-start.1 = (bf16[256,256]{1,0:T(8,128)(2,1)S(1)}, bf16[256,256]{1,0:T(8,128)(2,1)}, u32[]{:S(2)}) copy-start(bf16[256,256]{1,0:T(8,128)(2,1)} %param.13) | copy-start | bytes 393220
  22.9 7.0 %collective-permute-start.17 = (bf16[64,384]{1,0:T(8,128)(2,1)S(1)}, bf16[64,384]{1,0:T(8,128)(2,1)S(1)}, u32[]{:S(2)}, u32[]{:S(2)}) collective-permute-start(bf16[64,384]{1,0:T(8,128)(2,1)S(1)} %pad_maximum_fusion.11), channel_id=1, source_target_pairs={{0,4},{4,8},{8,12},{12,0},{1,5},{5,9},{9,13},{13,1},{2,6},{6,10},{... | collective-permute-start | bytes 147464 | tf_op jit(solution)/shard_map/ppermute | solution.py:29
  25.5 6.0 %collective-permute-start.16 = (bf16[64,384]{1,0:T(8,128)(2,1)S(1)}, bf16[64,384]{1,0:T(8,128)(2,1)S(1)}, u32[]{:S(2)}, u32[]{:S(2)}) collective-permute-start(bf16[64,384]{1,0:T(8,128)(2,1)S(1)} %pad_maximum_fusion.11), channel_id=1, source_target_pairs={{0,8},{4,12},{8,0},{12,4},{1,9},{5,13},{9,1},{13,5},{2,10},{6,14},... | collective-permute-start | bytes 147464 | tf_op jit(solution)/shard_map/ppermute | solution.py:29
  26.8 5.6 %collective-permute-start.15 = (bf16[64,384]{1,0:T(8,128)(2,1)S(1)}, bf16[64,384]{1,0:T(8,128)(2,1)S(1)}, u32[]{:S(2)}, u32[]{:S(2)}) collective-permute-start(bf16[64,384]{1,0:T(8,128)(2,1)S(1)} %pad_maximum_fusion.11), channel_id=1, source_target_pairs={{0,12},{4,0},{8,4},{12,8},{1,13},{5,1},{9,5},{13,9},{2,14},{6,2},{... | collective-permute-start | bytes 147464 | tf_op jit(solution)/shard_map/ppermute | solution.py:29
  29.0 0.7 %copy-start.4 = (f32[256]{0:T(256)S(1)}, f32[256]{0:T(256)}, u32[]{:S(2)}) copy-start(f32[256]{0:T(256)} %param.14) | copy-start | bytes 3076
  29.9 6.2 %collective-permute-start.14 = (bf16[64,512]{1,0:T(8,128)(2,1)S(1)}, bf16[64,512]{1,0:T(8,128)(2,1)S(1)}, u32[]{:S(2)}, u32[]{:S(2)}) collective-permute-start(bf16[64,512]{1,0:T(8,128)(2,1)S(1)} %pad_maximum_fusion.10), channel_id=1, source_target_pairs={{0,4},{4,8},{8,12},{12,0},{1,5},{5,9},{9,13},{13,1},{2,6},{6,10},{... | collective-permute-start | bytes 196616 | tf_op jit(solution)/shard_map/ppermute | solution.py:29
  31.6 6.6 %collective-permute-start.13 = (bf16[64,512]{1,0:T(8,128)(2,1)S(1)}, bf16[64,512]{1,0:T(8,128)(2,1)S(1)}, u32[]{:S(2)}, u32[]{:S(2)}) collective-permute-start(bf16[64,512]{1,0:T(8,128)(2,1)S(1)} %pad_maximum_fusion.10), channel_id=1, source_target_pairs={{0,8},{4,12},{8,0},{12,4},{1,9},{5,13},{9,1},{13,5},{2,10},{6,14},... | collective-permute-start | bytes 196616 | tf_op jit(solution)/shard_map/ppermute | solution.py:29
  32.3 6.4 %collective-permute-start.12 = (bf16[64,512]{1,0:T(8,128)(2,1)S(1)}, bf16[64,512]{1,0:T(8,128)(2,1)S(1)}, u32[]{:S(2)}, u32[]{:S(2)}) collective-permute-start(bf16[64,512]{1,0:T(8,128)(2,1)S(1)} %pad_maximum_fusion.10), channel_id=1, source_target_pairs={{0,12},{4,0},{8,4},{12,8},{1,13},{5,1},{9,5},{13,9},{2,14},{6,2},{... | collective-permute-start | bytes 196616 | tf_op jit(solution)/shard_map/ppermute | solution.py:29
  36.1 2.7 %collective-permute-start.5 = (bf16[128,256]{1,0:T(8,128)(2,1)S(1)}, bf16[128,256]{1,0:T(8,128)(2,1)S(1)}, u32[]{:S(2)}, u32[]{:S(2)}) collective-permute-start(bf16[128,256]{1,0:T(8,128)(2,1)S(1)} %get-tuple-element.17), channel_id=1, source_target_pairs={{0,3},{1,0},{2,1},{3,2},{4,7},{5,4},{6,5},{7,6},{8,11},{9,8},{10,9... | collective-permute-start | bytes 196616 | tf_op jit(solution)/shard_map/ppermute | solution.py:29
  38.2 4.9 %collective-permute-start.4 = (bf16[128,256]{1,0:T(8,128)(2,1)S(1)}, bf16[128,256]{1,0:T(8,128)(2,1)S(1)}, u32[]{:S(2)}, u32[]{:S(2)}) collective-permute-start(bf16[128,256]{1,0:T(8,128)(2,1)S(1)} %get-tuple-element.18), channel_id=1, source_target_pairs={{0,2},{1,3},{2,0},{3,1},{4,6},{5,7},{6,4},{7,5},{8,10},{9,11},{10,... | collective-permute-start | bytes 196616 | tf_op jit(solution)/shard_map/ppermute | solution.py:29
  38.8 4.4 %collective-permute-start.3 = (bf16[128,256]{1,0:T(8,128)(2,1)S(1)}, bf16[128,256]{1,0:T(8,128)(2,1)S(1)}, u32[]{:S(2)}, u32[]{:S(2)}) collective-permute-start(bf16[128,256]{1,0:T(8,128)(2,1)S(1)} %get-tuple-element.16), channel_id=1, source_target_pairs={{0,1},{1,2},{2,3},{3,0},{4,5},{5,6},{6,7},{7,4},{8,9},{9,10},{10,1... | collective-permute-start | bytes 196616 | tf_op jit(solution)/shard_map/ppermute | solution.py:29
  38.9 5.5 %collective-permute-start.20 = (bf16[64,896]{1,0:T(8,128)(2,1)S(1)}, bf16[64,896]{1,0:T(8,128)(2,1)S(1)}, u32[]{:S(2)}, u32[]{:S(2)}) collective-permute-start(bf16[64,896]{1,0:T(8,128)(2,1)S(1)} %pad_maximum_fusion.9), channel_id=1, source_target_pairs={{0,1},{1,2},{2,3},{3,0},{4,5},{5,6},{6,7},{7,4},{8,9},{9,10},{10,1... | collective-permute-start | bytes 344072 | tf_op jit(solution)/shard_map/ppermute | solution.py:29
  43.1 4.8 %collective-permute-start.19 = (bf16[64,896]{1,0:T(8,128)(2,1)S(1)}, bf16[64,896]{1,0:T(8,128)(2,1)S(1)}, u32[]{:S(2)}, u32[]{:S(2)}) collective-permute-start(bf16[64,896]{1,0:T(8,128)(2,1)S(1)} %pad_maximum_fusion.9), channel_id=1, source_target_pairs={{0,2},{1,3},{2,0},{3,1},{4,6},{5,7},{6,4},{7,5},{8,10},{9,11},{10,... | collective-permute-start | bytes 344072 | tf_op jit(solution)/shard_map/ppermute | solution.py:29
  43.1 4.8 %collective-permute-start.18 = (bf16[64,896]{1,0:T(8,128)(2,1)S(1)}, bf16[64,896]{1,0:T(8,128)(2,1)S(1)}, u32[]{:S(2)}, u32[]{:S(2)}) collective-permute-start(bf16[64,896]{1,0:T(8,128)(2,1)S(1)} %pad_maximum_fusion.9), channel_id=1, source_target_pairs={{0,3},{1,0},{2,1},{3,2},{4,7},{5,4},{6,5},{7,6},{8,11},{9,8},{10,9... | collective-permute-start | bytes 344072 | tf_op jit(solution)/shard_map/ppermute | solution.py:29
  44.4 6.1 %collective-permute-start.21 = (bf16[256,128]{0,1:T(8,128)(2,1)S(1)}, bf16[256,128]{0,1:T(8,128)(2,1)S(1)}, u32[]{:S(2)}, u32[]{:S(2)}) collective-permute-start(bf16[256,128]{0,1:T(8,128)(2,1)S(1)} %convolution_convert_fusion.4), channel_id=1, source_target_pairs={{0,4},{4,8},{8,12},{12,0},{1,5},{5,9},{9,13},{13,1},{2,6},{6,10},{... | collective-permute-start | bytes 196616 | tf_op jit(solution)/shard_map/ppermute | solution.py:29

commit v2 on v1

--- a/solution.py
+++ b/solution.py
@@ -24,18 +24,12 @@
     return lax.dot_general(left, right, (dims, ((), ())), preferred_element_type=F32)
 
 
-def shift(block, axis, step):
-    size = lax.axis_size(axis)
-    return lax.ppermute(block, axis, [(i, (i + step) % size) for i in range(size)])
-
-
-def gather_parts(block, axis):
-    size = lax.axis_size(axis)
-    return [block] + [shift(block, axis, -step) for step in range(1, size)]
-
-
-def swap_parts(parts, axis):
-    return [parts[0]] + [shift(parts[j], axis, j) for j in range(1, len(parts))]
+def trade(block, axis, step):
+    return lax.ppermute(block, axis, [(i, i ^ step) for i in range(lax.axis_size(axis))])
+
+
+def flip(pair, axis, bit):
+    return jnp.where(bit == 1, jnp.flip(pair, axis), pair)
 
 
 def compact_device(
@@ -55,75 +49,87 @@
     cols = lax.axis_size("col")
     row = lax.axis_index("row")
     col = lax.axis_index("col")
+    low, high = col % 2, col // 2
     nodes, width = features.shape
     slots = target_ids.shape[0]
     share = slots // cols
+    half = slots // 2
     tiles = tile_vals[0, 0]
 
-    feature_parts = gather_parts(features, "row")
-
-    ids = lax.dynamic_slice_in_dim(jnp.concatenate([target_ids, target_ids]), col * share, slots, 0)
+    feature_parts = [features] + [trade(features, "row", s) for s in range(1, rows)]
+
+    ids = jnp.swapaxes(target_ids.reshape(2, 2, share), 0, 1)
+    ids = flip(flip(ids, 0, low), 1, high).reshape(slots)
     place = jnp.arange(cols * nodes, dtype=jnp.int32)
-    slab = (row * cols + (col + place // nodes) % cols) * nodes + place % nodes
+    turn = place // nodes
+    slab = (row * cols + (col ^ (turn // 2 + turn % 2 * 2))) * nodes + place % nodes
     pick_slab = (ids[:, None] == slab[None, :]).astype(BF16)
     pick_own = pick_slab[:, :nodes]
-
-    degree_wide = jnp.broadcast_to(degree.astype(BF16)[:, None], (nodes, 128))
-    known = dot(pick_own, jnp.concatenate([features, cotangent, degree_wide], axis=1)).astype(BF16)
-    known = sum(swap_parts([known[j * share : (j + 1) * share] for j in range(cols)], "col"))
-    feature_slots = known[:, :width]
-    cotangent_slots = known[:, width : 2 * width]
-    degree_slots = known[:, 2 * width :]
+    column = ((row ^ turn) * cols + col) * nodes + place % nodes
+    pick_column = (ids[:, None] == column[None, :]).astype(BF16)
 
     usable = jnp.arange(tiles.shape[0], dtype=jnp.int32) < tile_count[0, 0]
-    src = (tile_src[0, 0] - row) % rows
-    dst = (tile_dst[0, 0] - col) % cols
+    src = tile_src[0, 0] ^ row
+    dst = tile_dst[0, 0] ^ col
     src = jnp.where(usable, src, rows)
+    dst = dst // 2 + dst % 2 * 2
     adjacency = jnp.zeros((rows, cols, nodes, nodes), BF16).at[src, dst].set(tiles, mode="drop")
     adjacency = adjacency.reshape(rows, cols * nodes, nodes)
     picked = [dot(pick_slab, adjacency[s]).astype(BF16) for s in range(rows)]
-    own_columns = sum(swap_parts(picked, "row"))
+
+    degree_wide = jnp.broadcast_to(degree.astype(BF16)[:, None], (nodes, 128))
+    known = dot(pick_own, jnp.concatenate([cotangent, degree_wide], axis=1)).astype(BF16)
 
     slab_features = jnp.concatenate(feature_parts, axis=0)
     part = dot(jnp.concatenate(picked, axis=1), slab_features)
-    part_low = part.astype(BF16)
-    agg_parts = swap_parts(
-        [part[:share]] + [part_low[j * share : (j + 1) * share] for j in range(1, cols)], "col"
-    )
-    agg_sum = sum(piece.astype(F32) for piece in agg_parts)
+    chosen = dot(pick_column, slab_features).astype(BF16)
+    fixed = jnp.concatenate([chosen, known], axis=1)
+    got = trade(jnp.concatenate([part[half:].astype(BF16), fixed[half:]], axis=1), "col", 1)
+    part = part[:half] + got[:, :width].astype(F32)
+    fixed = fixed[:half] + got[:, width:]
+    sent = jnp.concatenate([part[share:].astype(BF16), fixed[share:]], axis=1)
+    sent, picked = lax.optimization_barrier((sent, picked))
+    got = trade(sent, "col", 2)
+    own_columns = picked[0] + sum(trade(picked[s], "row", s) for s in range(1, rows))
+    agg_sum = part[:share] + got[:, :width].astype(F32)
+    fixed = fixed[:share] + got[:, width:]
+    feature_slots = fixed[:, :width]
+    cotangent_slots = fixed[:, width : 2 * width]
+    degree_slots = fixed[:, 2 * width :]
     degree_one = degree_slots[:, :1].astype(F32)
     inverse = jnp.where(degree_one > 0, 1.0 / jnp.maximum(degree_one, 1.0), 0.0)
     aggregate = (agg_sum * inverse).astype(BF16)
     before = dot(feature_slots, w_self) + dot(aggregate, w_neigh) + layer_bias
     slope = (cotangent_slots.astype(F32) * gelu_slope(before)).astype(BF16)
 
-    fixed = jnp.concatenate([feature_slots, degree_slots], axis=1)
-    fixed = sum(gather_parts(fixed, "row"))
-    found = jnp.concatenate([slope, aggregate], axis=1)
-    found = sum(gather_parts(found, "row"))
-    everything = jnp.concatenate(
-        gather_parts(jnp.concatenate([found, fixed], axis=1), "col"), axis=0
-    )
+    found = jnp.concatenate([slope, aggregate, degree_slots], axis=1)
+    found, feature_parts = lax.optimization_barrier((found, feature_parts))
+    found = found + trade(found, "row", 2)
+    found = found + trade(found, "row", 1)
+
+    dense = sum(dot(adjacency[s], feature_parts[s]) for s in range(rows))
+    middle = 2 * nodes
+    dense = dense[:middle] + trade(dense[middle:].astype(BF16), "col", 1).astype(F32)
+    own_sum = dense[:nodes] + trade(dense[nodes:].astype(BF16), "col", 2).astype(F32)
+
+    everything = jnp.concatenate([found, feature_slots], axis=1)
+    everything = jnp.concatenate([everything, trade(everything, "col", 2)], axis=0)
+    everything = jnp.concatenate([everything, trade(everything, "col", 1)], axis=0)
+    own_aggregate = (own_sum * (1.0 / degree.astype(F32))[:, None]).astype(BF16)
+    own_before = dot(features, w_self) + dot(own_aggregate, w_neigh) + layer_bias
+    hidden = gelu_value(own_before).astype(BF16)
+
     slope_all = everything[:, :width]
-    terms = dot(everything[:, width : 3 * width], slope_all, ((0,), (0,)))
+    aggregate_all = everything[:, width : 2 * width]
+    degree_all = everything[:, 2 * width : 2 * width + 1].astype(F32)
+    feature_all = everything[:, -width:]
     scale = 1.0 / math.sqrt(nodes * rows * cols)
-    grad_neigh = terms[:width] * scale
-    grad_self = terms[width:] * scale
+    grad_self = dot(feature_all, slope_all, ((0,), (0,))) * scale
+    grad_neigh = dot(aggregate_all, slope_all, ((0,), (0,))) * scale
     grad_bias = jnp.sum(slope_all.astype(F32), axis=0) * scale
-    degree_all = everything[:, 3 * width : 3 * width + 1].astype(F32)
     message = (dot(slope_all, w_neigh, ((1,), (1,))) / degree_all).astype(BF16)
     own_slope = dot(pick_own, slope_all, ((0,), (0,))).astype(BF16)
     grad_features = dot(own_slope, w_self, ((1,), (1,))) + dot(own_columns, message, ((0,), (0,)))
-
-    dense = sum(dot(adjacency[s], feature_parts[s]) for s in range(rows))
-    dense_low = dense.astype(BF16)
-    dense_parts = swap_parts(
-        [dense[:nodes]] + [dense_low[j * nodes : (j + 1) * nodes] for j in range(1, cols)], "col"
-    )
-    own_sum = sum(piece.astype(F32) for piece in dense_parts)
-    own_aggregate = (own_sum * (1.0 / degree.astype(F32))[:, None]).astype(BF16)
-    own_before = dot(features, w_self) + dot(own_aggregate, w_neigh) + layer_bias
-    hidden = gelu_value(own_before).astype(BF16)
     return (hidden, grad_features.astype(BF16), grad_self, grad_neigh, grad_bias)
 
 

time: 52 us -> 45.8 us (0.88)
  starting transfers between devices: 23.5 us -> 16.5 us
  matrix products: 5.55 us -> 7.47 us
  waiting for transfers between devices: 13.5 us -> 12.2 us
  local copies, waits for them, and re-layouts: 5.22 us -> 6.22 us
  other arithmetic: 2.05 us -> 1.38 us
    ppermute x24 -> x14, starting transfers between devices: 23.5 us -> 16.5 us  [trade(): lax.ppermute(block, axis, [(i, i ^ step) for i in range(lax.axis_size(axi...]
    dot_general x17 -> x19, matrix products: 5.55 us -> 7.47 us  [dot(): lax.dot_general(left, right, (dims, ((), ())), preferred_element_type=F32)]
    ppermute x24 -> x14, waiting for transfers between devices: 13.5 us -> 12.2 us  [trade(): lax.ppermute(block, axis, [(i, i ^ step) for i in range(lax.axis_size(axi...]
    mul x1 -> x0, other arithmetic: 0.84 us -> none  [compact_device(): grad_neigh = terms[:width] * scale]
    unnamed x20 -> x23, local copies, waits for them, and re-layouts: 4.01 us -> 4.78 us
  transfers between devices with their start and end apart: 24 -> 14, of which waited for: 9 -> 5; matrix products, arithmetic and copies ran while one was open for 15% -> 19% of each run, Pallas kernels for 0% -> 0%
where the time goes in v2:
time: 45.8 us; the launch traced here: 45.5 us
  starting transfers between devices  16.5 us (36%)
  waiting for transfers between devices  12.2 us (27%)
  matrix products  7.47 us (16%)
  local copies, waits for them, and re-layouts  6.22 us (14%)
  between operations  1.76 us (4%)
  other arithmetic  1.38 us (3%)
    ppermute x14, starting transfers between devices, trade(): lax.ppermute(block, axis, [(i, i ^ step) for i in range(lax.axis_size(axi...  16.5 us
    ppermute x14, waiting for transfers between devices, trade(): lax.ppermute(block, axis, [(i, i ^ step) for i in range(lax.axis_size(axi...  12.2 us
    dot_general x19, matrix products, dot(): lax.dot_general(left, right, (dims, ((), ())), preferred_element_type=F32)  7.47 us
    unnamed x23, local copies, waits for them, and re-layouts  4.78 us
  transfers between devices with their start and end apart: 14, of which 5 were waited for; matrix products, arithmetic and copies ran while one was open for 19% of the time, Pallas kernels for 0%

profile of v2, /device:TPU:0, one launch (start us, length us, event | category | flops | bytes accessed | tf_op | source)
XLA Modules:
  0.0 45.5 jit_solution(74890426702909528)
XLA Ops:
  0.6 0.0 copy-start
  0.6 3.1 %collective-permute-start = (bf16[128,256]{1,0:T(8,128)(2,1)}, bf16[128,256]{1,0:T(8,128)(2,1)S(1)}, u32[]{:S(2)}, u32[]{:S(2)}) collective-permute-start(bf16[128,256]{1,0:T(8,128)(2,1)} %param.11), channel_id=1, source_target_pairs={{0,4},{4,0},{8,12},{12,8},{1,5},{5,1},{9,13},{13,9},{2,6},{6,2},{1... | collective-permute-start | bytes 196616 | tf_op jit(solution)/shard_map/ppermute | solution.py:28
  3.7 2.6 %collective-permute-start.1 = (bf16[128,256]{1,0:T(8,128)(2,1)}, bf16[128,256]{1,0:T(8,128)(2,1)S(1)}, u32[]{:S(2)}, u32[]{:S(2)}) collective-permute-start(bf16[128,256]{1,0:T(8,128)(2,1)} %param.11), channel_id=1, source_target_pairs={{0,8},{4,12},{8,0},{12,4},{1,9},{5,13},{9,1},{13,5},{2,10},{6,14},... | collective-permute-start | bytes 196616 | tf_op jit(solution)/shard_map/ppermute | solution.py:28
  6.3 0.9 %constant_dynamic-update-slice_fusion.3 = bf16[512,256]{1,0:T(8,128)(2,1)S(1)} fusion(bf16[128,256]{1,0:T(8,128)(2,1)} %param.11), kind=kLoop, calls=%fused_computation.117 | loop fusion | bytes 131072
  7.2 0.7 %copy-done.6 = s32[256]{0:T(256)S(1)} copy-done((s32[256]{0:T(256)S(1)}, s32[256]{0:T(256)}, u32[]{:S(2)}) %copy-start.6) | copy-done | bytes 1048
  7.9 0.1 reshape.207
  8.1 0.1 eq.42
  8.8 0.0 copy-start.7
  8.8 0.6 %copy-done.7 = s32[1,1,8]{2,1,0:T(1,128)S(1)} copy-done((s32[1,1,8]{2,1,0:T(1,128)S(1)}, s32[1,1,8]{2,1,0:T(1,128)}, u32[]{:S(2)}) %copy-start.7) | copy-done | bytes 56
  9.5 0.0 copy-done.8
  9.5 0.0 copy-start.3
  9.5 0.1 broadcast_in_dim.9
  9.6 0.8 %copy-done.3 = bf16[1,1,8,128,128]{4,3,2,1,0:T(8,128)(2,1)S(1)} copy-done((bf16[1,1,8,128,128]{4,3,2,1,0:T(8,128)(2,1)S(1)}, bf16[1,1,8,128,128]{4,3,2,1,0:T(8,128)(2,1)}, u32[]{:S(2)}) %copy-start.3) | copy-done | bytes 262168
  10.4 0.9 %scatter_fusion = bf16[4,4,128,128]{3,2,1,0:T(8,128)(2,1)S(1)} fusion(bf16[4,4,128,128]{3,2,1,0:T(8,128)(2,1)S(1)} %broadcast_in_dim.9, s32[8]{0:T(128)S(1)} %fusion.106, bf16[8,128,128]{2,1,0:T(8,128)(2,1)S(1)} %bitcast.60), kind=kCustom, calls=%fused_computation | custom fusion | bytes 786496 | tf_op jit(solution)/shard_map/scatter | solution.py:76
  11.4 0.1 broadcast_compare_fusion
  11.5 0.3 convolution_convert_fusion.3
  11.8 0.3 convolution_convert_fusion.4
  12.2 0.3 convolution_convert_fusion.5
  12.5 0.0 copy-start.4
  12.5 0.3 convolution_convert_fusion.6
  12.8 0.3 copy-done.9
  13.1 0.1 broadcast_in_dim.11
  13.2 0.1 copy-done.4
  13.3 0.2 convolution_convert_fusion
  13.6 0.3 fusion.14
  13.9 0.4 convolution_convert_fusion.1
  14.3 0.1 copy.19
  14.4 0.1 collective-permute-start.3
  14.5 1.5 %collective-permute-done.3 = bf16[128,896]{1,0:T(8,128)(2,1)S(1)} collective-permute-done((bf16[128,896]{1,0:T(8,128)(2,1)S(1)}, bf16[128,896]{1,0:T(8,128)(2,1)S(1)}, u32[]{:S(2)}, u32[]{:S(2)}) %collective-permute-start.3) | collective-permute-done | bytes 229408 | tf_op jit(solution)/shard_map/ppermute | solution.py:28
  16.1 0.0 copy-start.1
  16.1 1.7 %collective-permute-start.4 = (bf16[64,896]{1,0:T(8,128)(2,1)S(1)}, bf16[64,896]{1,0:T(8,128)(2,1)S(1)}, u32[]{:S(2)}, u32[]{:S(2)}) collective-permute-start(bf16[64,896]{1,0:T(8,128)(2,1)S(1)} %pad_maximum_fusion.3), channel_id=1, source_target_pairs={{0,2},{1,3},{2,0},{3,1},{4,6},{5,7},{6,4},{7,5},{8,10},{9,11},{10,... | collective-permute-start | bytes 344072 | tf_op jit(solution)/shard_map/ppermute | solution.py:28
  17.9 0.2 fusion.113
  18.0 3.3 %collective-permute-done.4 = bf16[64,896]{1,0:T(8,128)(2,1)S(1)} collective-permute-done((bf16[64,896]{1,0:T(8,128)(2,1)S(1)}, bf16[64,896]{1,0:T(8,128)(2,1)S(1)}, u32[]{:S(2)}, u32[]{:S(2)}) %collective-permute-start.4) | collective-permute-done | bytes 114720 | tf_op jit(solution)/shard_map/ppermute | solution.py:28
  21.4 0.1 fusion.79
  21.5 0.1 fusion.72
  21.6 0.7 %copy-done.2 = bf16[256,256]{1,0:T(8,128)(2,1)S(1)} copy-done((bf16[256,256]{1,0:T(8,128)(2,1)S(1)}, bf16[256,256]{1,0:T(8,128)(2,1)}, u32[]{:S(2)}) %copy-start.2) | copy-done | bytes 131096
  22.3 0.1 fusion.114
  22.4 0.5 %copy-done.5 = f32[256]{0:T(256)S(1)} copy-done((f32[256]{0:T(256)S(1)}, f32[256]{0:T(256)}, u32[]{:S(2)}) %copy-start.5) | copy-done | bytes 1048
  23.0 0.2 fusion.69
  23.2 1.9 %collective-permute-start.7 = (bf16[64,640]{1,0:T(8,128)(2,1)S(1)}, bf16[64,640]{1,0:T(8,128)(2,1)S(1)}, u32[]{:S(2)}, u32[]{:S(2)}) collective-permute-start(bf16[64,640]{1,0:T(8,128)(2,1)S(1)} %pad_maximum_fusion.5), channel_id=1, source_target_pairs={{0,8},{4,12},{8,0},{12,4},{1,9},{5,13},{9,1},{13,5},{2,10},{6,14},... | collective-permute-start | bytes 245768 | tf_op jit(solution)/shard_map/ppermute | solution.py:28
  25.1 0.2 fusion.115
  25.3 0.2 fusion.116
  25.5 0.2 fusion.117
  25.8 0.2 fusion.1
  26.0 0.1 collective-permute-start.5
  26.1 3.7 %collective-permute-done.7 = bf16[64,640]{1,0:T(8,128)(2,1)S(1)} collective-permute-done((bf16[64,640]{1,0:T(8,128)(2,1)S(1)}, bf16[64,640]{1,0:T(8,128)(2,1)S(1)}, u32[]{:S(2)}, u32[]{:S(2)}) %collective-permute-start.7) | collective-permute-done | bytes 81952 | tf_op jit(solution)/shard_map/ppermute | solution.py:28
  29.8 0.4 collective-permute-start.8
  30.2 1.7 %collective-permute-start.11 = (bf16[256,128]{0,1:T(8,128)(2,1)S(1)}, bf16[256,128]{0,1:T(8,128)(2,1)S(1)}, u32[]{:S(2)}, u32[]{:S(2)}) collective-permute-start(bf16[256,128]{0,1:T(8,128)(2,1)S(1)} %convolution_convert_fusion.5), channel_id=1, source_target_pairs={{0,4},{4,0},{8,12},{12,8},{1,5},{5,1},{9,13},{13,9},{2,6},{6,2},{1... | collective-permute-start | bytes 196616 | tf_op jit(solution)/shard_map/ppermute | solution.py:28
  31.9 1.3 %collective-permute-start.12 = (bf16[256,128]{0,1:T(8,128)(2,1)S(1)}, bf16[256,128]{0,1:T(8,128)(2,1)S(1)}, u32[]{:S(2)}, u32[]{:S(2)}) collective-permute-start(bf16[256,128]{0,1:T(8,128)(2,1)S(1)} %convolution_convert_fusion.4), channel_id=1, source_target_pairs={{0,8},{4,12},{8,0},{12,4},{1,9},{5,13},{9,1},{13,5},{2,10},{6,14},... | collective-permute-start | bytes 196616 | tf_op jit(solution)/shard_map/ppermute | solution.py:28
  33.2 1.4 %collective-permute-start.13 = (bf16[256,128]{0,1:T(8,128)(2,1)S(1)}, bf16[256,128]{0,1:T(8,128)(2,1)S(1)}, u32[]{:S(2)}, u32[]{:S(2)}) collective-permute-start(bf16[256,128]{0,1:T(8,128)(2,1)S(1)} %convolution_convert_fusion.3), channel_id=1, source_target_pairs={{0,12},{4,8},{8,4},{12,0},{1,13},{5,9},{9,5},{13,1},{2,14},{6,10},... | collective-permute-start | bytes 196616 | tf_op jit(solution)/shard_map/ppermute | solution.py:28
  34.6 0.0 collective-permute-done.8
  34.7 1.6 %collective-permute-start.9 = (bf16[64,896]{1,0:T(8,128)(2,1)S(1)}, bf16[64,896]{1,0:T(8,128)(2,1)S(1)}, u32[]{:S(2)}, u32[]{:S(2)}) collective-permute-start(bf16[64,896]{1,0:T(8,128)(2,1)S(1)} %pad_maximum_fusion.4), channel_id=1, source_target_pairs={{0,2},{1,3},{2,0},{3,1},{4,6},{5,7},{6,4},{7,5},{8,10},{9,11},{10,... | collective-permute-start | bytes 344072 | tf_op jit(solution)/shard_map/ppermute | solution.py:28
  36.3 0.6 %collective-permute-start.6 = (bf16[128,256]{1,0:T(8,128)(2,1)S(1)}, bf16[128,256]{1,0:T(8,128)(2,1)S(1)}, u32[]{:S(2)}, u32[]{:S(2)}) collective-permute-start(bf16[128,256]{1,0:T(8,128)(2,1)S(1)} %slice.208), channel_id=1, source_target_pairs={{0,2},{1,3},{2,0},{3,1},{4,6},{5,7},{6,4},{7,5},{8,10},{9,11},{10,... | collective-permute-start | bytes 196616 | tf_op jit(solution)/shard_map/ppermute | solution.py:28
  36.9 2.6 %collective-permute-done.9 = bf16[64,896]{1,0:T(8,128)(2,1)S(1)} collective-permute-done((bf16[64,896]{1,0:T(8,128)(2,1)S(1)}, bf16[64,896]{1,0:T(8,128)(2,1)S(1)}, u32[]{:S(2)}, u32[]{:S(2)}) %collective-permute-start.9) | collective-permute-done | bytes 114720 | tf_op jit(solution)/shard_map/ppermute | solution.py:28
  39.6 0.1 collective-permute-start.10
  39.6 1.0 %collective-permute-done.6 = bf16[128,256]{1,0:T(8,128)(2,1)S(1)} collective-permute-done((bf16[128,256]{1,0:T(8,128)(2,1)S(1)}, bf16[128,256]{1,0:T(8,128)(2,1)S(1)}, u32[]{:S(2)}, u32[]{:S(2)}) %collective-permute-start.6) | collective-permute-done | bytes 65568 | tf_op jit(solution)/shard_map/ppermute | solution.py:28
  40.6 0.9 %multiply_convert_fusion = bf16[128,256]{1,0:T(8,128)(2,1)} fusion(f32[128,256]{1,0:T(8,128)S(1)} %fusion.113, bf16[256,256]{1,0:T(8,128)(2,1)S(1)} %copy-done.2, f32[256,256]{1,0:T(8,128)S(1)} %slice_add_fusion, bf16[128,256]{1,0:T(8,128)(2,1)S(1)} %collective-permute-done.6, f32[256]{0:T(256)S(1)} %copy-done.5, f32[128]{0:T(128)S(1)} %convert_divide_fusion), kind=kOutput, calls=%fused_computation.80 | convolution fusion | flops 17137664 | bytes 525824 | tf_op jit(solution)/shard_map/dot_general | solution.py:24
  41.5 0.3 fusion.8
  41.9 0.1 convert_reduce_fusion
  41.9 0.9 %convolution_multiply_fusion = f32[256,256]{1,0:T(8,128)} fusion(bf16[128,896]{1,0:T(8,128)(2,1)S(1)} %collective-permute-done.10, bf16[64,896]{1,0:T(8,128)(2,1)S(1)} %collective-permute-done.9, bf16[64,256]{1,0:T(8,128)(2,1)S(1)} %slice.147, bf16[64,640]{1,0:T(8,128)(2,1)S(1)} %add.252, bf16[256,896]{1,0:T(8,128)(2,1)S(1)} %pad_maximum_fusion), kind=kOutput, calls=%fused_computation.5 | convolution fusion | flops 34144256 | bytes 851968 | tf_op jit(solution)/shard_map/dot_general | solution.py:24
  42.9 0.9 %convolution_multiply_fusion.1 = f32[256,256]{1,0:T(8,128)} fusion(bf16[128,896]{1,0:T(8,128)(2,1)S(1)} %collective-permute-done.10, bf16[64,896]{1,0:T(8,128)(2,1)S(1)} %collective-permute-done.9, bf16[64,256]{1,0:T(8,128)(2,1)S(1)} %slice.147, bf16[64,640]{1,0:T(8,128)(2,1)S(1)} %add.252, bf16[256,896]{1,0:T(8,128)(2,1)S(1)} %pad_maximum_fusion), kind=kOutput, calls=%fused_computation.6 | convolution fusion | flops 34144256 | bytes 851968 | tf_op jit(solution)/shard_map/dot_general | solution.py:24
  43.8 0.6 %broadcast_multiply_fusion = f32[256]{0:T(256)} fusion(f32[256]{0:T(256)S(1)} %convert_reduce_fusion), kind=kLoop, calls=%fused_computation.167 | loop fusion | flops 256 | bytes 2048 | tf_op jit(solution)/shard_map/mul | solution.py:129
  44.4 0.1 convert_reduce_fusion.1
  44.5 1.0 %fusion.6 = bf16[128,256]{1,0:T(8,128)(2,1)} fusion(f32[128,256]{1,0:T(8,128)S(1)} %fusion.8, bf16[256,256]{1,0:T(8,128)(2,1)S(1)} %copy-done.2, f32[256]{0:T(256)S(1)} %convert_reduce_fusion.1, bf16[256,896]{1,0:T(8,128)(2,1)S(1)} %pad_maximum_fusion, bf16[256,128]{0,1:T(8,128)(2,1)S(1)} %convolution_convert_fusion.6, ...), kind=kOutput, calls=%fused_computation.14 | convolution fusion | flops 50626560 | bytes 721920 | tf_op jit(solution)/shard_map/dot_general | solution.py:24
  (48 shorter events, 0.5 us)
Async XLA Ops:
  0.6 17.2 %copy-start = (bf16[256,256]{1,0:T(8,128)(2,1)S(1)}, bf16[256,256]{1,0:T(8,128)(2,1)}, u32[]{:S(2)}) copy-start(bf16[256,256]{1,0:T(8,128)(2,1)} %param.12) | copy-start | bytes 393220
  0.6 12.9 %collective-permute-start = (bf16[128,256]{1,0:T(8,128)(2,1)}, bf16[128,256]{1,0:T(8,128)(2,1)S(1)}, u32[]{:S(2)}, u32[]{:S(2)}) collective-permute-start(bf16[128,256]{1,0:T(8,128)(2,1)} %param.11), channel_id=1, source_target_pairs={{0,4},{4,0},{8,12},{12,8},{1,5},{5,1},{9,13},{13,9},{2,6},{6,2},{1... | collective-permute-start | bytes 196616 | tf_op jit(solution)/shard_map/ppermute | solution.py:28
  3.7 9.9 %collective-permute-start.1 = (bf16[128,256]{1,0:T(8,128)(2,1)}, bf16[128,256]{1,0:T(8,128)(2,1)S(1)}, u32[]{:S(2)}, u32[]{:S(2)}) collective-permute-start(bf16[128,256]{1,0:T(8,128)(2,1)} %param.11), channel_id=1, source_target_pairs={{0,8},{4,12},{8,0},{12,4},{1,9},{5,13},{9,1},{13,5},{2,10},{6,14},... | collective-permute-start | bytes 196616 | tf_op jit(solution)/shard_map/ppermute | solution.py:28
  6.3 7.3 %collective-permute-start.2 = (bf16[128,256]{1,0:T(8,128)(2,1)}, bf16[128,256]{1,0:T(8,128)(2,1)S(1)}, u32[]{:S(2)}, u32[]{:S(2)}) collective-permute-start(bf16[128,256]{1,0:T(8,128)(2,1)} %param.11), channel_id=1, source_target_pairs={{0,12},{4,8},{8,4},{12,0},{1,13},{5,9},{9,5},{13,1},{2,14},{6,10},... | collective-permute-start | bytes 196616 | tf_op jit(solution)/shard_map/ppermute | solution.py:28
  7.2 0.7 %copy-start.6 = (s32[256]{0:T(256)S(1)}, s32[256]{0:T(256)}, u32[]{:S(2)}) copy-start(s32[256]{0:T(256)} %param.20) | copy-start | bytes 3076
  8.8 0.7 %copy-start.7 = (s32[1,1,8]{2,1,0:T(1,128)S(1)}, s32[1,1,8]{2,1,0:T(1,128)}, u32[]{:S(2)}) copy-start(s32[1,1,8]{2,1,0:T(1,128)} %param.16) | copy-start | bytes 100
  8.8 0.7 %copy-start.8 = (s32[1,1,8]{2,1,0:T(1,128)S(1)}, s32[1,1,8]{2,1,0:T(1,128)}, u32[]{:S(2)}) copy-start(s32[1,1,8]{2,1,0:T(1,128)} %param.17) | copy-start | bytes 100
  9.5 1.0 %copy-start.3 = (bf16[1,1,8,128,128]{4,3,2,1,0:T(8,128)(2,1)S(1)}, bf16[1,1,8,128,128]{4,3,2,1,0:T(8,128)(2,1)}, u32[]{:S(2)}) copy-start(bf16[1,1,8,128,128]{4,3,2,1,0:T(8,128)(2,1)} %param.15) | copy-start | bytes 786436
  12.5 0.7 %copy-start.9 = (s32[128]{0:T(128)S(1)}, s32[128]{0:T(128)}, u32[]{:S(2)}) copy-start(s32[128]{0:T(128)} %param.19) | copy-start | bytes 1540
  12.5 0.8 %copy-start.4 = (bf16[128,256]{1,0:T(8,128)(2,1)S(1)}, bf16[128,256]{1,0:T(8,128)(2,1)}, u32[]{:S(2)}) copy-start(bf16[128,256]{1,0:T(8,128)(2,1)} %param.21) | copy-start | bytes 196612
  14.4 1.6 %collective-permute-start.3 = (bf16[128,896]{1,0:T(8,128)(2,1)S(1)}, bf16[128,896]{1,0:T(8,128)(2,1)S(1)}, u32[]{:S(2)}, u32[]{:S(2)}) collective-permute-start(bf16[128,896]{1,0:T(8,128)(2,1)S(1)} %fusion.32), channel_id=1, source_target_pairs={{0,1},{1,0},{2,3},{3,2},{4,5},{5,4},{6,7},{7,6},{8,9},{9,8},{10,11... | collective-permute-start | bytes 688136 | tf_op jit(solution)/shard_map/ppermute | solution.py:28
  16.1 1.8 %copy-start.1 = (bf16[128,256]{1,0:T(8,128)(2,1)S(1)}, bf16[128,256]{1,0:T(8,128)(2,1)}, u32[]{:S(2)}) copy-start(bf16[128,256]{1,0:T(8,128)(2,1)} %param.11) | copy-start | bytes 196612
  16.1 5.3 %collective-permute-start.4 = (bf16[64,896]{1,0:T(8,128)(2,1)S(1)}, bf16[64,896]{1,0:T(8,128)(2,1)S(1)}, u32[]{:S(2)}, u32[]{:S(2)}) collective-permute-start(bf16[64,896]{1,0:T(8,128)(2,1)S(1)} %pad_maximum_fusion.3), channel_id=1, source_target_pairs={{0,2},{1,3},{2,0},{3,1},{4,6},{5,7},{6,4},{7,5},{8,10},{9,11},{10,... | collective-permute-start | bytes 344072 | tf_op jit(solution)/shard_map/ppermute | solution.py:28
  21.4 0.9 %copy-start.2 = (bf16[256,256]{1,0:T(8,128)(2,1)S(1)}, bf16[256,256]{1,0:T(8,128)(2,1)}, u32[]{:S(2)}) copy-start(bf16[256,256]{1,0:T(8,128)(2,1)} %param.13) | copy-start | bytes 393220
  22.3 0.7 %copy-start.5 = (f32[256]{0:T(256)S(1)}, f32[256]{0:T(256)}, u32[]{:S(2)}) copy-start(f32[256]{0:T(256)} %param.14) | copy-start | bytes 3076
  23.2 6.6 %collective-permute-start.7 = (bf16[64,640]{1,0:T(8,128)(2,1)S(1)}, bf16[64,640]{1,0:T(8,128)(2,1)S(1)}, u32[]{:S(2)}, u32[]{:S(2)}) collective-permute-start(bf16[64,640]{1,0:T(8,128)(2,1)S(1)} %pad_maximum_fusion.5), channel_id=1, source_target_pairs={{0,8},{4,12},{8,0},{12,4},{1,9},{5,13},{9,1},{13,5},{2,10},{6,14},... | collective-permute-start | bytes 245768 | tf_op jit(solution)/shard_map/ppermute | solution.py:28
  26.0 10.2 %collective-permute-start.5 = (bf16[256,256]{1,0:T(8,128)(2,1)S(1)}, bf16[256,256]{1,0:T(8,128)(2,1)S(1)}, u32[]{:S(2)}, u32[]{:S(2)}) collective-permute-start(bf16[256,256]{1,0:T(8,128)(2,1)S(1)} %slice.207), channel_id=1, source_target_pairs={{0,1},{1,0},{2,3},{3,2},{4,5},{5,4},{6,7},{7,6},{8,9},{9,8},{10,11... | collective-permute-start | bytes 393224 | tf_op jit(solution)/shard_map/ppermute | solution.py:28
  29.8 4.8 %collective-permute-start.8 = (bf16[64,640]{1,0:T(8,128)(2,1)S(1)}, bf16[64,640]{1,0:T(8,128)(2,1)S(1)}, u32[]{:S(2)}, u32[]{:S(2)}) collective-permute-start(bf16[64,640]{1,0:T(8,128)(2,1)S(1)} %add.251), channel_id=1, source_target_pairs={{0,4},{4,0},{8,12},{12,8},{1,5},{5,1},{9,13},{13,9},{2,6},{6,2},{1... | collective-permute-start | bytes 245768 | tf_op jit(solution)/shard_map/ppermute | solution.py:28
  30.2 14.3 %collective-permute-start.11 = (bf16[256,128]{0,1:T(8,128)(2,1)S(1)}, bf16[256,128]{0,1:T(8,128)(2,1)S(1)}, u32[]{:S(2)}, u32[]{:S(2)}) collective-permute-start(bf16[256,128]{0,1:T(8,128)(2,1)S(1)} %convolution_convert_fusion.5), channel_id=1, source_target_pairs={{0,4},{4,0},{8,12},{12,8},{1,5},{5,1},{9,13},{13,9},{2,6},{6,2},{1... | collective-permute-start | bytes 196616 | tf_op jit(solution)/shard_map/ppermute | solution.py:28
  31.9 12.5 %collective-permute-start.12 = (bf16[256,128]{0,1:T(8,128)(2,1)S(1)}, bf16[256,128]{0,1:T(8,128)(2,1)S(1)}, u32[]{:S(2)}, u32[]{:S(2)}) collective-permute-start(bf16[256,128]{0,1:T(8,128)(2,1)S(1)} %convolution_convert_fusion.4), channel_id=1, source_target_pairs={{0,8},{4,12},{8,0},{12,4},{1,9},{5,13},{9,1},{13,5},{2,10},{6,14},... | collective-permute-start | bytes 196616 | tf_op jit(solution)/shard_map/ppermute | solution.py:28
  33.2 11.3 %collective-permute-start.13 = (bf16[256,128]{0,1:T(8,128)(2,1)S(1)}, bf16[256,128]{0,1:T(8,128)(2,1)S(1)}, u32[]{:S(2)}, u32[]{:S(2)}) collective-permute-start(bf16[256,128]{0,1:T(8,128)(2,1)S(1)} %convolution_convert_fusion.3), channel_id=1, source_target_pairs={{0,12},{4,8},{8,4},{12,0},{1,13},{5,9},{9,5},{13,1},{2,14},{6,10},... | collective-permute-start | bytes 196616 | tf_op jit(solution)/shard_map/ppermute | solution.py:28
  34.7 4.9 %collective-permute-start.9 = (bf16[64,896]{1,0:T(8,128)(2,1)S(1)}, bf16[64,896]{1,0:T(8,128)(2,1)S(1)}, u32[]{:S(2)}, u32[]{:S(2)}) collective-permute-start(bf16[64,896]{1,0:T(8,128)(2,1)S(1)} %pad_maximum_fusion.4), channel_id=1, source_target_pairs={{0,2},{1,3},{2,0},{3,1},{4,6},{5,7},{6,4},{7,5},{8,10},{9,11},{10,... | collective-permute-start | bytes 344072 | tf_op jit(solution)/shard_map/ppermute | solution.py:28
  36.3 4.3 %collective-permute-start.6 = (bf16[128,256]{1,0:T(8,128)(2,1)S(1)}, bf16[128,256]{1,0:T(8,128)(2,1)S(1)}, u32[]{:S(2)}, u32[]{:S(2)}) collective-permute-start(bf16[128,256]{1,0:T(8,128)(2,1)S(1)} %slice.208), channel_id=1, source_target_pairs={{0,2},{1,3},{2,0},{3,1},{4,6},{5,7},{6,4},{7,5},{8,10},{9,11},{10,... | collective-permute-start | bytes 196616 | tf_op jit(solution)/shard_map/ppermute | solution.py:28
  39.6 1.9 %collective-permute-start.10 = (bf16[128,896]{1,0:T(8,128)(2,1)S(1)}, bf16[128,896]{1,0:T(8,128)(2,1)S(1)}, u32[]{:S(2)}, u32[]{:S(2)}) collective-permute-start(bf16[128,896]{1,0:T(8,128)(2,1)S(1)} %pad_maximum_fusion.2), channel_id=1, source_target_pairs={{0,1},{1,0},{2,3},{3,2},{4,5},{5,4},{6,7},{7,6},{8,9},{9,8},{10,11... | collective-permute-start | bytes 688136 | tf_op jit(solution)/shard_map/ppermute | solution.py:28

commit v3 on v0

--- a/solution.py
+++ b/solution.py
@@ -1,9 +1,16 @@
+import functools
+import itertools
 import math
 
 import jax
 import jax.numpy as jnp
 from jax import lax
+from jax.experimental import pallas as pl
+from jax.experimental.pallas import tpu as pltpu
 from jax.sharding import PartitionSpec as P
+
+F32 = jnp.float32
+BF16 = jnp.bfloat16
 
 
 def gelu_value(inputs):
@@ -15,6 +22,271 @@
         0.5 * (1.0 + jax.scipy.special.erf(inputs * 0.7071067811865476))
         + inputs * jnp.exp(-0.5 * inputs * inputs) * 0.3989422804014327
     )
+
+
+def dot(left, right, dims=((1,), (0,))):
+    return lax.dot_general(left, right, (dims, ((), ())), preferred_element_type=F32)
+
+
+def trade(block, axis, step):
+    return lax.ppermute(block, axis, [(i, i ^ step) for i in range(lax.axis_size(axis))])
+
+
+def flip(pair, axis, bit):
+    return jnp.where(bit == 1, jnp.flip(pair, axis), pair)
+
+
+def call(kernel, outputs, *inputs, spaces=(), scratch=()):
+    inputs = [
+        pltpu.with_memory_space_constraint(x, y) if y == pltpu.HBM else x
+        for x, y in itertools.zip_longest(inputs, spaces)
+    ]
+    spaces = list(spaces) + [pltpu.VMEM] * (len(inputs) - len(spaces))
+    return pl.pallas_call(
+        kernel,
+        out_shape=[jax.ShapeDtypeStruct(shape, dtype) for shape, dtype in outputs],
+        in_specs=[pl.BlockSpec(memory_space=space) for space in spaces],
+        out_specs=[pl.BlockSpec(memory_space=pltpu.VMEM) for _ in outputs],
+        scratch_shapes=scratch,
+        compiler_params=pltpu.CompilerParams(vmem_limit_bytes=32 * 2**20),
+    )(*inputs)
+
+
+def spread(block, axis):
+    return [trade(block, axis, step) for step in range(lax.axis_size(axis) - 1, 0, -1)]
+
+
+def swap_bits(index):
+    return index // 2 + index % 2 * 2
+
+
+def select(rows, cols, ids_in, src_in, dst_in, count_in, tiles_in, cotangent_in, degree_in, *refs):
+    weights_in, refs = refs[:3], refs[3:]
+    adjacency, column_picks, own_picks, known = refs[:4]
+    picked, refs = refs[4 : 4 + rows], refs[4 + rows :]
+    weights, (picks, src, dst, count, tiles, cotangent, degree, ids, sems) = refs[:3], refs[3:]
+    pairs = [(src_in, src), (dst_in, dst), (count_in, count), (tiles_in, tiles)]
+    pairs += [(cotangent_in, cotangent), (degree_in, degree), (ids_in, ids)]
+    pairs += list(zip(weights_in, weights))
+    copies = [pltpu.make_async_copy(a, b, sems.at[i]) for i, (a, b) in enumerate(pairs)]
+    for copy in copies:
+        copy.start()
+    row, col = lax.axis_index("row"), lax.axis_index("col")
+    share, nodes, width = ids.shape[1], cotangent.shape[0], cotangent.shape[1]
+    slots = share * cols
+    adjacency[...] = jnp.zeros(adjacency.shape, adjacency.dtype)
+    for copy in copies[:7]:
+        copy.wait()
+    for k in range(tiles.shape[2]):
+
+        @pl.when(k < count[0, 0])
+        def _():
+            down = pl.multiple_of(swap_bits(dst[0, 0, k] ^ col) * nodes, nodes)
+            adjacency[src[0, 0, k] ^ row, pl.ds(down, nodes), :] = tiles[0, 0, k]
+
+    lanes = lax.broadcasted_iota(jnp.int32, (share, nodes), 1)
+    across = lax.broadcasted_iota(jnp.int32, (nodes, share), 0)
+    for p in range(cols):
+        here = pl.ds(p * share, share)
+        line = jnp.broadcast_to(ids[pl.ds(col ^ swap_bits(p), 1), :], (nodes, share))
+        stack = line.T
+        for k in range(cols):
+            base = (row * cols + (col ^ swap_bits(k))) * nodes
+            picks[here, k * nodes : (k + 1) * nodes] = (stack == lanes + base).astype(BF16)
+        for s in range(rows):
+            base = ((row ^ s) * cols + col) * nodes
+            column_picks[here, s * nodes : (s + 1) * nodes] = (stack == lanes + base).astype(BF16)
+        base = (row * cols + col) * nodes
+        own_picks[:, here] = (line == across + base).astype(BF16)
+    for s in range(rows):
+        picked[s][...] = dot(picks[...], adjacency[s]).astype(BF16)
+    own = picks[:, :nodes]
+    known[:, :width] = dot(own, cotangent[...]).astype(BF16)
+    for copy in copies[7:]:
+        copy.wait()
+    counts = degree[...].astype(F32)
+    counts = jnp.sum(own.astype(F32) * counts, axis=1, keepdims=True)
+    known[:, width:] = jnp.broadcast_to(counts, (slots, 128)).astype(BF16)
+
+
+def combine(rows, *refs):
+    column_picks, known, *rest = refs
+    features, picked = rest[:rows][::-1], rest[rows : 2 * rows]
+    sent, part, fixed = rest[2 * rows :]
+    nodes, width = features[0].shape
+    half = part.shape[0]
+    sums = sum(dot(picked[s][...], features[s][...]) for s in range(rows))
+    chosen = sum(
+        dot(column_picks[:, s * nodes : (s + 1) * nodes], features[s][...]) for s in range(rows)
+    ).astype(BF16)
+    part[...] = sums[:half]
+    fixed[:, :width] = chosen[:half]
+    fixed[:, width:] = known[:half, :]
+    sent[:, :width] = sums[half:].astype(BF16)
+    sent[:, width : 2 * width] = chosen[half:]
+    sent[:, 2 * width :] = known[half:, :]
+
+
+def relay(part, fixed, got, sent, part_out, fixed_out):
+    share, width = part_out.shape
+    sums = part[...] + got[:, :width].astype(F32)
+    rest = fixed[...] + got[:, width:]
+    part_out[...] = sums[:share]
+    fixed_out[...] = rest[:share]
+    sent[:, :width] = sums[share:].astype(BF16)
+    sent[:, width:] = rest[share:]
+
+
+def slopes(part, fixed, got, w_self, w_neigh, layer_bias, found, features):
+    width = part.shape[1]
+    total = part[...] + got[:, :width].astype(F32)
+    rest = fixed[...] + got[:, width:]
+    features[...] = rest[:, :width]
+    cotangent = rest[:, width : 2 * width].astype(F32)
+    degrees = rest[:, 2 * width :]
+    degree = degrees[:, :1].astype(F32)
+    inverse = jnp.where(degree > 0, 1.0 / jnp.maximum(degree, 1.0), 0.0)
+    aggregate = (total * inverse).astype(BF16)
+    before = dot(rest[:, :width], w_self[...]) + dot(aggregate, w_neigh[...]) + layer_bias[...]
+    found[:, :width] = (cotangent * gelu_slope(before)).astype(BF16)
+    found[:, width : 2 * width] = aggregate
+    found[:, 2 * width :] = degrees
+
+
+def merge(*refs):
+    *parts, features, everything = refs
+    width = features.shape[1]
+    everything[:, :-width] = sum(part[...] for part in parts)
+    everything[:, -width:] = features[...]
+
+
+def finish(scale, mine, other, own_columns, own_picks, w_self, w_neigh, *outs):
+    grad_features, grad_self, grad_neigh, grad_bias = outs
+    width = w_self.shape[0]
+    half = mine.shape[0]
+    front, back = ((0,), (0,)), ((1,), (1,))
+    slope = [mine[:, :width], other[:, :width]]
+    both = (mine, other)
+    pairs = list(zip(both, slope))
+    grad_self[...] = sum(dot(e[:, -width:], g, front) for e, g in pairs) * scale
+    grad_neigh[...] = sum(dot(e[:, width : 2 * width], g, front) for e, g in pairs) * scale
+    grad_bias[...] = sum(jnp.sum(g.astype(F32), axis=0, keepdims=True) for g in slope) * scale
+    own_slope = dot(own_picks[:, :half], slope[0]) + dot(own_picks[:, half:], slope[1])
+    total = dot(own_slope.astype(BF16), w_self[...], back)
+    for j, (e, g) in enumerate(pairs):
+        degree = e[:, 2 * width : 2 * width + 1].astype(F32)
+        message = (dot(g, w_neigh[...], back) / degree).astype(BF16)
+        total += dot(own_columns[j * half : (j + 1) * half, :], message, front)
+    grad_features[...] = total.astype(BF16)
+
+
+def compact_device(
+    features,
+    w_self,
+    w_neigh,
+    layer_bias,
+    tile_vals,
+    tile_dst,
+    tile_src,
+    tile_count,
+    degree,
+    target_ids,
+    cotangent,
+):
+    rows = lax.axis_size("row")
+    cols = lax.axis_size("col")
+    nodes, width = features.shape
+    slots = target_ids.shape[0]
+    share = slots // cols
+    half = slots // 2
+
+    feature_parts = spread(features, "row") + [features]
+
+    bias = layer_bias.reshape(1, width)
+    adjacency, column_picks, own_picks, known, *picked = call(
+        functools.partial(select, rows, cols),
+        [
+            ((rows, cols * nodes, nodes), BF16),
+            ((slots, rows * nodes), BF16),
+            ((nodes, slots), BF16),
+            ((slots, width + 128), BF16),
+        ]
+        + [((slots, nodes), BF16)] * rows
+        + [((width, width), BF16)] * 2
+        + [((1, width), F32)],
+        target_ids.reshape(cols, share),
+        tile_src,
+        tile_dst,
+        tile_count,
+        tile_vals,
+        cotangent,
+        degree.reshape(1, nodes),
+        w_self,
+        w_neigh,
+        bias,
+        spaces=[pl.ANY] + [pltpu.HBM] * 2 + [pl.ANY] + [pltpu.HBM] * 6,
+        scratch=[pltpu.VMEM((slots, cols * nodes), BF16)]
+        + [pltpu.SMEM(x.shape, x.dtype) for x in (tile_src, tile_dst, tile_count)]
+        + [pltpu.VMEM(x.shape, x.dtype) for x in (tile_vals, cotangent)]
+        + [pltpu.VMEM((1, nodes), jnp.int32), pltpu.VMEM((cols, share), jnp.int32)]
+        + [pltpu.SemaphoreType.DMA((10,))],
+    )
+    *picked, w_self, w_neigh, bias = picked
+    own_columns = sum(trade(picked[s], "row", s) for s in range(rows - 1, 0, -1)) + picked[0]
+    sent, part, fixed = call(
+        functools.partial(combine, rows),
+        [((half, 2 * width + width + 128), BF16), ((half, width), F32), ((half, 2 * width + 128), BF16)],
+        column_picks,
+        known,
+        *feature_parts,
+        *picked,
+    )
+    got = trade(sent, "col", 1)
+    sent, part, fixed = call(
+        relay,
+        [((share, 3 * width + 128), BF16), ((share, width), F32), ((share, 2 * width + 128), BF16)],
+        part,
+        fixed,
+        got,
+    )
+    sent, feature_parts = lax.optimization_barrier((sent, feature_parts))
+    got = trade(sent, "col", 2)
+    found, feature_slots = call(
+        slopes,
+        [((share, 2 * width + 128), BF16), ((share, width), BF16)],
+        part,
+        fixed,
+        got,
+        w_self,
+        w_neigh,
+        bias,
+    )
+    (everything,) = call(
+        merge, [((share, 3 * width + 128), BF16)], *spread(found, "row"), found, feature_slots
+    )
+
+    dense = sum(dot(adjacency[s], feature_parts[-1 - s]) for s in range(rows))
+    middle = 2 * nodes
+    dense = dense[:middle] + trade(dense[middle:].astype(BF16), "col", 1).astype(F32)
+    own_sum = dense[:nodes] + trade(dense[nodes:].astype(BF16), "col", 2).astype(F32)
+
+    everything = jnp.concatenate([everything, trade(everything, "col", 2)], axis=0)
+    other = trade(everything, "col", 1)
+    own_aggregate = (own_sum * (1.0 / degree.astype(F32))[:, None]).astype(BF16)
+    own_before = dot(features, w_self) + dot(own_aggregate, w_neigh) + bias
+    hidden = gelu_value(own_before).astype(BF16)
+
+    grad_features, grad_self, grad_neigh, grad_bias = call(
+        functools.partial(finish, 1.0 / math.sqrt(nodes * rows * cols)),
+        [((nodes, width), BF16), ((width, width), F32), ((width, width), F32), ((1, width), F32)],
+        everything,
+        other,
+        own_columns,
+        own_picks,
+        w_self,
+        w_neigh,
+    )
+    return (hidden, grad_features, grad_self, grad_neigh, grad_bias.reshape(width))
 
 
 def tile_sum(values, take_index, put_index, usable, source, out_tiles, transpose, first_tile):
@@ -44,7 +316,7 @@
     return running.reshape(out_tiles * tile_width, columns)
 
 
-def per_device(
+def dense_device(
     features,
     w_self,
     w_neigh,
@@ -155,6 +427,8 @@
         P("groups", None),
         P("groups"),
     )
+    parts = mesh.shape["row"] * mesh.shape["col"]
+    per_device = compact_device if parts <= 16 else dense_device
     return jax.shard_map(
         per_device, mesh=mesh, in_specs=in_specs, out_specs=out_specs, check_vma=False
     )

time: 184 us -> 40.3 us (0.22)
  waiting for transfers between devices: 95.3 us -> 13.2 us
  blocking collectives: 54.5 us -> 0 us
  starting transfers between devices: 0.12 us -> 18.7 us
  between operations: 14.7 us -> 1.45 us
  local copies, waits for them, and re-layouts: 7.4 us -> 1.54 us
  matrix products: 6.39 us -> 1.34 us
  other arithmetic: 5.12 us -> 0.07 us
  Pallas kernels: 0 us -> 3.89 us
    psum x1 -> x0, waiting for transfers between devices: 53.9 us -> none  [per_device(): lax.psum((self_term, neigh_term, bias_term), ('row', 'col'))]
    reduce_scatter x2 -> x0, waiting for transfers between devices: 41.3 us -> none  [the longest x1 21.6 us: per_device(): lax.psum_scatter(partial_value, 'col', scatter_dimension=0, tiled=True)]
    psum x1 -> x0, blocking collectives: 32.9 us -> none  [per_device(): lax.psum((self_term, neigh_term, bias_term), ('row', 'col'))]
    all_gather x2 -> x0, blocking collectives: 21.6 us -> none  [the longest x1 15.8 us: per_device(): source = lax.all_gather(features, 'row', axis=0, tiled=True)]
    ppermute x0 -> x15, starting transfers between devices: none -> 18.7 us  [trade(): lax.ppermute(block, axis, [(i, i ^ step) for i in range(lax.axis_size(axi...]
    ppermute x0 -> x15, waiting for transfers between devices: none -> 13.2 us  [trade(): lax.ppermute(block, axis, [(i, i ^ step) for i in range(lax.axis_size(axi...]
    dot_general x8 -> x6, matrix products: 6.39 us -> 1.34 us  [dot(): lax.dot_general(left, right, (dims, ((), ())), preferred_element_type=F32)]
    unnamed x28 -> x5, local copies, waits for them, and re-layouts: 5.51 us -> 0.76 us
  transfers between devices with their start and end apart: 3 -> 15, of which waited for: 3 -> 6; matrix products, arithmetic and copies ran while one was open for 3% -> 7% of each run, Pallas kernels for 0% -> 7%
where the time goes in v3:
time: 40.3 us; the launch traced here: 40.2 us
  starting transfers between devices  18.7 us (46%)
  waiting for transfers between devices  13.2 us (33%)
  Pallas kernels  3.89 us (10%)
  local copies, waits for them, and re-layouts  1.54 us (4%)
  between operations  1.45 us (4%)
  matrix products  1.34 us (3%)
    ppermute x15, starting transfers between devices, trade(): lax.ppermute(block, axis, [(i, i ^ step) for i in range(lax.axis_size(axi...  18.7 us
    ppermute x15, waiting for transfers between devices, trade(): lax.ppermute(block, axis, [(i, i ^ step) for i in range(lax.axis_size(axi...  13.2 us
    pallas_call x6, Pallas kernels, call(): pl.pallas_call(kernel, out_shape=[jax.ShapeDtypeStruct(shape, dtype) for...  3.89 us
    dot_general x6, matrix products, dot(): lax.dot_general(left, right, (dims, ((), ())), preferred_element_type=F32)  1.34 us
  transfers between devices with their start and end apart: 15, of which 6 were waited for; matrix products, arithmetic and copies ran while one was open for 7% of the time, Pallas kernels for 7%

profile of v3, /device:TPU:0, one launch (start us, length us, event | category | flops | bytes accessed | tf_op | source)
XLA Modules:
  0.0 40.2 jit_solution(11807863627929398930)
XLA Ops:
  0.6 5.1 %collective-permute-start = (bf16[128,256]{1,0:T(8,128)(2,1)}, bf16[128,256]{1,0:T(8,128)(2,1)S(1)}, u32[]{:S(2)}, u32[]{:S(2)}) collective-permute-start(bf16[128,256]{1,0:T(8,128)(2,1)} %refs_5_.1), channel_id=1, source_target_pairs={{0,12},{4,8},{8,4},{12,0},{1,13},{5,9},{9,5},{13,1},{2,14},{6,10},... | collective-permute-start | bytes 196616 | tf_op jit(solution)/shard_map/ppermute | solution.py:32
  5.7 0.0 collective-permute-start.1
  5.7 0.6 %collective-permute-start.2 = (bf16[128,256]{1,0:T(8,128)(2,1)}, bf16[128,256]{1,0:T(8,128)(2,1)S(1)}, u32[]{:S(2)}, u32[]{:S(2)}) collective-permute-start(bf16[128,256]{1,0:T(8,128)(2,1)} %refs_5_.1), channel_id=1, source_target_pairs={{0,4},{4,0},{8,12},{12,8},{1,5},{5,1},{9,13},{13,9},{2,6},{6,2},{1... | collective-permute-start | bytes 196616 | tf_op jit(solution)/shard_map/ppermute | solution.py:32
  6.4 0.8 %reshape.23.ids_in = s32[4,64]{1,0:T(4,128)S(1)} reshape(s32[256]{0:T(256)} %param.20) | data formatting | bytes 2048 | tf_op jit(solution)/shard_map/reshape | solution.py:217
  7.8 0.0 copy-start
  7.8 1.9 %shard_map.146 = (bf16[4,512,128]{2,1,0:T(8,128)(2,1)S(1)}, bf16[256,512]{1,0:T(8,128)(2,1)S(1)}, bf16[128,256]{1,0:T(8,128)(2,1)S(1)}, bf16[256,384]{1,0:T(8,12...) custom-call(s32[4,64]{1,0:T(4,128)S(1)} %reshape.23.ids_in, ...), custom_call_target="tpu_custom_call" | custom-call | tf_op jit(solution)/shard_map/pallas_call | solution.py:45
  9.7 0.0 copy-start.1
  9.7 3.8 %collective-permute-start.12 = (bf16[256,128]{1,0:T(8,128)(2,1)S(1)}, bf16[256,128]{1,0:T(8,128)(2,1)S(1)}, u32[]{:S(2)}, u32[]{:S(2)}) collective-permute-start(bf16[256,128]{1,0:T(8,128)(2,1)S(1)} %get-tuple-element.40.refs_9_), channel_id=1, source_target_pairs={{0,12},{4,8},{8,4},{12,0},{1,13},{5,9},{9,5},{13,1},{2,14},{6,10},... | collective-permute-start | bytes 196616 | tf_op jit(solution)/shard_map/ppermute | solution.py:32
  13.5 0.0 collective-permute-start.13
  13.5 0.0 copy-done.1
  13.6 0.0 collective-permute-done.refs_2_
  13.6 0.7 %collective-permute-start.14 = (bf16[256,128]{1,0:T(8,128)(2,1)S(1)}, bf16[256,128]{1,0:T(8,128)(2,1)S(1)}, u32[]{:S(2)}, u32[]{:S(2)}) collective-permute-start(bf16[256,128]{1,0:T(8,128)(2,1)S(1)} %get-tuple-element.38.refs_7_), channel_id=1, source_target_pairs={{0,4},{4,0},{8,12},{12,8},{1,5},{5,1},{9,13},{13,9},{2,6},{6,2},{1... | collective-permute-start | bytes 196616 | tf_op jit(solution)/shard_map/ppermute | solution.py:32
  14.3 0.0 collective-permute-done.1.refs_3_
  14.3 0.0 collective-permute-done.2.refs_4_
  14.3 0.0 copy-done
  14.3 0.4 %shard_map.147 = (bf16[128,896]{1,0:T(8,128)(2,1)S(1)}, f32[128,256]{1,0:T(8,128)S(1)}, bf16[128,640]{1,0:T(8,128)(2,1)S(1)}) custom-call(bf16[256,512]{1,0:T(8,128)(2,1)S(1)} %get-tuple-element.35.refs_0_, bf16[256,384]{1,0:T(8,128)(2,1)S(1)} %get-tuple-element.36.refs_1_, bf16[128,256]{1,0:T(8,128)(2,1)S(1)} %collective-permute-done.refs_2_, ...), custom_call_target="tpu_custom_call" | custom-call | tf_op jit(solution)/shard_map/pallas_call | solution.py:45
  14.7 0.1 collective-permute-start.3
  14.8 0.2 convolution_bitcast_fusion
  15.0 1.3 %collective-permute-done.3.got = bf16[128,896]{1,0:T(8,128)(2,1)S(1)} collective-permute-done((bf16[128,896]{1,0:T(8,128)(2,1)S(1)}, bf16[128,896]{1,0:T(8,128)(2,1)S(1)}, u32[]{:S(2)}, u32[]{:S(2)}) %collective-permute-start.3) | collective-permute-done | bytes 229408 | tf_op jit(solution)/shard_map/ppermute | solution.py:32
  16.3 1.6 %collective-permute-start.6 = (bf16[64,896]{1,0:T(8,128)(2,1)S(1)}, bf16[64,896]{1,0:T(8,128)(2,1)S(1)}, u32[]{:S(2)}, u32[]{:S(2)}) collective-permute-start(bf16[64,896]{1,0:T(8,128)(2,1)S(1)} %get-tuple-element.53), channel_id=1, source_target_pairs={{0,2},{1,3},{2,0},{3,1},{4,6},{5,7},{6,4},{7,5},{8,10},{9,11},{10,... | collective-permute-start | bytes 344072 | tf_op jit(solution)/shard_map/ppermute | solution.py:32
  17.9 0.2 fusion.9
  18.1 0.2 fusion.7
  18.4 0.2 fusion.5
  18.6 0.2 fusion.1
  18.8 0.1 collective-permute-start.4
  18.9 2.6 %collective-permute-done.6.got = bf16[64,896]{1,0:T(8,128)(2,1)S(1)} collective-permute-done((bf16[64,896]{1,0:T(8,128)(2,1)S(1)}, bf16[64,896]{1,0:T(8,128)(2,1)S(1)}, u32[]{:S(2)}, u32[]{:S(2)}) %collective-permute-start.6) | collective-permute-done | bytes 114720 | tf_op jit(solution)/shard_map/ppermute | solution.py:32
  21.6 0.2 shard_map.149
  21.8 3.8 %collective-permute-start.7 = (bf16[64,640]{1,0:T(8,128)(2,1)S(1)}, bf16[64,640]{1,0:T(8,128)(2,1)S(1)}, u32[]{:S(2)}, u32[]{:S(2)}) collective-permute-start(bf16[64,640]{1,0:T(8,128)(2,1)S(1)} %get-tuple-element.54.refs_3_), channel_id=1, source_target_pairs={{0,12},{4,8},{8,4},{12,0},{1,13},{5,9},{9,5},{13,1},{2,14},{6,10},... | collective-permute-start | bytes 245768 | tf_op jit(solution)/shard_map/ppermute | solution.py:32
  25.6 0.0 collective-permute-done.12
  25.6 0.0 collective-permute-start.8
  25.6 0.0 collective-permute-done.13
  25.6 0.7 %collective-permute-start.9 = (bf16[64,640]{1,0:T(8,128)(2,1)S(1)}, bf16[64,640]{1,0:T(8,128)(2,1)S(1)}, u32[]{:S(2)}, u32[]{:S(2)}) collective-permute-start(bf16[64,640]{1,0:T(8,128)(2,1)S(1)} %get-tuple-element.54.refs_3_), channel_id=1, source_target_pairs={{0,4},{4,0},{8,12},{12,8},{1,5},{5,1},{9,13},{13,9},{2,6},{6,2},{1... | collective-permute-start | bytes 245768 | tf_op jit(solution)/shard_map/ppermute | solution.py:32
  26.3 0.0 collective-permute-done.14
  26.3 2.3 %collective-permute-done.7.refs_0_ = bf16[64,640]{1,0:T(8,128)(2,1)S(1)} collective-permute-done((bf16[64,640]{1,0:T(8,128)(2,1)S(1)}, bf16[64,640]{1,0:T(8,128)(2,1)S(1)}, u32[]{:S(2)}, u32[]{:S(2)}) %collective-permute-start.7) | collective-permute-done | bytes 81952 | tf_op jit(solution)/shard_map/ppermute | solution.py:32
  28.5 3.4 %collective-permute-done.8.refs_1_ = bf16[64,640]{1,0:T(8,128)(2,1)S(1)} collective-permute-done((bf16[64,640]{1,0:T(8,128)(2,1)S(1)}, bf16[64,640]{1,0:T(8,128)(2,1)S(1)}, u32[]{:S(2)}, u32[]{:S(2)}) %collective-permute-start.8) | collective-permute-done | bytes 81952 | tf_op jit(solution)/shard_map/ppermute | solution.py:32
  31.9 0.0 collective-permute-done.9.refs_2_
  31.9 1.6 %collective-permute-start.10 = (bf16[64,896]{1,0:T(8,128)(2,1)S(1)}, bf16[64,896]{1,0:T(8,128)(2,1)S(1)}, u32[]{:S(2)}, u32[]{:S(2)}) collective-permute-start(bf16[64,896]{1,0:T(8,128)(2,1)S(1)} %shard_map.150), channel_id=1, source_target_pairs={{0,2},{1,3},{2,0},{3,1},{4,6},{5,7},{6,4},{7,5},{8,10},{9,11},{10,... | collective-permute-start | bytes 344072 | tf_op jit(solution)/shard_map/ppermute | solution.py:32
  33.5 0.0 collective-permute-done.4
  33.5 0.6 %collective-permute-start.5 = (bf16[128,256]{1,0:T(8,128)(2,1)S(1)}, bf16[128,256]{1,0:T(8,128)(2,1)S(1)}, u32[]{:S(2)}, u32[]{:S(2)}) collective-permute-start(bf16[128,256]{1,0:T(8,128)(2,1)S(1)} %slice.64), channel_id=1, source_target_pairs={{0,2},{1,3},{2,0},{3,1},{4,6},{5,7},{6,4},{7,5},{8,10},{9,11},{10,... | collective-permute-start | bytes 196616 | tf_op jit(solution)/shard_map/ppermute | solution.py:32
  34.1 3.0 %collective-permute-done.10 = bf16[64,896]{1,0:T(8,128)(2,1)S(1)} collective-permute-done((bf16[64,896]{1,0:T(8,128)(2,1)S(1)}, bf16[64,896]{1,0:T(8,128)(2,1)S(1)}, u32[]{:S(2)}, u32[]{:S(2)}) %collective-permute-start.10) | collective-permute-done | bytes 114720 | tf_op jit(solution)/shard_map/ppermute | solution.py:32
  37.2 0.1 collective-permute-start.11
  37.3 0.6 %collective-permute-done.5 = bf16[128,256]{1,0:T(8,128)(2,1)S(1)} collective-permute-done((bf16[128,256]{1,0:T(8,128)(2,1)S(1)}, bf16[128,256]{1,0:T(8,128)(2,1)S(1)}, u32[]{:S(2)}, u32[]{:S(2)}) %collective-permute-start.5) | collective-permute-done | bytes 65568 | tf_op jit(solution)/shard_map/ppermute | solution.py:32
  37.9 0.3 multiply_convert_fusion
  38.2 0.7 %copy.17 = bf16[128,256]{1,0:T(8,128)(2,1)} copy(bf16[128,256]{0,1:T(8,128)(2,1)S(1)} %multiply_convert_fusion) | data formatting | bytes 131072
  38.9 0.0 collective-permute-done.11.other
  38.9 1.3 %shard_map.151 = (bf16[128,256]{1,0:T(8,128)(2,1)}, f32[256,256]{1,0:T(8,128)}, f32[256,256]{1,0:T(8,128)}, f32[1,256]{1,0:T(1,128)}) custom-call(bf16[128,896]{1,0:T(8,128)(2,1)S(1)} %pad_maximum_fusion.mine, bf16[128,896]{1,0:T(8,128)(2,1)S(1)} %collective-permute-done.11.other, bf16[256,128]{1,0:T(8,128)(2,1)S(1)} %add_add_fusion.own_columns, ...), custom_call_target="tpu_custom_call" | custom-call | tf_op jit(solution)/shard_map/pallas_call | solution.py:45
  (8 shorter events, 0.1 us)
Async XLA Ops:
  0.6 12.9 %collective-permute-start = (bf16[128,256]{1,0:T(8,128)(2,1)}, bf16[128,256]{1,0:T(8,128)(2,1)S(1)}, u32[]{:S(2)}, u32[]{:S(2)}) collective-permute-start(bf16[128,256]{1,0:T(8,128)(2,1)} %refs_5_.1), channel_id=1, source_target_pairs={{0,12},{4,8},{8,4},{12,0},{1,13},{5,9},{9,5},{13,1},{2,14},{6,10},... | collective-permute-start | bytes 196616 | tf_op jit(solution)/shard_map/ppermute | solution.py:32
  5.7 8.5 %collective-permute-start.1 = (bf16[128,256]{1,0:T(8,128)(2,1)}, bf16[128,256]{1,0:T(8,128)(2,1)S(1)}, u32[]{:S(2)}, u32[]{:S(2)}) collective-permute-start(bf16[128,256]{1,0:T(8,128)(2,1)} %refs_5_.1), channel_id=1, source_target_pairs={{0,8},{4,12},{8,0},{12,4},{1,9},{5,13},{9,1},{13,5},{2,10},{6,14},... | collective-permute-start | bytes 196616 | tf_op jit(solution)/shard_map/ppermute | solution.py:32
  5.7 8.5 %collective-permute-start.2 = (bf16[128,256]{1,0:T(8,128)(2,1)}, bf16[128,256]{1,0:T(8,128)(2,1)S(1)}, u32[]{:S(2)}, u32[]{:S(2)}) collective-permute-start(bf16[128,256]{1,0:T(8,128)(2,1)} %refs_5_.1), channel_id=1, source_target_pairs={{0,4},{4,0},{8,12},{12,8},{1,5},{5,1},{9,13},{13,9},{2,6},{6,2},{1... | collective-permute-start | bytes 196616 | tf_op jit(solution)/shard_map/ppermute | solution.py:32
  7.8 6.5 %copy-start = (bf16[128,256]{1,0:T(8,128)(2,1)S(1)}, bf16[128,256]{1,0:T(8,128)(2,1)}, u32[]{:S(2)}) copy-start(bf16[128,256]{1,0:T(8,128)(2,1)} %refs_5_.1) | copy-start | bytes 196612
  9.7 3.8 %copy-start.1 = (s32[128]{0:T(128)S(1)}, s32[128]{0:T(128)}, u32[]{:S(2)}) copy-start(s32[128]{0:T(128)} %param.19) | copy-start | bytes 1540
  9.7 15.9 %collective-permute-start.12 = (bf16[256,128]{1,0:T(8,128)(2,1)S(1)}, bf16[256,128]{1,0:T(8,128)(2,1)S(1)}, u32[]{:S(2)}, u32[]{:S(2)}) collective-permute-start(bf16[256,128]{1,0:T(8,128)(2,1)S(1)} %get-tuple-element.40.refs_9_), channel_id=1, source_target_pairs={{0,12},{4,8},{8,4},{12,0},{1,13},{5,9},{9,5},{13,1},{2,14},{6,10},... | collective-permute-start | bytes 196616 | tf_op jit(solution)/shard_map/ppermute | solution.py:32
  13.5 12.1 %collective-permute-start.13 = (bf16[256,128]{1,0:T(8,128)(2,1)S(1)}, bf16[256,128]{1,0:T(8,128)(2,1)S(1)}, u32[]{:S(2)}, u32[]{:S(2)}) collective-permute-start(bf16[256,128]{1,0:T(8,128)(2,1)S(1)} %get-tuple-element.39.refs_8_), channel_id=1, source_target_pairs={{0,8},{4,12},{8,0},{12,4},{1,9},{5,13},{9,1},{13,5},{2,10},{6,14},... | collective-permute-start | bytes 196616 | tf_op jit(solution)/shard_map/ppermute | solution.py:32
  13.6 12.7 %collective-permute-start.14 = (bf16[256,128]{1,0:T(8,128)(2,1)S(1)}, bf16[256,128]{1,0:T(8,128)(2,1)S(1)}, u32[]{:S(2)}, u32[]{:S(2)}) collective-permute-start(bf16[256,128]{1,0:T(8,128)(2,1)S(1)} %get-tuple-element.38.refs_7_), channel_id=1, source_target_pairs={{0,4},{4,0},{8,12},{12,8},{1,5},{5,1},{9,13},{13,9},{2,6},{6,2},{1... | collective-permute-start | bytes 196616 | tf_op jit(solution)/shard_map/ppermute | solution.py:32
  14.7 1.6 %collective-permute-start.3 = (bf16[128,896]{1,0:T(8,128)(2,1)S(1)}, bf16[128,896]{1,0:T(8,128)(2,1)S(1)}, u32[]{:S(2)}, u32[]{:S(2)}) collective-permute-start(bf16[128,896]{1,0:T(8,128)(2,1)S(1)} %get-tuple-element.43), channel_id=1, source_target_pairs={{0,1},{1,0},{2,3},{3,2},{4,5},{5,4},{6,7},{7,6},{8,9},{9,8},{10,11... | collective-permute-start | bytes 688136 | tf_op jit(solution)/shard_map/ppermute | solution.py:32
  16.3 5.3 %collective-permute-start.6 = (bf16[64,896]{1,0:T(8,128)(2,1)S(1)}, bf16[64,896]{1,0:T(8,128)(2,1)S(1)}, u32[]{:S(2)}, u32[]{:S(2)}) collective-permute-start(bf16[64,896]{1,0:T(8,128)(2,1)S(1)} %get-tuple-element.53), channel_id=1, source_target_pairs={{0,2},{1,3},{2,0},{3,1},{4,6},{5,7},{6,4},{7,5},{8,10},{9,11},{10,... | collective-permute-start | bytes 344072 | tf_op jit(solution)/shard_map/ppermute | solution.py:32
  18.8 14.7 %collective-permute-start.4 = (bf16[256,256]{1,0:T(8,128)(2,1)S(1)}, bf16[256,256]{1,0:T(8,128)(2,1)S(1)}, u32[]{:S(2)}, u32[]{:S(2)}) collective-permute-start(bf16[256,256]{1,0:T(8,128)(2,1)S(1)} %slice.63), channel_id=1, source_target_pairs={{0,1},{1,0},{2,3},{3,2},{4,5},{5,4},{6,7},{7,6},{8,9},{9,8},{10,11... | collective-permute-start | bytes 393224 | tf_op jit(solution)/shard_map/ppermute | solution.py:32
  21.8 6.7 %collective-permute-start.7 = (bf16[64,640]{1,0:T(8,128)(2,1)S(1)}, bf16[64,640]{1,0:T(8,128)(2,1)S(1)}, u32[]{:S(2)}, u32[]{:S(2)}) collective-permute-start(bf16[64,640]{1,0:T(8,128)(2,1)S(1)} %get-tuple-element.54.refs_3_), channel_id=1, source_target_pairs={{0,12},{4,8},{8,4},{12,0},{1,13},{5,9},{9,5},{13,1},{2,14},{6,10},... | collective-permute-start | bytes 245768 | tf_op jit(solution)/shard_map/ppermute | solution.py:32
  25.6 6.3 %collective-permute-start.8 = (bf16[64,640]{1,0:T(8,128)(2,1)S(1)}, bf16[64,640]{1,0:T(8,128)(2,1)S(1)}, u32[]{:S(2)}, u32[]{:S(2)}) collective-permute-start(bf16[64,640]{1,0:T(8,128)(2,1)S(1)} %get-tuple-element.54.refs_3_), channel_id=1, source_target_pairs={{0,8},{4,12},{8,0},{12,4},{1,9},{5,13},{9,1},{13,5},{2,10},{6,14},... | collective-permute-start | bytes 245768 | tf_op jit(solution)/shard_map/ppermute | solution.py:32
  25.6 6.3 %collective-permute-start.9 = (bf16[64,640]{1,0:T(8,128)(2,1)S(1)}, bf16[64,640]{1,0:T(8,128)(2,1)S(1)}, u32[]{:S(2)}, u32[]{:S(2)}) collective-permute-start(bf16[64,640]{1,0:T(8,128)(2,1)S(1)} %get-tuple-element.54.refs_3_), channel_id=1, source_target_pairs={{0,4},{4,0},{8,12},{12,8},{1,5},{5,1},{9,13},{13,9},{2,6},{6,2},{1... | collective-permute-start | bytes 245768 | tf_op jit(solution)/shard_map/ppermute | solution.py:32
  31.9 5.2 %collective-permute-start.10 = (bf16[64,896]{1,0:T(8,128)(2,1)S(1)}, bf16[64,896]{1,0:T(8,128)(2,1)S(1)}, u32[]{:S(2)}, u32[]{:S(2)}) collective-permute-start(bf16[64,896]{1,0:T(8,128)(2,1)S(1)} %shard_map.150), channel_id=1, source_target_pairs={{0,2},{1,3},{2,0},{3,1},{4,6},{5,7},{6,4},{7,5},{8,10},{9,11},{10,... | collective-permute-start | bytes 344072 | tf_op jit(solution)/shard_map/ppermute | solution.py:32
  33.5 4.3 %collective-permute-start.5 = (bf16[128,256]{1,0:T(8,128)(2,1)S(1)}, bf16[128,256]{1,0:T(8,128)(2,1)S(1)}, u32[]{:S(2)}, u32[]{:S(2)}) collective-permute-start(bf16[128,256]{1,0:T(8,128)(2,1)S(1)} %slice.64), channel_id=1, source_target_pairs={{0,2},{1,3},{2,0},{3,1},{4,6},{5,7},{6,4},{7,5},{8,10},{9,11},{10,... | collective-permute-start | bytes 196616 | tf_op jit(solution)/shard_map/ppermute | solution.py:32
  37.2 1.7 %collective-permute-start.11 = (bf16[128,896]{1,0:T(8,128)(2,1)S(1)}, bf16[128,896]{1,0:T(8,128)(2,1)S(1)}, u32[]{:S(2)}, u32[]{:S(2)}) collective-permute-start(bf16[128,896]{1,0:T(8,128)(2,1)S(1)} %pad_maximum_fusion.mine), channel_id=1, source_target_pairs={{0,1},{1,0},{2,3},{3,2},{4,5},{5,4},{6,7},{7,6},{8,9},{9,8},{10,11... | collective-permute-start | bytes 688136 | tf_op jit(solution)/shard_map/ppermute | solution.py:32

commit v4 on v3

--- a/solution.py
+++ b/solution.py
@@ -32,11 +32,18 @@
     return lax.ppermute(block, axis, [(i, i ^ step) for i in range(lax.axis_size(axis))])
 
 
-def flip(pair, axis, bit):
-    return jnp.where(bit == 1, jnp.flip(pair, axis), pair)
-
-
-def call(kernel, outputs, *inputs, spaces=(), scratch=()):
+def swap_quarters(line):
+    first, second, third, last = jnp.split(line, 4, axis=1)
+    return jnp.concatenate([first, third, second, last], axis=1)
+
+
+def flip(line, parts, bit):
+    cut = jnp.split(line, parts, axis=1)
+    turned = [cut[i ^ 1] for i in range(parts)]
+    return jnp.where(bit == 1, jnp.concatenate(turned, axis=1), line)
+
+
+def call(kernel, outputs, *inputs, spaces=(), scratch=(), out_space=pltpu.VMEM, cost=0):
     inputs = [
         pltpu.with_memory_space_constraint(x, y) if y == pltpu.HBM else x
         for x, y in itertools.zip_longest(inputs, spaces)
@@ -46,14 +53,18 @@
         kernel,
         out_shape=[jax.ShapeDtypeStruct(shape, dtype) for shape, dtype in outputs],
         in_specs=[pl.BlockSpec(memory_space=space) for space in spaces],
-        out_specs=[pl.BlockSpec(memory_space=pltpu.VMEM) for _ in outputs],
+        out_specs=[pl.BlockSpec(memory_space=out_space) for _ in outputs],
         scratch_shapes=scratch,
+        cost_estimate=pl.CostEstimate(flops=int(cost * 1e9), bytes_accessed=0, transcendentals=0) if cost else None,
         compiler_params=pltpu.CompilerParams(vmem_limit_bytes=32 * 2**20),
     )(*inputs)
 
 
-def spread(block, axis):
-    return [trade(block, axis, step) for step in range(lax.axis_size(axis) - 1, 0, -1)]
+CFG = {'forder': [2, 3, 1], 'split': True, 'halves': [0, 2, 1, 3], 'a1': 'none', 'a2': 'none', 'dd': 'sent', 'p3d': True, 'p3': [3, 1, 2], 'p3split': False, 'fp': 'found1', 'dx': 'found1', 'hid': 'none', 'cd': 3}
+
+
+def spread(block, axis, steps):
+    return {step: trade(block, axis, step) for step in steps}
 
 
 def swap_bits(index):
@@ -62,8 +73,7 @@
 
 def select(rows, cols, ids_in, src_in, dst_in, count_in, tiles_in, cotangent_in, degree_in, *refs):
     weights_in, refs = refs[:3], refs[3:]
-    adjacency, column_picks, own_picks, known = refs[:4]
-    picked, refs = refs[4 : 4 + rows], refs[4 + rows :]
+    adjacency, column_picks, own_picks, known, near, far, inverse, *refs = refs
     weights, (picks, src, dst, count, tiles, cotangent, degree, ids, sems) = refs[:3], refs[3:]
     pairs = [(src_in, src), (dst_in, dst), (count_in, count), (tiles_in, tiles)]
     pairs += [(cotangent_in, cotangent), (degree_in, degree), (ids_in, ids)]
@@ -72,8 +82,7 @@
     for copy in copies:
         copy.start()
     row, col = lax.axis_index("row"), lax.axis_index("col")
-    share, nodes, width = ids.shape[1], cotangent.shape[0], cotangent.shape[1]
-    slots = share * cols
+    slots, (nodes, width) = ids.shape[1], cotangent.shape
     adjacency[...] = jnp.zeros(adjacency.shape, adjacency.dtype)
     for copy in copies[:7]:
         copy.wait()
@@ -84,46 +93,66 @@
             down = pl.multiple_of(swap_bits(dst[0, 0, k] ^ col) * nodes, nodes)
             adjacency[src[0, 0, k] ^ row, pl.ds(down, nodes), :] = tiles[0, 0, k]
 
-    lanes = lax.broadcasted_iota(jnp.int32, (share, nodes), 1)
-    across = lax.broadcasted_iota(jnp.int32, (nodes, share), 0)
-    for p in range(cols):
-        here = pl.ds(p * share, share)
-        line = jnp.broadcast_to(ids[pl.ds(col ^ swap_bits(p), 1), :], (nodes, share))
-        stack = line.T
-        for k in range(cols):
-            base = (row * cols + (col ^ swap_bits(k))) * nodes
-            picks[here, k * nodes : (k + 1) * nodes] = (stack == lanes + base).astype(BF16)
-        for s in range(rows):
-            base = ((row ^ s) * cols + col) * nodes
-            column_picks[here, s * nodes : (s + 1) * nodes] = (stack == lanes + base).astype(BF16)
-        base = (row * cols + col) * nodes
-        own_picks[:, here] = (line == across + base).astype(BF16)
+    line = flip(flip(swap_quarters(ids[...]), 2, col % 2), 4, col // 2)
+    line = jnp.broadcast_to(line, (nodes, slots))
+    stack = line.T
+    lanes = lax.broadcasted_iota(jnp.int32, (slots, nodes), 1)
+    for k in range(cols):
+        base = (row * cols + (col ^ swap_bits(k))) * nodes
+        picks[:, k * nodes : (k + 1) * nodes] = (stack == lanes + base).astype(BF16)
     for s in range(rows):
-        picked[s][...] = dot(picks[...], adjacency[s]).astype(BF16)
+        base = ((row ^ s) * cols + col) * nodes
+        column_picks[:, s * nodes : (s + 1) * nodes] = (stack == lanes + base).astype(BF16)
+    base = (row * cols + col) * nodes
+    across = lax.broadcasted_iota(jnp.int32, (nodes, slots), 0)
+    own_picks[...] = (line == across + base).astype(BF16)
+    for s in range(rows):
+        block = dot(picks[...], adjacency[s]).astype(BF16)
+        index = list(CFG["halves"]).index(s)
+        (far if index // 2 else near)[index % 2 * slots : (index % 2 + 1) * slots, :] = block
     own = picks[:, :nodes]
     known[:, :width] = dot(own, cotangent[...]).astype(BF16)
     for copy in copies[7:]:
         copy.wait()
     counts = degree[...].astype(F32)
+    inverse[...] = 1.0 / jnp.broadcast_to(counts, (nodes, nodes)).T
     counts = jnp.sum(own.astype(F32) * counts, axis=1, keepdims=True)
     known[:, width:] = jnp.broadcast_to(counts, (slots, 128)).astype(BF16)
 
 
-def combine(rows, *refs):
-    column_picks, known, *rest = refs
-    features, picked = rest[:rows][::-1], rest[rows : 2 * rows]
-    sent, part, fixed = rest[2 * rows :]
+def block_of(step, near, far, slots):
+    index = list(CFG["halves"]).index(step)
+    return (far if index // 2 else near)[index % 2 * slots : (index % 2 + 1) * slots, :]
+
+
+def dense_part(steps, adjacency, *refs):
+    *features, kept, sent = refs
+    total = sum(dot(adjacency[step], block[...]) for step, block in zip(steps, features))
+    half = kept.shape[0]
+    kept[...] = total[:half]
+    sent[...] = total[half:].astype(BF16)
+
+
+def begin(step, column_picks, features, near, far, total, chosen):
+    slots, nodes = column_picks.shape[0], features.shape[0]
+    total[...] = dot(block_of(step, near, far, slots), features[...])
+    chosen[...] = dot(column_picks[:, step * nodes : (step + 1) * nodes], features[...])
+
+
+def combine(steps, column_picks, known, *refs):
+    features, (near, far, *first, sent, part, fixed) = refs[: len(steps)], refs[len(steps) :]
     nodes, width = features[0].shape
     half = part.shape[0]
-    sums = sum(dot(picked[s][...], features[s][...]) for s in range(rows))
-    chosen = sum(
-        dot(column_picks[:, s * nodes : (s + 1) * nodes], features[s][...]) for s in range(rows)
-    ).astype(BF16)
+    sums, picked = [x[...] for x in first] or [0.0, 0.0]
+    for step, block in zip(steps, features):
+        sums += dot(block_of(step, near, far, 2 * half), block[...])
+        picked += dot(column_picks[:, step * nodes : (step + 1) * nodes], block[...])
+    picked = picked.astype(BF16)
     part[...] = sums[:half]
-    fixed[:, :width] = chosen[:half]
+    fixed[:, :width] = picked[:half]
     fixed[:, width:] = known[:half, :]
     sent[:, :width] = sums[half:].astype(BF16)
-    sent[:, width : 2 * width] = chosen[half:]
+    sent[:, width : 2 * width] = picked[half:]
     sent[:, 2 * width :] = known[half:, :]
 
 
@@ -148,36 +177,65 @@
     inverse = jnp.where(degree > 0, 1.0 / jnp.maximum(degree, 1.0), 0.0)
     aggregate = (total * inverse).astype(BF16)
     before = dot(rest[:, :width], w_self[...]) + dot(aggregate, w_neigh[...]) + layer_bias[...]
-    found[:, :width] = (cotangent * gelu_slope(before)).astype(BF16)
-    found[:, width : 2 * width] = aggregate
-    found[:, 2 * width :] = degrees
+    slope = (cotangent * gelu_slope(before)).astype(BF16)
+    share, bands = part.shape[0], width // 128
+    for b in range(bands):
+        found[b * share : (b + 1) * share, :] = slope[:, b * 128 : (b + 1) * 128]
+        down = (bands + b) * share
+        found[down : down + share, :] = aggregate[:, b * 128 : (b + 1) * 128]
+    line = degrees.astype(F32).T[:16, :]
+    line = jnp.concatenate([line, jnp.zeros((16, 128 - share), F32)], axis=1)
+    found[2 * bands * share :, :] = line.astype(BF16)
 
 
 def merge(*refs):
-    *parts, features, everything = refs
-    width = features.shape[1]
-    everything[:, :-width] = sum(part[...] for part in parts)
-    everything[:, -width:] = features[...]
-
-
-def finish(scale, mine, other, own_columns, own_picks, w_self, w_neigh, *outs):
-    grad_features, grad_self, grad_neigh, grad_bias = outs
-    width = w_self.shape[0]
-    half = mine.shape[0]
+    refs[-1][...] = sum(part[...] for part in refs[:-1])
+
+
+def activate(features, total, got, inverse, w_self, w_neigh, layer_bias, hidden):
+    total = total[...] + got[...].astype(F32)
+    aggregate = (total * inverse[:, :1]).astype(BF16)
+    before = dot(features[...], w_self[...]) + dot(aggregate, w_neigh[...]) + layer_bias[...]
+    hidden[...] = gelu_value(before).astype(BF16)
+
+
+def finish(scale, *refs):
+    found, features, refs = refs[:2], refs[2:4], refs[4:]
+    own_columns, own_picks, w_self, w_neigh, *refs = refs
+    outs, (slope, aggregate, *results, sems) = refs[:4], refs[4:]
+    grad_features, grad_self, grad_neigh, grad_bias = results
+    slots, width = slope.shape
+    half, bands = slots // 2, width // 128
+    share = half // 2
+    size = found[0].shape[0] // 2
     front, back = ((0,), (0,)), ((1,), (1,))
-    slope = [mine[:, :width], other[:, :width]]
-    both = (mine, other)
-    pairs = list(zip(both, slope))
-    grad_self[...] = sum(dot(e[:, -width:], g, front) for e, g in pairs) * scale
-    grad_neigh[...] = sum(dot(e[:, width : 2 * width], g, front) for e, g in pairs) * scale
-    grad_bias[...] = sum(jnp.sum(g.astype(F32), axis=0, keepdims=True) for g in slope) * scale
-    own_slope = dot(own_picks[:, :half], slope[0]) + dot(own_picks[:, half:], slope[1])
-    total = dot(own_slope.astype(BF16), w_self[...], back)
-    for j, (e, g) in enumerate(pairs):
-        degree = e[:, 2 * width : 2 * width + 1].astype(F32)
-        message = (dot(g, w_neigh[...], back) / degree).astype(BF16)
-        total += dot(own_columns[j * half : (j + 1) * half, :], message, front)
+    degrees = []
+    for q in range(4):
+        part, base, here = found[q // 2], q % 2 * size, slice(q * share, (q + 1) * share)
+        for b in range(bands):
+            lanes = slice(b * 128, (b + 1) * 128)
+            slope[here, lanes] = part[base + b * share : base + (b + 1) * share, :]
+            down = base + (bands + b) * share
+            aggregate[here, lanes] = part[down : down + share, :]
+        degrees.append(part[base + size - 16 : base + size, :].astype(F32)[:1, :share])
+    copies = [pltpu.make_async_copy(a, b, sems.at[i]) for i, (a, b) in enumerate(zip(results, outs))]
+    grad_self[...] = scale * (
+        dot(features[0][...], slope[:half, :], front)
+        + dot(features[1][...], slope[half:, :], front)
+    )
+    copies[1].start()
+    grad_neigh[...] = dot(aggregate[...], slope[...], front) * scale
+    copies[2].start()
+    grad_bias[...] = jnp.sum(slope[...].astype(F32), axis=0, keepdims=True) * scale
+    copies[3].start()
+    degree = jnp.broadcast_to(jnp.concatenate(degrees, axis=1), (128, slots)).T[:, :1]
+    message = (dot(slope[...], w_neigh[...], back) / degree).astype(BF16)
+    own_slope = dot(own_picks[...], slope[...]).astype(BF16)
+    total = dot(own_slope, w_self[...], back) + dot(own_columns[...], message, front)
     grad_features[...] = total.astype(BF16)
+    copies[0].start()
+    for copy in copies:
+        copy.wait()
 
 
 def compact_device(
@@ -200,10 +258,13 @@
     share = slots // cols
     half = slots // 2
 
-    feature_parts = spread(features, "row") + [features]
+    tie = lax.optimization_barrier
+    feature_parts = spread(features, "row", CFG["forder"])
+    steps = tuple(feature_parts)
+    feature_parts[0] = features
 
     bias = layer_bias.reshape(1, width)
-    adjacency, column_picks, own_picks, known, *picked = call(
+    adjacency, column_picks, own_picks, known, near, far, inverse, w_self, w_neigh, bias = call(
         functools.partial(select, rows, cols),
         [
             ((rows, cols * nodes, nodes), BF16),
@@ -211,10 +272,11 @@
             ((nodes, slots), BF16),
             ((slots, width + 128), BF16),
         ]
-        + [((slots, nodes), BF16)] * rows
+        + [((rows // 2 * slots, nodes), BF16)] * 2
+        + [((nodes, nodes), F32)]
         + [((width, width), BF16)] * 2
         + [((1, width), F32)],
-        target_ids.reshape(cols, share),
+        target_ids.reshape(1, slots),
         tile_src,
         tile_dst,
         tile_count,
@@ -224,22 +286,33 @@
         w_self,
         w_neigh,
         bias,
-        spaces=[pl.ANY] + [pltpu.HBM] * 2 + [pl.ANY] + [pltpu.HBM] * 6,
+        spaces=[pltpu.HBM] * 3 + [pl.ANY] + [pltpu.HBM] * 6,
         scratch=[pltpu.VMEM((slots, cols * nodes), BF16)]
         + [pltpu.SMEM(x.shape, x.dtype) for x in (tile_src, tile_dst, tile_count)]
         + [pltpu.VMEM(x.shape, x.dtype) for x in (tile_vals, cotangent)]
-        + [pltpu.VMEM((1, nodes), jnp.int32), pltpu.VMEM((cols, share), jnp.int32)]
+        + [pltpu.VMEM((1, nodes), jnp.int32), pltpu.VMEM((1, slots), jnp.int32)]
         + [pltpu.SemaphoreType.DMA((10,))],
     )
-    *picked, w_self, w_neigh, bias = picked
-    own_columns = sum(trade(picked[s], "row", s) for s in range(rows - 1, 0, -1)) + picked[0]
+    first = ()
+    if CFG["split"]:
+        first = call(
+            functools.partial(begin, steps[0]),
+            [((slots, width), F32)] * 2,
+            column_picks,
+            feature_parts[steps[0]],
+            near,
+            far,
+        )
+    later = steps[len(first) // 2 :] + (0,)
     sent, part, fixed = call(
-        functools.partial(combine, rows),
-        [((half, 2 * width + width + 128), BF16), ((half, width), F32), ((half, 2 * width + 128), BF16)],
+        functools.partial(combine, later),
+        [((half, 3 * width + 128), BF16), ((half, width), F32), ((half, 2 * width + 128), BF16)],
         column_picks,
         known,
-        *feature_parts,
-        *picked,
+        *[feature_parts[step] for step in later],
+        near,
+        far,
+        *first,
     )
     got = trade(sent, "col", 1)
     sent, part, fixed = call(
@@ -249,11 +322,14 @@
         fixed,
         got,
     )
-    sent, feature_parts = lax.optimization_barrier((sent, feature_parts))
+    if CFG["a1"] == "sent":
+        sent, far = tie((sent, far))
+    if CFG["dd"] == "sent":
+        sent, feature_parts = tie((sent, feature_parts))
     got = trade(sent, "col", 2)
     found, feature_slots = call(
         slopes,
-        [((share, 2 * width + 128), BF16), ((share, width), BF16)],
+        [((2 * (width // 128) * share + 16, 128), BF16), ((share, width), BF16)],
         part,
         fixed,
         got,
@@ -261,30 +337,85 @@
         w_neigh,
         bias,
     )
-    (everything,) = call(
-        merge, [((share, 3 * width + 128), BF16)], *spread(found, "row"), found, feature_slots
-    )
-
-    dense = sum(dot(adjacency[s], feature_parts[-1 - s]) for s in range(rows))
-    middle = 2 * nodes
-    dense = dense[:middle] + trade(dense[middle:].astype(BF16), "col", 1).astype(F32)
-    own_sum = dense[:nodes] + trade(dense[nodes:].astype(BF16), "col", 2).astype(F32)
-
-    everything = jnp.concatenate([everything, trade(everything, "col", 2)], axis=0)
-    other = trade(everything, "col", 1)
-    own_aggregate = (own_sum * (1.0 / degree.astype(F32))[:, None]).astype(BF16)
-    own_before = dot(features, w_self) + dot(own_aggregate, w_neigh) + bias
-    hidden = gelu_value(own_before).astype(BF16)
-
+    if CFG["a1"] == "found":
+        found, far = tie((found, far))
+    if CFG["dd"] == "found":
+        found, feature_parts = tie((found, feature_parts))
+    near_step, far_step = CFG["halves"][1], CFG["halves"][2]
+    columns = near + trade(far, "row", far_step)
+    if CFG["a2"] == "found":
+        found, columns = tie((found, columns))
+
+    def prepare_dense(feature_parts):
+        kept, dense = call(
+            functools.partial(dense_part, steps + (0,)),
+            [((2 * nodes, width), F32), ((2 * nodes, width), BF16)],
+            adjacency,
+            *[feature_parts[step] for step in steps + (0,)],
+            cost=CFG["cd"],
+        )
+        return kept + trade(dense, "col", 1).astype(F32)
+
+    dense = prepare_dense(feature_parts)
+    parts = spread(found, "row", CFG["p3"]) if CFG["p3d"] else None
+    if CFG["p3d"]:
+        if CFG["p3split"]:
+            (found,) = call(merge, [(found.shape, BF16)], parts.pop(CFG["p3"][0]), found)
+    else:
+        (found,) = call(merge, [(found.shape, BF16)], trade(found, "row", CFG["p3"][0]), found)
+    if CFG["a2"] == "found1":
+        found, columns = tie((found, columns))
+    if CFG["fp"] == "found1":
+        found, feature_slots = tie((found, feature_slots))
+    if CFG["dx"] == "found1":
+        found, dense = tie((found, dense))
+    if CFG["p3d"]:
+        (found,) = call(merge, [(found.shape, BF16)], *parts.values(), found)
+    else:
+        (found,) = call(merge, [(found.shape, BF16)], trade(found, "row", CFG["p3"][1]), found)
+    if CFG["dx"] == "merged":
+        found, dense = tie((found, dense))
+    own_columns = columns[:slots] + trade(columns[slots:], "row", near_step)
+    dense_got = trade(dense[nodes:].astype(BF16), "col", 2)
+    if CFG["fp"] != "none":
+        feature_mine = jnp.concatenate([feature_slots, trade(feature_slots, "col", 2)], axis=0)
+        feature_other = trade(feature_mine, "col", 1)
+        everything = found
+    else:
+        everything = jnp.concatenate([found, feature_slots], axis=1)
+    found_mine = jnp.concatenate([everything, trade(everything, "col", 2)], axis=0)
+    if CFG["hid"] == "mine":
+        found_mine, dense_got = tie((found_mine, dense_got))
+    found_other = trade(found_mine, "col", 1)
+    if CFG["fp"] == "none":
+        feature_mine, feature_other = found_mine[:, -width:], found_other[:, -width:]
+    (hidden,) = call(
+        activate,
+        [((nodes, width), BF16)],
+        features,
+        dense[:nodes],
+        dense_got,
+        inverse,
+        w_self,
+        w_neigh,
+        bias,
+    )
+    results = [((nodes, width), BF16), ((width, width), F32), ((width, width), F32), ((1, width), F32)]
     grad_features, grad_self, grad_neigh, grad_bias = call(
         functools.partial(finish, 1.0 / math.sqrt(nodes * rows * cols)),
-        [((nodes, width), BF16), ((width, width), F32), ((width, width), F32), ((1, width), F32)],
-        everything,
-        other,
+        results,
+        found_mine,
+        found_other,
+        feature_mine,
+        feature_other,
         own_columns,
         own_picks,
         w_self,
         w_neigh,
+        scratch=[pltpu.VMEM((slots, width), BF16)] * 2
+        + [pltpu.VMEM(*result) for result in results]
+        + [pltpu.SemaphoreType.DMA((4,))],
+        out_space=pl.ANY,
     )
     return (hidden, grad_features, grad_self, grad_neigh, grad_bias.reshape(width))
 

time: 40.3 us -> 36.4 us (0.903)
  waiting for transfers between devices: 13.2 us -> 8.01 us
  starting transfers between devices: 18.7 us -> 21.3 us
  local copies, waits for them, and re-layouts: 1.54 us -> 0.04 us
  Pallas kernels: 3.89 us -> 5.35 us
  matrix products: 1.34 us -> 0 us
    ppermute x15 -> x16, waiting for transfers between devices: 13.2 us -> 8.01 us  [trade(): lax.ppermute(block, axis, [(i, i ^ step) for i in range(lax.axis_size(axi...]
    ppermute x15 -> x16, starting transfers between devices: 18.7 us -> 21.3 us  [trade(): lax.ppermute(block, axis, [(i, i ^ step) for i in range(lax.axis_size(axi...]
    pallas_call x6 -> x9, Pallas kernels: 3.89 us -> 5.35 us  [call(): pl.pallas_call(kernel, out_shape=[jax.ShapeDtypeStruct(shape, dtype) for...]
    dot_general x6 -> x0, matrix products: 1.34 us -> none  [dot(): lax.dot_general(left, right, (dims, ((), ())), preferred_element_type=F32)]
    reshape x1 -> x0, local copies, waits for them, and re-layouts: 0.76 us -> none  [compact_device(): target_ids.reshape(cols, share)]
    unnamed x5 -> x3, local copies, waits for them, and re-layouts: 0.76 us -> 0.01 us
  transfers between devices with their start and end apart: 15 -> 16, of which waited for: 6 -> 7; matrix products, arithmetic and copies ran while one was open for 7% -> 0% of each run, Pallas kernels for 7% -> 11%
where the time goes in v4:
time: 36.4 us; the launch traced here: 36.2 us
  starting transfers between devices  21.3 us (59%)
  waiting for transfers between devices  8.01 us (22%)
  Pallas kernels  5.35 us (15%)
  between operations  1.44 us (4%)
    ppermute x16, starting transfers between devices, trade(): lax.ppermute(block, axis, [(i, i ^ step) for i in range(lax.axis_size(axi...  21.3 us
    ppermute x16, waiting for transfers between devices, trade(): lax.ppermute(block, axis, [(i, i ^ step) for i in range(lax.axis_size(axi...  8.01 us
    pallas_call x9, Pallas kernels, call(): pl.pallas_call(kernel, out_shape=[jax.ShapeDtypeStruct(shape, dtype) for...  5.35 us
  transfers between devices with their start and end apart: 16, of which 7 were waited for; matrix products, arithmetic and copies ran while one was open for 0% of the time, Pallas kernels for 11%

profile of v4, /device:TPU:0, one launch (start us, length us, event | category | flops | bytes accessed | tf_op | source)
XLA Modules:
  0.0 36.2 jit_solution(8914300264778698632)
XLA Ops:
  0.6 4.1 %collective-permute-start.2 = (bf16[128,256]{1,0:T(8,128)(2,1)}, bf16[128,256]{1,0:T(8,128)(2,1)S(1)}, u32[]{:S(2)}, u32[]{:S(2)}) collective-permute-start(bf16[128,256]{1,0:T(8,128)(2,1)} %features.1), channel_id=1, source_target_pairs={{0,8},{4,12},{8,0},{12,4},{1,9},{5,13},{9,1},{13,5},{2,10},{6,14},... | collective-permute-start | bytes 196616 | tf_op jit(solution)/shard_map/ppermute | solution.py:32
  4.7 1.3 %collective-permute-start = (bf16[128,256]{1,0:T(8,128)(2,1)}, bf16[128,256]{1,0:T(8,128)(2,1)S(1)}, u32[]{:S(2)}, u32[]{:S(2)}) collective-permute-start(bf16[128,256]{1,0:T(8,128)(2,1)} %features.1), channel_id=1, source_target_pairs={{0,12},{4,8},{8,4},{12,0},{1,13},{5,9},{9,5},{13,1},{2,14},{6,10},... | collective-permute-start | bytes 196616 | tf_op jit(solution)/shard_map/ppermute | solution.py:32
  6.1 0.2 collective-permute-start.1
  7.0 2.0 %shard_map.146 = (bf16[4,512,128]{2,1,0:T(8,128)(2,1)S(1)}, bf16[256,512]{1,0:T(8,128)(2,1)S(1)}, bf16[128,256]{1,0:T(8,128)(2,1)S(1)}, bf16[256,384]{1,0:T(8,12...) custom-call(s32[1,256]{1,0:T(1,128)} %bitcast.4, ...), custom_call_target="tpu_custom_call" | custom-call | tf_op jit(solution)/shard_map/pallas_call | solution.py:52
  9.0 0.0 collective-permute-done.2.features.refs_0_
  9.0 0.0 copy-start
  9.0 0.2 shard_map.147
  9.2 1.9 %collective-permute-done.refs_0_.refs_1_ = bf16[128,256]{1,0:T(8,128)(2,1)S(1)} collective-permute-done((bf16[128,256]{1,0:T(8,128)(2,1)}, bf16[128,256]{1,0:T(8,128)(2,1)S(1)}, u32[]{:S(2)}, u32[]{:S(2)}) %collective-permute-start) | collective-permute-done | bytes 65568 | tf_op jit(solution)/shard_map/ppermute | solution.py:32
  11.2 0.1 collective-permute-done.1.refs_1_.refs_2_
  11.3 0.0 copy-done
  11.3 0.3 shard_map.148
  11.6 0.1 collective-permute-start.3
  11.7 0.9 %collective-permute-start.14 = (bf16[512,128]{1,0:T(8,128)(2,1)S(1)}, bf16[512,128]{1,0:T(8,128)(2,1)S(1)}, u32[]{:S(2)}, u32[]{:S(2)}) collective-permute-start(bf16[512,128]{1,0:T(8,128)(2,1)S(1)} %get-tuple-element.42.far.refs_4_), channel_id=1, source_target_pairs={{0,4},{4,0},{8,12},{12,8},{1,5},{5,1},{9,13},{13,9},{2,6},{6,2},{1... | collective-permute-start | bytes 393224 | tf_op jit(solution)/shard_map/ppermute | solution.py:32
  12.6 0.5 %collective-permute-done.3.got = bf16[128,896]{1,0:T(8,128)(2,1)S(1)} collective-permute-done((bf16[128,896]{1,0:T(8,128)(2,1)S(1)}, bf16[128,896]{1,0:T(8,128)(2,1)S(1)}, u32[]{:S(2)}, u32[]{:S(2)}) %collective-permute-start.3) | collective-permute-done | bytes 229408 | tf_op jit(solution)/shard_map/ppermute | solution.py:32
  13.2 1.6 %collective-permute-start.4 = (bf16[64,896]{1,0:T(8,128)(2,1)S(1)}, bf16[64,896]{1,0:T(8,128)(2,1)S(1)}, u32[]{:S(2)}, u32[]{:S(2)}) collective-permute-start(bf16[64,896]{1,0:T(8,128)(2,1)S(1)} %get-tuple-element.51), channel_id=1, source_target_pairs={{0,2},{1,3},{2,0},{3,1},{4,6},{5,7},{6,4},{7,5},{8,10},{9,11},{10,... | collective-permute-start | bytes 344072 | tf_op jit(solution)/shard_map/ppermute | solution.py:32
  14.8 0.4 %shard_map.151 = (f32[256,256]{1,0:T(8,128)S(1)}, bf16[256,256]{1,0:T(8,128)(2,1)S(1)}) custom-call(bf16[4,512,128]{2,1,0:T(8,128)(2,1)S(1)} %get-tuple-element.56.adjacency, bf16[128,256]{1,0:T(8,128)(2,1)S(1)} %collective-permute-done.2.features.refs_0_, bf16[128,256]{1,0:T(8,128)(2,1)S(1)} %collective-permute-done.refs_0_.refs_1_, ...), custom_call_target="tpu_custom_call" | custom-call | flops 3000000000 | tf_op jit(solution)/shard_map/pallas_call | solution.py:52
  15.2 0.1 collective-permute-start.5
  15.3 2.3 %collective-permute-done.14 = bf16[512,128]{1,0:T(8,128)(2,1)S(1)} collective-permute-done((bf16[512,128]{1,0:T(8,128)(2,1)S(1)}, bf16[512,128]{1,0:T(8,128)(2,1)S(1)}, u32[]{:S(2)}, u32[]{:S(2)}) %collective-permute-start.14) | collective-permute-done | bytes 131104 | tf_op jit(solution)/shard_map/ppermute | solution.py:32
  17.7 2.7 %collective-permute-start.15 = (bf16[256,128]{1,0:T(8,128)(2,1)S(1)}, bf16[256,128]{1,0:T(8,128)(2,1)S(1)}, u32[]{:S(2)}, u32[]{:S(2)}) collective-permute-start(bf16[256,128]{1,0:T(8,128)(2,1)S(1)} %slice.19), channel_id=1, source_target_pairs={{0,8},{4,12},{8,0},{12,4},{1,9},{5,13},{9,1},{13,5},{2,10},{6,14},... | collective-permute-start | bytes 196616 | tf_op jit(solution)/shard_map/ppermute | solution.py:32
  20.4 0.0 collective-permute-done.4.got
  20.4 0.2 shard_map.150
  20.7 1.5 %collective-permute-start.7 = (bf16[272,128]{1,0:T(8,128)(2,1)S(1)}, bf16[272,128]{1,0:T(8,128)(2,1)S(1)}, u32[]{:S(2)}, u32[]{:S(2)}) collective-permute-start(bf16[272,128]{1,0:T(8,128)(2,1)S(1)} %get-tuple-element.65), channel_id=1, source_target_pairs={{0,12},{4,8},{8,4},{12,0},{1,13},{5,9},{9,5},{13,1},{2,14},{6,10},... | collective-permute-start | bytes 208904 | tf_op jit(solution)/shard_map/ppermute | solution.py:32
  22.2 0.0 collective-permute-start.8
  22.2 1.5 %collective-permute-start.12 = (bf16[64,256]{1,0:T(8,128)(2,1)S(1)}, bf16[64,256]{1,0:T(8,128)(2,1)S(1)}, u32[]{:S(2)}, u32[]{:S(2)}) collective-permute-start(bf16[64,256]{1,0:T(8,128)(2,1)S(1)} %get-tuple-element.67), channel_id=1, source_target_pairs={{0,2},{1,3},{2,0},{3,1},{4,6},{5,7},{6,4},{7,5},{8,10},{9,11},{10,... | collective-permute-start | bytes 98312 | tf_op jit(solution)/shard_map/ppermute | solution.py:32
  23.7 0.0 collective-permute-done.5
  23.7 2.9 %collective-permute-start.9 = (bf16[272,128]{1,0:T(8,128)(2,1)S(1)}, bf16[272,128]{1,0:T(8,128)(2,1)S(1)}, u32[]{:S(2)}, u32[]{:S(2)}) collective-permute-start(bf16[272,128]{1,0:T(8,128)(2,1)S(1)} %get-tuple-element.65), channel_id=1, source_target_pairs={{0,8},{4,12},{8,0},{12,4},{1,9},{5,13},{9,1},{13,5},{2,10},{6,14},... | collective-permute-start | bytes 208904 | tf_op jit(solution)/shard_map/ppermute | solution.py:32
  26.6 0.4 %collective-permute-done.7.refs_0_ = bf16[272,128]{1,0:T(8,128)(2,1)S(1)} collective-permute-done((bf16[272,128]{1,0:T(8,128)(2,1)S(1)}, bf16[272,128]{1,0:T(8,128)(2,1)S(1)}, u32[]{:S(2)}, u32[]{:S(2)}) %collective-permute-start.7) | collective-permute-done | bytes 69664 | tf_op jit(solution)/shard_map/ppermute | solution.py:32
  27.0 2.1 %collective-permute-start.6 = (bf16[128,256]{1,0:T(8,128)(2,1)S(1)}, bf16[128,256]{1,0:T(8,128)(2,1)S(1)}, u32[]{:S(2)}, u32[]{:S(2)}) collective-permute-start(bf16[128,256]{1,0:T(8,128)(2,1)S(1)} %slice.22), channel_id=1, source_target_pairs={{0,2},{1,3},{2,0},{3,1},{4,6},{5,7},{6,4},{7,5},{8,10},{9,11},{10,... | collective-permute-start | bytes 196616 | tf_op jit(solution)/shard_map/ppermute | solution.py:32
  29.1 0.0 collective-permute-done.8.refs_1_
  29.1 0.0 collective-permute-done.9.refs_2_
  29.1 2.2 %collective-permute-start.10 = (bf16[272,128]{1,0:T(8,128)(2,1)S(1)}, bf16[272,128]{1,0:T(8,128)(2,1)S(1)}, u32[]{:S(2)}, u32[]{:S(2)}) collective-permute-start(bf16[272,128]{1,0:T(8,128)(2,1)S(1)} %shard_map.153), channel_id=1, source_target_pairs={{0,2},{1,3},{2,0},{3,1},{4,6},{5,7},{6,4},{7,5},{8,10},{9,11},{10,... | collective-permute-start | bytes 208904 | tf_op jit(solution)/shard_map/ppermute | solution.py:32
  31.3 0.0 collective-permute-done.12
  31.3 0.0 collective-permute-start.13
  31.3 2.3 %collective-permute-done.10 = bf16[272,128]{1,0:T(8,128)(2,1)S(1)} collective-permute-done((bf16[272,128]{1,0:T(8,128)(2,1)S(1)}, bf16[272,128]{1,0:T(8,128)(2,1)S(1)}, u32[]{:S(2)}, u32[]{:S(2)}) %collective-permute-start.10) | collective-permute-done | bytes 69664 | tf_op jit(solution)/shard_map/ppermute | solution.py:32
  33.6 0.1 collective-permute-start.11
  33.7 0.0 collective-permute-done.15
  33.8 0.0 collective-permute-done.6.got
  33.8 0.9 %shard_map.152 = bf16[128,256]{1,0:T(8,128)(2,1)} custom-call(bf16[128,256]{1,0:T(8,128)(2,1)S(1)} %copy-done, f32[128,256]{1,0:T(8,128)S(1)} %slice.13.total, bf16[128,256]{1,0:T(8,128)(2,1)S(1)} %collective-permute-done.6.got, f32[128,128]{1,0:T(8,128)S(1)} %get-tuple-element.64.inverse, bf16[256,256]{1,0:T(8,128)(2,1)S(1)} %get-tuple-element.52.w_self.refs_6_, ...), custom_call_target="tpu_custom_call" | custom-call | tf_op jit(solution)/shard_map/pallas_call | solution.py:52
  34.6 0.0 collective-permute-done.13.refs_3_
  34.6 0.4 %collective-permute-done.11.refs_1_ = bf16[544,128]{1,0:T(8,128)(2,1)S(1)} collective-permute-done((bf16[544,128]{1,0:T(8,128)(2,1)S(1)}, bf16[544,128]{1,0:T(8,128)(2,1)S(1)}, u32[]{:S(2)}, u32[]{:S(2)}) %collective-permute-start.11) | collective-permute-done | bytes 139296 | tf_op jit(solution)/shard_map/ppermute | solution.py:32
  35.1 1.2 %shard_map.154 = (bf16[128,256]{1,0:T(8,128)(2,1)}, f32[256,256]{1,0:T(8,128)}, f32[256,256]{1,0:T(8,128)}, f32[1,256]{1,0:T(1,128)}) custom-call(bf16[544,128]{1,0:T(8,128)(2,1)S(1)} %pad_maximum_fusion.refs_0_, bf16[544,128]{1,0:T(8,128)(2,1)S(1)} %collective-permute-done.11.refs_1_, bf16[128,256]{1,0:T(8,128)(2,1)S(1)} %constant_dynamic-update-slice_fusion.refs_2_, ...), custom_call_target="tpu_custom_call" | custom-call | tf_op jit(solution)/shard_map/pallas_call | solution.py:52
  (11 shorter events, 0.2 us)
Async XLA Ops:
  0.6 8.4 %collective-permute-start.2 = (bf16[128,256]{1,0:T(8,128)(2,1)}, bf16[128,256]{1,0:T(8,128)(2,1)S(1)}, u32[]{:S(2)}, u32[]{:S(2)}) collective-permute-start(bf16[128,256]{1,0:T(8,128)(2,1)} %features.1), channel_id=1, source_target_pairs={{0,8},{4,12},{8,0},{12,4},{1,9},{5,13},{9,1},{13,5},{2,10},{6,14},... | collective-permute-start | bytes 196616 | tf_op jit(solution)/shard_map/ppermute | solution.py:32
  4.7 6.4 %collective-permute-start = (bf16[128,256]{1,0:T(8,128)(2,1)}, bf16[128,256]{1,0:T(8,128)(2,1)S(1)}, u32[]{:S(2)}, u32[]{:S(2)}) collective-permute-start(bf16[128,256]{1,0:T(8,128)(2,1)} %features.1), channel_id=1, source_target_pairs={{0,12},{4,8},{8,4},{12,0},{1,13},{5,9},{9,5},{13,1},{2,14},{6,10},... | collective-permute-start | bytes 196616 | tf_op jit(solution)/shard_map/ppermute | solution.py:32
  6.1 5.2 %collective-permute-start.1 = (bf16[128,256]{1,0:T(8,128)(2,1)}, bf16[128,256]{1,0:T(8,128)(2,1)S(1)}, u32[]{:S(2)}, u32[]{:S(2)}) collective-permute-start(bf16[128,256]{1,0:T(8,128)(2,1)} %features.1), channel_id=1, source_target_pairs={{0,4},{4,0},{8,12},{12,8},{1,5},{5,1},{9,13},{13,9},{2,6},{6,2},{1... | collective-permute-start | bytes 196616 | tf_op jit(solution)/shard_map/ppermute | solution.py:32
  9.0 2.3 %copy-start = (bf16[128,256]{1,0:T(8,128)(2,1)S(1)}, bf16[128,256]{1,0:T(8,128)(2,1)}, u32[]{:S(2)}) copy-start(bf16[128,256]{1,0:T(8,128)(2,1)} %features.1) | copy-start | bytes 196612
  11.6 1.6 %collective-permute-start.3 = (bf16[128,896]{1,0:T(8,128)(2,1)S(1)}, bf16[128,896]{1,0:T(8,128)(2,1)S(1)}, u32[]{:S(2)}, u32[]{:S(2)}) collective-permute-start(bf16[128,896]{1,0:T(8,128)(2,1)S(1)} %get-tuple-element.47), channel_id=1, source_target_pairs={{0,1},{1,0},{2,3},{3,2},{4,5},{5,4},{6,7},{7,6},{8,9},{9,8},{10,11... | collective-permute-start | bytes 688136 | tf_op jit(solution)/shard_map/ppermute | solution.py:32
  11.7 5.9 %collective-permute-start.14 = (bf16[512,128]{1,0:T(8,128)(2,1)S(1)}, bf16[512,128]{1,0:T(8,128)(2,1)S(1)}, u32[]{:S(2)}, u32[]{:S(2)}) collective-permute-start(bf16[512,128]{1,0:T(8,128)(2,1)S(1)} %get-tuple-element.42.far.refs_4_), channel_id=1, source_target_pairs={{0,4},{4,0},{8,12},{12,8},{1,5},{5,1},{9,13},{13,9},{2,6},{6,2},{1... | collective-permute-start | bytes 393224 | tf_op jit(solution)/shard_map/ppermute | solution.py:32
  13.2 7.2 %collective-permute-start.4 = (bf16[64,896]{1,0:T(8,128)(2,1)S(1)}, bf16[64,896]{1,0:T(8,128)(2,1)S(1)}, u32[]{:S(2)}, u32[]{:S(2)}) collective-permute-start(bf16[64,896]{1,0:T(8,128)(2,1)S(1)} %get-tuple-element.51), channel_id=1, source_target_pairs={{0,2},{1,3},{2,0},{3,1},{4,6},{5,7},{6,4},{7,5},{8,10},{9,11},{10,... | collective-permute-start | bytes 344072 | tf_op jit(solution)/shard_map/ppermute | solution.py:32
  15.2 8.5 %collective-permute-start.5 = (bf16[256,256]{1,0:T(8,128)(2,1)S(1)}, bf16[256,256]{1,0:T(8,128)(2,1)S(1)}, u32[]{:S(2)}, u32[]{:S(2)}) collective-permute-start(bf16[256,256]{1,0:T(8,128)(2,1)S(1)} %get-tuple-element.62), channel_id=1, source_target_pairs={{0,1},{1,0},{2,3},{3,2},{4,5},{5,4},{6,7},{7,6},{8,9},{9,8},{10,11... | collective-permute-start | bytes 393224 | tf_op jit(solution)/shard_map/ppermute | solution.py:32
  17.7 16.0 %collective-permute-start.15 = (bf16[256,128]{1,0:T(8,128)(2,1)S(1)}, bf16[256,128]{1,0:T(8,128)(2,1)S(1)}, u32[]{:S(2)}, u32[]{:S(2)}) collective-permute-start(bf16[256,128]{1,0:T(8,128)(2,1)S(1)} %slice.19), channel_id=1, source_target_pairs={{0,8},{4,12},{8,0},{12,4},{1,9},{5,13},{9,1},{13,5},{2,10},{6,14},... | collective-permute-start | bytes 196616 | tf_op jit(solution)/shard_map/ppermute | solution.py:32
  20.7 6.4 %collective-permute-start.7 = (bf16[272,128]{1,0:T(8,128)(2,1)S(1)}, bf16[272,128]{1,0:T(8,128)(2,1)S(1)}, u32[]{:S(2)}, u32[]{:S(2)}) collective-permute-start(bf16[272,128]{1,0:T(8,128)(2,1)S(1)} %get-tuple-element.65), channel_id=1, source_target_pairs={{0,12},{4,8},{8,4},{12,0},{1,13},{5,9},{9,5},{13,1},{2,14},{6,10},... | collective-permute-start | bytes 208904 | tf_op jit(solution)/shard_map/ppermute | solution.py:32
  22.2 6.9 %collective-permute-start.8 = (bf16[272,128]{1,0:T(8,128)(2,1)S(1)}, bf16[272,128]{1,0:T(8,128)(2,1)S(1)}, u32[]{:S(2)}, u32[]{:S(2)}) collective-permute-start(bf16[272,128]{1,0:T(8,128)(2,1)S(1)} %get-tuple-element.65), channel_id=1, source_target_pairs={{0,4},{4,0},{8,12},{12,8},{1,5},{5,1},{9,13},{13,9},{2,6},{6,2},{1... | collective-permute-start | bytes 208904 | tf_op jit(solution)/shard_map/ppermute | solution.py:32
  22.2 9.1 %collective-permute-start.12 = (bf16[64,256]{1,0:T(8,128)(2,1)S(1)}, bf16[64,256]{1,0:T(8,128)(2,1)S(1)}, u32[]{:S(2)}, u32[]{:S(2)}) collective-permute-start(bf16[64,256]{1,0:T(8,128)(2,1)S(1)} %get-tuple-element.67), channel_id=1, source_target_pairs={{0,2},{1,3},{2,0},{3,1},{4,6},{5,7},{6,4},{7,5},{8,10},{9,11},{10,... | collective-permute-start | bytes 98312 | tf_op jit(solution)/shard_map/ppermute | solution.py:32
  23.7 5.4 %collective-permute-start.9 = (bf16[272,128]{1,0:T(8,128)(2,1)S(1)}, bf16[272,128]{1,0:T(8,128)(2,1)S(1)}, u32[]{:S(2)}, u32[]{:S(2)}) collective-permute-start(bf16[272,128]{1,0:T(8,128)(2,1)S(1)} %get-tuple-element.65), channel_id=1, source_target_pairs={{0,8},{4,12},{8,0},{12,4},{1,9},{5,13},{9,1},{13,5},{2,10},{6,14},... | collective-permute-start | bytes 208904 | tf_op jit(solution)/shard_map/ppermute | solution.py:32
  27.0 6.7 %collective-permute-start.6 = (bf16[128,256]{1,0:T(8,128)(2,1)S(1)}, bf16[128,256]{1,0:T(8,128)(2,1)S(1)}, u32[]{:S(2)}, u32[]{:S(2)}) collective-permute-start(bf16[128,256]{1,0:T(8,128)(2,1)S(1)} %slice.22), channel_id=1, source_target_pairs={{0,2},{1,3},{2,0},{3,1},{4,6},{5,7},{6,4},{7,5},{8,10},{9,11},{10,... | collective-permute-start | bytes 196616 | tf_op jit(solution)/shard_map/ppermute | solution.py:32
  29.1 4.5 %collective-permute-start.10 = (bf16[272,128]{1,0:T(8,128)(2,1)S(1)}, bf16[272,128]{1,0:T(8,128)(2,1)S(1)}, u32[]{:S(2)}, u32[]{:S(2)}) collective-permute-start(bf16[272,128]{1,0:T(8,128)(2,1)S(1)} %shard_map.153), channel_id=1, source_target_pairs={{0,2},{1,3},{2,0},{3,1},{4,6},{5,7},{6,4},{7,5},{8,10},{9,11},{10,... | collective-permute-start | bytes 208904 | tf_op jit(solution)/shard_map/ppermute | solution.py:32
  31.3 3.3 %collective-permute-start.13 = (bf16[128,256]{1,0:T(8,128)(2,1)S(1)}, bf16[128,256]{1,0:T(8,128)(2,1)S(1)}, u32[]{:S(2)}, u32[]{:S(2)}) collective-permute-start(bf16[128,256]{1,0:T(8,128)(2,1)S(1)} %constant_dynamic-update-slice_fusion.refs_2_), channel_id=1, source_target_pairs={{0,1},{1,0},{2,3},{3,2},{4,5},{5,4},{6,7},{7,6},{8,9},{9,8},{10,11... | collective-permute-start | bytes 196616 | tf_op jit(solution)/shard_map/ppermute | solution.py:32
  33.6 1.4 %collective-permute-start.11 = (bf16[544,128]{1,0:T(8,128)(2,1)S(1)}, bf16[544,128]{1,0:T(8,128)(2,1)S(1)}, u32[]{:S(2)}, u32[]{:S(2)}) collective-permute-start(bf16[544,128]{1,0:T(8,128)(2,1)S(1)} %pad_maximum_fusion.refs_0_), channel_id=1, source_target_pairs={{0,1},{1,0},{2,3},{3,2},{4,5},{5,4},{6,7},{7,6},{8,9},{9,8},{10,11... | collective-permute-start | bytes 417800 | tf_op jit(solution)/shard_map/ppermute | solution.py:32

commit v5 on v4

--- a/solution.py
+++ b/solution.py
@@ -60,7 +60,7 @@
     )(*inputs)
 
 
-CFG = {'forder': [2, 3, 1], 'split': True, 'halves': [0, 2, 1, 3], 'a1': 'none', 'a2': 'none', 'dd': 'sent', 'p3d': True, 'p3': [3, 1, 2], 'p3split': False, 'fp': 'found1', 'dx': 'found1', 'hid': 'none', 'cd': 3}
+CFG = {'forder': [3, 1, 2], 'split': True, 'halves': [0, 1, 2, 3], 'a1': 'none', 'a2': 'found', 'dd': 'none', 'p3d': True, 'p3': [3, 1, 2], 'p3split': True, 'fp': 'found1', 'dx': 'found1', 'hid': 'none', 'cd': 3, 'fwd': False, 'ck': 0, 'cb': 0, 'cr': 0, 'cs': 0, 'cm': 0.5, 'ca': 0}
 
 
 def spread(block, axis, steps):
@@ -72,9 +72,9 @@
 
 
 def select(rows, cols, ids_in, src_in, dst_in, count_in, tiles_in, cotangent_in, degree_in, *refs):
-    weights_in, refs = refs[:3], refs[3:]
+    weights_in, refs = refs[:4], refs[4:]
     adjacency, column_picks, own_picks, known, near, far, inverse, *refs = refs
-    weights, (picks, src, dst, count, tiles, cotangent, degree, ids, sems) = refs[:3], refs[3:]
+    weights, (picks, src, dst, count, tiles, cotangent, degree, ids, sems) = refs[:4], refs[4:]
     pairs = [(src_in, src), (dst_in, dst), (count_in, count), (tiles_in, tiles)]
     pairs += [(cotangent_in, cotangent), (degree_in, degree), (ids_in, ids)]
     pairs += list(zip(weights_in, weights))
@@ -259,12 +259,16 @@
     half = slots // 2
 
     tie = lax.optimization_barrier
-    feature_parts = spread(features, "row", CFG["forder"])
-    steps = tuple(feature_parts)
-    feature_parts[0] = features
+    if CFG["fwd"]:
+        feature_parts = spread(features, "row", (2, 1))
+        feature_parts[3] = trade(feature_parts[2], "row", 1)
+    else:
+        feature_parts = spread(features, "row", tuple(CFG["forder"]))
+    steps = tuple(CFG["forder"])
+    raw_features = features
 
     bias = layer_bias.reshape(1, width)
-    adjacency, column_picks, own_picks, known, near, far, inverse, w_self, w_neigh, bias = call(
+    adjacency, column_picks, own_picks, known, near, far, inverse, *resident = call(
         functools.partial(select, rows, cols),
         [
             ((rows, cols * nodes, nodes), BF16),
@@ -275,7 +279,7 @@
         + [((rows // 2 * slots, nodes), BF16)] * 2
         + [((nodes, nodes), F32)]
         + [((width, width), BF16)] * 2
-        + [((1, width), F32)],
+        + [((1, width), F32), ((nodes, width), BF16)],
         target_ids.reshape(1, slots),
         tile_src,
         tile_dst,
@@ -286,13 +290,17 @@
         w_self,
         w_neigh,
         bias,
-        spaces=[pltpu.HBM] * 3 + [pl.ANY] + [pltpu.HBM] * 6,
+        raw_features,
+        spaces=[pltpu.HBM] * 3 + [pl.ANY] + [pltpu.HBM] * 7,
+        cost=CFG["ck"],
         scratch=[pltpu.VMEM((slots, cols * nodes), BF16)]
         + [pltpu.SMEM(x.shape, x.dtype) for x in (tile_src, tile_dst, tile_count)]
         + [pltpu.VMEM(x.shape, x.dtype) for x in (tile_vals, cotangent)]
         + [pltpu.VMEM((1, nodes), jnp.int32), pltpu.VMEM((1, slots), jnp.int32)]
-        + [pltpu.SemaphoreType.DMA((10,))],
-    )
+        + [pltpu.SemaphoreType.DMA((11,))],
+    )
+    w_self, w_neigh, bias, features = resident
+    feature_parts[0] = features
     first = ()
     if CFG["split"]:
         first = call(
@@ -302,6 +310,7 @@
             feature_parts[steps[0]],
             near,
             far,
+            cost=CFG["cb"],
         )
     later = steps[len(first) // 2 :] + (0,)
     sent, part, fixed = call(
@@ -313,6 +322,7 @@
         near,
         far,
         *first,
+        cost=CFG["cb"],
     )
     got = trade(sent, "col", 1)
     sent, part, fixed = call(
@@ -321,6 +331,7 @@
         part,
         fixed,
         got,
+        cost=CFG["cr"],
     )
     if CFG["a1"] == "sent":
         sent, far = tie((sent, far))
@@ -336,6 +347,7 @@
         w_self,
         w_neigh,
         bias,
+        cost=CFG["cs"],
     )
     if CFG["a1"] == "found":
         found, far = tie((found, far))
@@ -360,9 +372,9 @@
     parts = spread(found, "row", CFG["p3"]) if CFG["p3d"] else None
     if CFG["p3d"]:
         if CFG["p3split"]:
-            (found,) = call(merge, [(found.shape, BF16)], parts.pop(CFG["p3"][0]), found)
+            (found,) = call(merge, [(found.shape, BF16)], *[parts.pop(CFG["p3"][0]), found], cost=CFG["cm"])
     else:
-        (found,) = call(merge, [(found.shape, BF16)], trade(found, "row", CFG["p3"][0]), found)
+        (found,) = call(merge, [(found.shape, BF16)], *[trade(found, "row", CFG["p3"][0]), found], cost=CFG["cm"])
     if CFG["a2"] == "found1":
         found, columns = tie((found, columns))
     if CFG["fp"] == "found1":
@@ -370,15 +382,22 @@
     if CFG["dx"] == "found1":
         found, dense = tie((found, dense))
     if CFG["p3d"]:
-        (found,) = call(merge, [(found.shape, BF16)], *parts.values(), found)
+        (found,) = call(merge, [(found.shape, BF16)], *[*parts.values(), found], cost=CFG["cm"])
     else:
-        (found,) = call(merge, [(found.shape, BF16)], trade(found, "row", CFG["p3"][1]), found)
+        (found,) = call(merge, [(found.shape, BF16)], *[trade(found, "row", CFG["p3"][1]), found], cost=CFG["cm"])
     if CFG["dx"] == "merged":
         found, dense = tie((found, dense))
     own_columns = columns[:slots] + trade(columns[slots:], "row", near_step)
-    dense_got = trade(dense[nodes:].astype(BF16), "col", 2)
+    if CFG["fp"] == "join":
+        joined = jnp.concatenate([feature_slots, dense[nodes:].astype(BF16)], axis=0)
+        found, joined = tie((found, joined))
+        joined = trade(joined, "col", 2)
+        feature_mine = jnp.concatenate([feature_slots, joined[:share]], axis=0)
+        dense_got = joined[share:]
+    else:
+        dense_got = trade(dense[nodes:].astype(BF16), "col", 2)
+        feature_mine = jnp.concatenate([feature_slots, trade(feature_slots, "col", 2)], axis=0)
     if CFG["fp"] != "none":
-        feature_mine = jnp.concatenate([feature_slots, trade(feature_slots, "col", 2)], axis=0)
         feature_other = trade(feature_mine, "col", 1)
         everything = found
     else:
@@ -399,6 +418,7 @@
         w_self,
         w_neigh,
         bias,
+        cost=CFG["ca"],
     )
     results = [((nodes, width), BF16), ((width, width), F32), ((width, width), F32), ((1, width), F32)]
     grad_features, grad_self, grad_neigh, grad_bias = call(

time: 36.4 us -> 35.8 us (0.984)
  starting transfers between devices: 21.3 us -> 19.7 us
  waiting for transfers between devices: 8.01 us -> 9.01 us
    ppermute x16, starting transfers between devices: 21.3 us -> 19.7 us  [trade(): lax.ppermute(block, axis, [(i, i ^ step) for i in range(lax.axis_size(axi...]
    ppermute x16, waiting for transfers between devices: 8.01 us -> 9.01 us  [trade(): lax.ppermute(block, axis, [(i, i ^ step) for i in range(lax.axis_size(axi...]
    pallas_call x9 -> x10, Pallas kernels: 5.35 us -> 5.43 us  [call(): pl.pallas_call(kernel, out_shape=[jax.ShapeDtypeStruct(shape, dtype) for...]
  transfers between devices with their start and end apart: 16 -> 16, of which waited for: 7 -> 7; matrix products, arithmetic and copies ran while one was open for 0% -> 0% of each run, Pallas kernels for 11% -> 12%
where the time goes in v5:
time: 35.8 us; the launch traced here: 35.7 us
  starting transfers between devices  19.7 us (55%)
  waiting for transfers between devices  9.01 us (25%)
  Pallas kernels  5.43 us (15%)
  between operations  1.43 us (4%)
    ppermute x16, starting transfers between devices, trade(): lax.ppermute(block, axis, [(i, i ^ step) for i in range(lax.axis_size(axi...  19.7 us
    ppermute x16, waiting for transfers between devices, trade(): lax.ppermute(block, axis, [(i, i ^ step) for i in range(lax.axis_size(axi...  9.01 us
    pallas_call x10, Pallas kernels, call(): pl.pallas_call(kernel, out_shape=[jax.ShapeDtypeStruct(shape, dtype) for...  5.43 us
  transfers between devices with their start and end apart: 16, of which 7 were waited for; matrix products, arithmetic and copies ran while one was open for 0% of the time, Pallas kernels for 12%

profile of v5, /device:TPU:0, one launch (start us, length us, event | category | flops | bytes accessed | tf_op | source)
XLA Modules:
  0.0 35.7 jit_solution(9769453788454228793)
XLA Ops:
  0.6 5.1 %collective-permute-start.2 = (bf16[128,256]{1,0:T(8,128)(2,1)}, bf16[128,256]{1,0:T(8,128)(2,1)S(1)}, u32[]{:S(2)}, u32[]{:S(2)}) collective-permute-start(bf16[128,256]{1,0:T(8,128)(2,1)} %refs_3_.1), channel_id=1, source_target_pairs={{0,12},{4,8},{8,4},{12,0},{1,13},{5,9},{9,5},{13,1},{2,14},{6,10},... | collective-permute-start | bytes 196616 | tf_op jit(solution)/shard_map/ppermute | solution.py:32
  5.8 0.0 collective-permute-start
  5.8 0.6 %collective-permute-start.1 = (bf16[128,256]{1,0:T(8,128)(2,1)}, bf16[128,256]{1,0:T(8,128)(2,1)S(1)}, u32[]{:S(2)}, u32[]{:S(2)}) collective-permute-start(bf16[128,256]{1,0:T(8,128)(2,1)} %refs_3_.1), channel_id=1, source_target_pairs={{0,8},{4,12},{8,0},{12,4},{1,9},{5,13},{9,1},{13,5},{2,10},{6,14},... | collective-permute-start | bytes 196616 | tf_op jit(solution)/shard_map/ppermute | solution.py:32
  7.0 2.1 %shard_map.146 = (bf16[4,512,128]{2,1,0:T(8,128)(2,1)S(1)}, bf16[256,512]{1,0:T(8,128)(2,1)S(1)}, bf16[128,256]{1,0:T(8,128)(2,1)S(1)}, bf16[256,384]{1,0:T(8,12...) custom-call(s32[1,256]{1,0:T(1,128)} %bitcast.4, ...), custom_call_target="tpu_custom_call" | custom-call | tf_op jit(solution)/shard_map/pallas_call | solution.py:52
  9.1 2.4 %collective-permute-start.5 = (bf16[512,128]{1,0:T(8,128)(2,1)S(1)}, bf16[512,128]{1,0:T(8,128)(2,1)S(1)}, u32[]{:S(2)}, u32[]{:S(2)}) collective-permute-start(bf16[512,128]{1,0:T(8,128)(2,1)S(1)} %get-tuple-element.42.far.refs_4_), channel_id=1, source_target_pairs={{0,8},{4,12},{8,0},{12,4},{1,9},{5,13},{9,1},{13,5},{2,10},{6,14},... | collective-permute-start | bytes 393224 | tf_op jit(solution)/shard_map/ppermute | solution.py:32
  11.5 0.0 collective-permute-done.2.features.refs_0_
  11.5 0.2 shard_map.147
  11.7 0.0 collective-permute-done.refs_0_.refs_1_
  11.7 0.0 collective-permute-done.1.refs_1_.refs_2_
  11.7 0.4 shard_map.148
  12.1 0.1 collective-permute-start.3
  12.2 0.4 %shard_map.152 = (f32[256,256]{1,0:T(8,128)S(1)}, bf16[256,256]{1,0:T(8,128)(2,1)S(1)}) custom-call(bf16[4,512,128]{2,1,0:T(8,128)(2,1)S(1)} %get-tuple-element.58.adjacency, bf16[128,256]{1,0:T(8,128)(2,1)S(1)} %collective-permute-done.2.features.refs_0_, bf16[128,256]{1,0:T(8,128)(2,1)S(1)} %collective-permute-done.refs_0_.refs_1_, ...), custom_call_target="tpu_custom_call" | custom-call | flops 3000000000 | tf_op jit(solution)/shard_map/pallas_call | solution.py:52
  12.6 0.6 %collective-permute-start.7 = (bf16[256,256]{1,0:T(8,128)(2,1)S(1)}, bf16[256,256]{1,0:T(8,128)(2,1)S(1)}, u32[]{:S(2)}, u32[]{:S(2)}) collective-permute-start(bf16[256,256]{1,0:T(8,128)(2,1)S(1)} %get-tuple-element.60), channel_id=1, source_target_pairs={{0,1},{1,0},{2,3},{3,2},{4,5},{5,4},{6,7},{7,6},{8,9},{9,8},{10,11... | collective-permute-start | bytes 393224 | tf_op jit(solution)/shard_map/ppermute | solution.py:32
  13.2 0.5 %collective-permute-done.3.got = bf16[128,896]{1,0:T(8,128)(2,1)S(1)} collective-permute-done((bf16[128,896]{1,0:T(8,128)(2,1)S(1)}, bf16[128,896]{1,0:T(8,128)(2,1)S(1)}, u32[]{:S(2)}, u32[]{:S(2)}) %collective-permute-start.3) | collective-permute-done | bytes 229408 | tf_op jit(solution)/shard_map/ppermute | solution.py:32
  13.7 1.5 %collective-permute-start.4 = (bf16[64,896]{1,0:T(8,128)(2,1)S(1)}, bf16[64,896]{1,0:T(8,128)(2,1)S(1)}, u32[]{:S(2)}, u32[]{:S(2)}) collective-permute-start(bf16[64,896]{1,0:T(8,128)(2,1)S(1)} %get-tuple-element.50), channel_id=1, source_target_pairs={{0,2},{1,3},{2,0},{3,1},{4,6},{5,7},{6,4},{7,5},{8,10},{9,11},{10,... | collective-permute-start | bytes 344072 | tf_op jit(solution)/shard_map/ppermute | solution.py:32
  15.2 3.0 %collective-permute-done.5 = bf16[512,128]{1,0:T(8,128)(2,1)S(1)} collective-permute-done((bf16[512,128]{1,0:T(8,128)(2,1)S(1)}, bf16[512,128]{1,0:T(8,128)(2,1)S(1)}, u32[]{:S(2)}, u32[]{:S(2)}) %collective-permute-start.5) | collective-permute-done | bytes 131104 | tf_op jit(solution)/shard_map/ppermute | solution.py:32
  18.2 0.7 %collective-permute-done.4.got = bf16[64,896]{1,0:T(8,128)(2,1)S(1)} collective-permute-done((bf16[64,896]{1,0:T(8,128)(2,1)S(1)}, bf16[64,896]{1,0:T(8,128)(2,1)S(1)}, u32[]{:S(2)}, u32[]{:S(2)}) %collective-permute-start.4) | collective-permute-done | bytes 114720 | tf_op jit(solution)/shard_map/ppermute | solution.py:32
  18.9 0.2 shard_map.150
  19.2 2.1 %collective-permute-start.6 = (bf16[272,128]{1,0:T(8,128)(2,1)S(1)}, bf16[272,128]{1,0:T(8,128)(2,1)S(1)}, u32[]{:S(2)}, u32[]{:S(2)}) collective-permute-start(bf16[272,128]{1,0:T(8,128)(2,1)S(1)} %get-tuple-element.55.refs_1_), channel_id=1, source_target_pairs={{0,12},{4,8},{8,4},{12,0},{1,13},{5,9},{9,5},{13,1},{2,14},{6,10},... | collective-permute-start | bytes 208904 | tf_op jit(solution)/shard_map/ppermute | solution.py:32
  21.3 0.0 collective-permute-done.7
  21.3 1.5 %collective-permute-start.10 = (bf16[272,128]{1,0:T(8,128)(2,1)S(1)}, bf16[272,128]{1,0:T(8,128)(2,1)S(1)}, u32[]{:S(2)}, u32[]{:S(2)}) collective-permute-start(bf16[272,128]{1,0:T(8,128)(2,1)S(1)} %get-tuple-element.55.refs_1_), channel_id=1, source_target_pairs={{0,8},{4,12},{8,0},{12,4},{1,9},{5,13},{9,1},{13,5},{2,10},{6,14},... | collective-permute-start | bytes 208904 | tf_op jit(solution)/shard_map/ppermute | solution.py:32
  22.8 0.9 %collective-permute-start.9 = (bf16[272,128]{1,0:T(8,128)(2,1)S(1)}, bf16[272,128]{1,0:T(8,128)(2,1)S(1)}, u32[]{:S(2)}, u32[]{:S(2)}) collective-permute-start(bf16[272,128]{1,0:T(8,128)(2,1)S(1)} %get-tuple-element.55.refs_1_), channel_id=1, source_target_pairs={{0,4},{4,0},{8,12},{12,8},{1,5},{5,1},{9,13},{13,9},{2,6},{6,2},{1... | collective-permute-start | bytes 208904 | tf_op jit(solution)/shard_map/ppermute | solution.py:32
  23.7 1.1 %collective-permute-start.15 = (bf16[256,128]{1,0:T(8,128)(2,1)S(1)}, bf16[256,128]{1,0:T(8,128)(2,1)S(1)}, u32[]{:S(2)}, u32[]{:S(2)}) collective-permute-start(bf16[256,128]{1,0:T(8,128)(2,1)S(1)} %slice.16), channel_id=1, source_target_pairs={{0,4},{4,0},{8,12},{12,8},{1,5},{5,1},{9,13},{13,9},{2,6},{6,2},{1... | collective-permute-start | bytes 196616 | tf_op jit(solution)/shard_map/ppermute | solution.py:32
  24.8 0.6 %collective-permute-done.6.refs_0_ = bf16[272,128]{1,0:T(8,128)(2,1)S(1)} collective-permute-done((bf16[272,128]{1,0:T(8,128)(2,1)S(1)}, bf16[272,128]{1,0:T(8,128)(2,1)S(1)}, u32[]{:S(2)}, u32[]{:S(2)}) %collective-permute-start.6) | collective-permute-done | bytes 69664 | tf_op jit(solution)/shard_map/ppermute | solution.py:32
  25.5 1.5 %collective-permute-start.13 = (bf16[64,256]{1,0:T(8,128)(2,1)S(1)}, bf16[64,256]{1,0:T(8,128)(2,1)S(1)}, u32[]{:S(2)}, u32[]{:S(2)}) collective-permute-start(bf16[64,256]{1,0:T(8,128)(2,1)S(1)} %get-tuple-element.64), channel_id=1, source_target_pairs={{0,2},{1,3},{2,0},{3,1},{4,6},{5,7},{6,4},{7,5},{8,10},{9,11},{10,... | collective-permute-start | bytes 98312 | tf_op jit(solution)/shard_map/ppermute | solution.py:32
  27.0 0.6 %collective-permute-start.8 = (bf16[128,256]{1,0:T(8,128)(2,1)S(1)}, bf16[128,256]{1,0:T(8,128)(2,1)S(1)}, u32[]{:S(2)}, u32[]{:S(2)}) collective-permute-start(bf16[128,256]{1,0:T(8,128)(2,1)S(1)} %slice.20), channel_id=1, source_target_pairs={{0,2},{1,3},{2,0},{3,1},{4,6},{5,7},{6,4},{7,5},{8,10},{9,11},{10,... | collective-permute-start | bytes 196616 | tf_op jit(solution)/shard_map/ppermute | solution.py:32
  27.6 1.0 %collective-permute-done.10.refs_1_ = bf16[272,128]{1,0:T(8,128)(2,1)S(1)} collective-permute-done((bf16[272,128]{1,0:T(8,128)(2,1)S(1)}, bf16[272,128]{1,0:T(8,128)(2,1)S(1)}, u32[]{:S(2)}, u32[]{:S(2)}) %collective-permute-start.10) | collective-permute-done | bytes 69664 | tf_op jit(solution)/shard_map/ppermute | solution.py:32
  28.6 0.0 collective-permute-done.9.refs_0_
  28.7 1.6 %collective-permute-start.11 = (bf16[272,128]{1,0:T(8,128)(2,1)S(1)}, bf16[272,128]{1,0:T(8,128)(2,1)S(1)}, u32[]{:S(2)}, u32[]{:S(2)}) collective-permute-start(bf16[272,128]{1,0:T(8,128)(2,1)S(1)} %shard_map.154), channel_id=1, source_target_pairs={{0,2},{1,3},{2,0},{3,1},{4,6},{5,7},{6,4},{7,5},{8,10},{9,11},{10,... | collective-permute-start | bytes 208904 | tf_op jit(solution)/shard_map/ppermute | solution.py:32
  30.2 0.0 collective-permute-done.13
  30.3 0.0 collective-permute-start.14
  30.3 2.8 %collective-permute-done.11 = bf16[272,128]{1,0:T(8,128)(2,1)S(1)} collective-permute-done((bf16[272,128]{1,0:T(8,128)(2,1)S(1)}, bf16[272,128]{1,0:T(8,128)(2,1)S(1)}, u32[]{:S(2)}, u32[]{:S(2)}) %collective-permute-start.11) | collective-permute-done | bytes 69664 | tf_op jit(solution)/shard_map/ppermute | solution.py:32
  33.1 0.1 collective-permute-start.12
  33.2 0.0 collective-permute-done.15
  33.2 0.0 collective-permute-done.8.got
  33.2 0.9 %shard_map.153 = bf16[128,256]{1,0:T(8,128)(2,1)} custom-call(bf16[128,256]{1,0:T(8,128)(2,1)S(1)} %get-tuple-element.38.refs_2_.refs_3_.features, f32[128,256]{1,0:T(8,128)S(1)} %slice.13.total, bf16[128,256]{1,0:T(8,128)(2,1)S(1)} %collective-permute-done.8.got, f32[128,128]{1,0:T(8,128)S(1)} %get-tuple-element.62.inverse, ...), custom_call_target="tpu_custom_call" | custom-call | tf_op jit(solution)/shard_map/pallas_call | solution.py:52
  34.1 0.0 collective-permute-done.14.refs_3_
  34.1 0.4 %collective-permute-done.12.refs_1_ = bf16[544,128]{1,0:T(8,128)(2,1)S(1)} collective-permute-done((bf16[544,128]{1,0:T(8,128)(2,1)S(1)}, bf16[544,128]{1,0:T(8,128)(2,1)S(1)}, u32[]{:S(2)}, u32[]{:S(2)}) %collective-permute-start.12) | collective-permute-done | bytes 139296 | tf_op jit(solution)/shard_map/ppermute | solution.py:32
  34.5 1.2 %shard_map.155 = (bf16[128,256]{1,0:T(8,128)(2,1)}, f32[256,256]{1,0:T(8,128)}, f32[256,256]{1,0:T(8,128)}, f32[1,256]{1,0:T(1,128)}) custom-call(bf16[544,128]{1,0:T(8,128)(2,1)S(1)} %pad_maximum_fusion.refs_0_, bf16[544,128]{1,0:T(8,128)(2,1)S(1)} %collective-permute-done.12.refs_1_, bf16[128,256]{1,0:T(8,128)(2,1)S(1)} %constant_dynamic-update-slice_fusion.refs_2_, ...), custom_call_target="tpu_custom_call" | custom-call | tf_op jit(solution)/shard_map/pallas_call | solution.py:52
  (12 shorter events, 0.2 us)
Async XLA Ops:
  0.6 10.9 %collective-permute-start.2 = (bf16[128,256]{1,0:T(8,128)(2,1)}, bf16[128,256]{1,0:T(8,128)(2,1)S(1)}, u32[]{:S(2)}, u32[]{:S(2)}) collective-permute-start(bf16[128,256]{1,0:T(8,128)(2,1)} %refs_3_.1), channel_id=1, source_target_pairs={{0,12},{4,8},{8,4},{12,0},{1,13},{5,9},{9,5},{13,1},{2,14},{6,10},... | collective-permute-start | bytes 196616 | tf_op jit(solution)/shard_map/ppermute | solution.py:32
  5.8 6.0 %collective-permute-start = (bf16[128,256]{1,0:T(8,128)(2,1)}, bf16[128,256]{1,0:T(8,128)(2,1)S(1)}, u32[]{:S(2)}, u32[]{:S(2)}) collective-permute-start(bf16[128,256]{1,0:T(8,128)(2,1)} %refs_3_.1), channel_id=1, source_target_pairs={{0,4},{4,0},{8,12},{12,8},{1,5},{5,1},{9,13},{13,9},{2,6},{6,2},{1... | collective-permute-start | bytes 196616 | tf_op jit(solution)/shard_map/ppermute | solution.py:32
  5.8 6.0 %collective-permute-start.1 = (bf16[128,256]{1,0:T(8,128)(2,1)}, bf16[128,256]{1,0:T(8,128)(2,1)S(1)}, u32[]{:S(2)}, u32[]{:S(2)}) collective-permute-start(bf16[128,256]{1,0:T(8,128)(2,1)} %refs_3_.1), channel_id=1, source_target_pairs={{0,8},{4,12},{8,0},{12,4},{1,9},{5,13},{9,1},{13,5},{2,10},{6,14},... | collective-permute-start | bytes 196616 | tf_op jit(solution)/shard_map/ppermute | solution.py:32
  9.1 9.1 %collective-permute-start.5 = (bf16[512,128]{1,0:T(8,128)(2,1)S(1)}, bf16[512,128]{1,0:T(8,128)(2,1)S(1)}, u32[]{:S(2)}, u32[]{:S(2)}) collective-permute-start(bf16[512,128]{1,0:T(8,128)(2,1)S(1)} %get-tuple-element.42.far.refs_4_), channel_id=1, source_target_pairs={{0,8},{4,12},{8,0},{12,4},{1,9},{5,13},{9,1},{13,5},{2,10},{6,14},... | collective-permute-start | bytes 393224 | tf_op jit(solution)/shard_map/ppermute | solution.py:32
  12.1 1.6 %collective-permute-start.3 = (bf16[128,896]{1,0:T(8,128)(2,1)S(1)}, bf16[128,896]{1,0:T(8,128)(2,1)S(1)}, u32[]{:S(2)}, u32[]{:S(2)}) collective-permute-start(bf16[128,896]{1,0:T(8,128)(2,1)S(1)} %get-tuple-element.47), channel_id=1, source_target_pairs={{0,1},{1,0},{2,3},{3,2},{4,5},{5,4},{6,7},{7,6},{8,9},{9,8},{10,11... | collective-permute-start | bytes 688136 | tf_op jit(solution)/shard_map/ppermute | solution.py:32
  12.6 8.7 %collective-permute-start.7 = (bf16[256,256]{1,0:T(8,128)(2,1)S(1)}, bf16[256,256]{1,0:T(8,128)(2,1)S(1)}, u32[]{:S(2)}, u32[]{:S(2)}) collective-permute-start(bf16[256,256]{1,0:T(8,128)(2,1)S(1)} %get-tuple-element.60), channel_id=1, source_target_pairs={{0,1},{1,0},{2,3},{3,2},{4,5},{5,4},{6,7},{7,6},{8,9},{9,8},{10,11... | collective-permute-start | bytes 393224 | tf_op jit(solution)/shard_map/ppermute | solution.py:32
  13.7 5.3 %collective-permute-start.4 = (bf16[64,896]{1,0:T(8,128)(2,1)S(1)}, bf16[64,896]{1,0:T(8,128)(2,1)S(1)}, u32[]{:S(2)}, u32[]{:S(2)}) collective-permute-start(bf16[64,896]{1,0:T(8,128)(2,1)S(1)} %get-tuple-element.50), channel_id=1, source_target_pairs={{0,2},{1,3},{2,0},{3,1},{4,6},{5,7},{6,4},{7,5},{8,10},{9,11},{10,... | collective-permute-start | bytes 344072 | tf_op jit(solution)/shard_map/ppermute | solution.py:32
  19.2 6.3 %collective-permute-start.6 = (bf16[272,128]{1,0:T(8,128)(2,1)S(1)}, bf16[272,128]{1,0:T(8,128)(2,1)S(1)}, u32[]{:S(2)}, u32[]{:S(2)}) collective-permute-start(bf16[272,128]{1,0:T(8,128)(2,1)S(1)} %get-tuple-element.55.refs_1_), channel_id=1, source_target_pairs={{0,12},{4,8},{8,4},{12,0},{1,13},{5,9},{9,5},{13,1},{2,14},{6,10},... | collective-permute-start | bytes 208904 | tf_op jit(solution)/shard_map/ppermute | solution.py:32
  21.3 7.4 %collective-permute-start.10 = (bf16[272,128]{1,0:T(8,128)(2,1)S(1)}, bf16[272,128]{1,0:T(8,128)(2,1)S(1)}, u32[]{:S(2)}, u32[]{:S(2)}) collective-permute-start(bf16[272,128]{1,0:T(8,128)(2,1)S(1)} %get-tuple-element.55.refs_1_), channel_id=1, source_target_pairs={{0,8},{4,12},{8,0},{12,4},{1,9},{5,13},{9,1},{13,5},{2,10},{6,14},... | collective-permute-start | bytes 208904 | tf_op jit(solution)/shard_map/ppermute | solution.py:32
  22.8 5.8 %collective-permute-start.9 = (bf16[272,128]{1,0:T(8,128)(2,1)S(1)}, bf16[272,128]{1,0:T(8,128)(2,1)S(1)}, u32[]{:S(2)}, u32[]{:S(2)}) collective-permute-start(bf16[272,128]{1,0:T(8,128)(2,1)S(1)} %get-tuple-element.55.refs_1_), channel_id=1, source_target_pairs={{0,4},{4,0},{8,12},{12,8},{1,5},{5,1},{9,13},{13,9},{2,6},{6,2},{1... | collective-permute-start | bytes 208904 | tf_op jit(solution)/shard_map/ppermute | solution.py:32
  23.7 9.4 %collective-permute-start.15 = (bf16[256,128]{1,0:T(8,128)(2,1)S(1)}, bf16[256,128]{1,0:T(8,128)(2,1)S(1)}, u32[]{:S(2)}, u32[]{:S(2)}) collective-permute-start(bf16[256,128]{1,0:T(8,128)(2,1)S(1)} %slice.16), channel_id=1, source_target_pairs={{0,4},{4,0},{8,12},{12,8},{1,5},{5,1},{9,13},{13,9},{2,6},{6,2},{1... | collective-permute-start | bytes 196616 | tf_op jit(solution)/shard_map/ppermute | solution.py:32
  25.5 4.8 %collective-permute-start.13 = (bf16[64,256]{1,0:T(8,128)(2,1)S(1)}, bf16[64,256]{1,0:T(8,128)(2,1)S(1)}, u32[]{:S(2)}, u32[]{:S(2)}) collective-permute-start(bf16[64,256]{1,0:T(8,128)(2,1)S(1)} %get-tuple-element.64), channel_id=1, source_target_pairs={{0,2},{1,3},{2,0},{3,1},{4,6},{5,7},{6,4},{7,5},{8,10},{9,11},{10,... | collective-permute-start | bytes 98312 | tf_op jit(solution)/shard_map/ppermute | solution.py:32
  27.0 6.2 %collective-permute-start.8 = (bf16[128,256]{1,0:T(8,128)(2,1)S(1)}, bf16[128,256]{1,0:T(8,128)(2,1)S(1)}, u32[]{:S(2)}, u32[]{:S(2)}) collective-permute-start(bf16[128,256]{1,0:T(8,128)(2,1)S(1)} %slice.20), channel_id=1, source_target_pairs={{0,2},{1,3},{2,0},{3,1},{4,6},{5,7},{6,4},{7,5},{8,10},{9,11},{10,... | collective-permute-start | bytes 196616 | tf_op jit(solution)/shard_map/ppermute | solution.py:32
  28.7 4.4 %collective-permute-start.11 = (bf16[272,128]{1,0:T(8,128)(2,1)S(1)}, bf16[272,128]{1,0:T(8,128)(2,1)S(1)}, u32[]{:S(2)}, u32[]{:S(2)}) collective-permute-start(bf16[272,128]{1,0:T(8,128)(2,1)S(1)} %shard_map.154), channel_id=1, source_target_pairs={{0,2},{1,3},{2,0},{3,1},{4,6},{5,7},{6,4},{7,5},{8,10},{9,11},{10,... | collective-permute-start | bytes 208904 | tf_op jit(solution)/shard_map/ppermute | solution.py:32
  30.3 3.8 %collective-permute-start.14 = (bf16[128,256]{1,0:T(8,128)(2,1)S(1)}, bf16[128,256]{1,0:T(8,128)(2,1)S(1)}, u32[]{:S(2)}, u32[]{:S(2)}) collective-permute-start(bf16[128,256]{1,0:T(8,128)(2,1)S(1)} %constant_dynamic-update-slice_fusion.refs_2_), channel_id=1, source_target_pairs={{0,1},{1,0},{2,3},{3,2},{4,5},{5,4},{6,7},{7,6},{8,9},{9,8},{10,11... | collective-permute-start | bytes 196616 | tf_op jit(solution)/shard_map/ppermute | solution.py:32
  33.1 1.4 %collective-permute-start.12 = (bf16[544,128]{1,0:T(8,128)(2,1)S(1)}, bf16[544,128]{1,0:T(8,128)(2,1)S(1)}, u32[]{:S(2)}, u32[]{:S(2)}) collective-permute-start(bf16[544,128]{1,0:T(8,128)(2,1)S(1)} %pad_maximum_fusion.refs_0_), channel_id=1, source_target_pairs={{0,1},{1,0},{2,3},{3,2},{4,5},{5,4},{6,7},{7,6},{8,9},{9,8},{10,11... | collective-permute-start | bytes 417800 | tf_op jit(solution)/shard_map/ppermute | solution.py:32

commit v6 on v4

--- a/solution.py
+++ b/solution.py
@@ -43,7 +43,11 @@
     return jnp.where(bit == 1, jnp.concatenate(turned, axis=1), line)
 
 
-def call(kernel, outputs, *inputs, spaces=(), scratch=(), out_space=pltpu.VMEM, cost=0):
+MERGE_COST = pl.CostEstimate(flops=2 * 10**9, bytes_accessed=0, transcendentals=0)
+DENSE_COST = pl.CostEstimate(flops=3 * 10**9, bytes_accessed=0, transcendentals=0)
+
+
+def call(kernel, outputs, *inputs, spaces=(), scratch=(), out_space=pltpu.VMEM, cost=None):
     inputs = [
         pltpu.with_memory_space_constraint(x, y) if y == pltpu.HBM else x
         for x, y in itertools.zip_longest(inputs, spaces)
@@ -55,14 +59,11 @@
         in_specs=[pl.BlockSpec(memory_space=space) for space in spaces],
         out_specs=[pl.BlockSpec(memory_space=out_space) for _ in outputs],
         scratch_shapes=scratch,
-        cost_estimate=pl.CostEstimate(flops=int(cost * 1e9), bytes_accessed=0, transcendentals=0) if cost else None,
+        cost_estimate=cost,
         compiler_params=pltpu.CompilerParams(vmem_limit_bytes=32 * 2**20),
     )(*inputs)
 
 
-CFG = {'forder': [2, 3, 1], 'split': True, 'halves': [0, 2, 1, 3], 'a1': 'none', 'a2': 'none', 'dd': 'sent', 'p3d': True, 'p3': [3, 1, 2], 'p3split': False, 'fp': 'found1', 'dx': 'found1', 'hid': 'none', 'cd': 3}
-
-
 def spread(block, axis, steps):
     return {step: trade(block, axis, step) for step in steps}
 
@@ -72,11 +73,11 @@
 
 
 def select(rows, cols, ids_in, src_in, dst_in, count_in, tiles_in, cotangent_in, degree_in, *refs):
-    weights_in, refs = refs[:3], refs[3:]
+    weights_in, refs = refs[:4], refs[4:]
     adjacency, column_picks, own_picks, known, near, far, inverse, *refs = refs
-    weights, (picks, src, dst, count, tiles, cotangent, degree, ids, sems) = refs[:3], refs[3:]
-    pairs = [(src_in, src), (dst_in, dst), (count_in, count), (tiles_in, tiles)]
-    pairs += [(cotangent_in, cotangent), (degree_in, degree), (ids_in, ids)]
+    weights, (picks, src, dst, count, tiles, cotangent, degree, ids, sems) = refs[:4], refs[4:]
+    pairs = [(ids_in, ids), (cotangent_in, cotangent), (degree_in, degree), (tiles_in, tiles)]
+    pairs += [(src_in, src), (dst_in, dst), (count_in, count)]
     pairs += list(zip(weights_in, weights))
     copies = [pltpu.make_async_copy(a, b, sems.at[i]) for i, (a, b) in enumerate(pairs)]
     for copy in copies:
@@ -84,15 +85,7 @@
     row, col = lax.axis_index("row"), lax.axis_index("col")
     slots, (nodes, width) = ids.shape[1], cotangent.shape
     adjacency[...] = jnp.zeros(adjacency.shape, adjacency.dtype)
-    for copy in copies[:7]:
-        copy.wait()
-    for k in range(tiles.shape[2]):
-
-        @pl.when(k < count[0, 0])
-        def _():
-            down = pl.multiple_of(swap_bits(dst[0, 0, k] ^ col) * nodes, nodes)
-            adjacency[src[0, 0, k] ^ row, pl.ds(down, nodes), :] = tiles[0, 0, k]
-
+    copies[0].wait()
     line = flip(flip(swap_quarters(ids[...]), 2, col % 2), 4, col // 2)
     line = jnp.broadcast_to(line, (nodes, slots))
     stack = line.T
@@ -106,23 +99,30 @@
     base = (row * cols + col) * nodes
     across = lax.broadcasted_iota(jnp.int32, (nodes, slots), 0)
     own_picks[...] = (line == across + base).astype(BF16)
-    for s in range(rows):
-        block = dot(picks[...], adjacency[s]).astype(BF16)
-        index = list(CFG["halves"]).index(s)
-        (far if index // 2 else near)[index % 2 * slots : (index % 2 + 1) * slots, :] = block
+    for copy in copies[1:3]:
+        copy.wait()
     own = picks[:, :nodes]
     known[:, :width] = dot(own, cotangent[...]).astype(BF16)
-    for copy in copies[7:]:
-        copy.wait()
     counts = degree[...].astype(F32)
     inverse[...] = 1.0 / jnp.broadcast_to(counts, (nodes, nodes)).T
     counts = jnp.sum(own.astype(F32) * counts, axis=1, keepdims=True)
     known[:, width:] = jnp.broadcast_to(counts, (slots, 128)).astype(BF16)
+    for copy in copies[3:]:
+        copy.wait()
+    for k in range(tiles.shape[2]):
+
+        @pl.when(k < count[0, 0])
+        def _():
+            down = pl.multiple_of(swap_bits(dst[0, 0, k] ^ col) * nodes, nodes)
+            adjacency[src[0, 0, k] ^ row, pl.ds(down, nodes), :] = tiles[0, 0, k]
+
+    for s in range(rows):
+        block = dot(picks[...], adjacency[s]).astype(BF16)
+        (far if s // 2 else near)[s % 2 * slots : (s % 2 + 1) * slots, :] = block
 
 
 def block_of(step, near, far, slots):
-    index = list(CFG["halves"]).index(step)
-    return (far if index // 2 else near)[index % 2 * slots : (index % 2 + 1) * slots, :]
+    return (far if step // 2 else near)[step % 2 * slots : (step % 2 + 1) * slots, :]
 
 
 def dense_part(steps, adjacency, *refs):
@@ -133,17 +133,11 @@
     sent[...] = total[half:].astype(BF16)
 
 
-def begin(step, column_picks, features, near, far, total, chosen):
-    slots, nodes = column_picks.shape[0], features.shape[0]
-    total[...] = dot(block_of(step, near, far, slots), features[...])
-    chosen[...] = dot(column_picks[:, step * nodes : (step + 1) * nodes], features[...])
-
-
 def combine(steps, column_picks, known, *refs):
-    features, (near, far, *first, sent, part, fixed) = refs[: len(steps)], refs[len(steps) :]
+    features, (near, far, sent, part, fixed) = refs[: len(steps)], refs[len(steps) :]
     nodes, width = features[0].shape
     half = part.shape[0]
-    sums, picked = [x[...] for x in first] or [0.0, 0.0]
+    sums, picked = 0.0, 0.0
     for step, block in zip(steps, features):
         sums += dot(block_of(step, near, far, 2 * half), block[...])
         picked += dot(column_picks[:, step * nodes : (step + 1) * nodes], block[...])
@@ -258,13 +252,11 @@
     share = slots // cols
     half = slots // 2
 
-    tie = lax.optimization_barrier
-    feature_parts = spread(features, "row", CFG["forder"])
-    steps = tuple(feature_parts)
-    feature_parts[0] = features
+    order = (3, 1, 2)
+    feature_parts = spread(features, "row", order)
 
     bias = layer_bias.reshape(1, width)
-    adjacency, column_picks, own_picks, known, near, far, inverse, w_self, w_neigh, bias = call(
+    adjacency, column_picks, own_picks, known, near, far, inverse, *resident = call(
         functools.partial(select, rows, cols),
         [
             ((rows, cols * nodes, nodes), BF16),
@@ -275,7 +267,7 @@
         + [((rows // 2 * slots, nodes), BF16)] * 2
         + [((nodes, nodes), F32)]
         + [((width, width), BF16)] * 2
-        + [((1, width), F32)],
+        + [((1, width), F32), ((nodes, width), BF16)],
         target_ids.reshape(1, slots),
         tile_src,
         tile_dst,
@@ -286,33 +278,24 @@
         w_self,
         w_neigh,
         bias,
-        spaces=[pltpu.HBM] * 3 + [pl.ANY] + [pltpu.HBM] * 6,
+        features,
+        spaces=[pltpu.HBM] * 3 + [pl.ANY] + [pltpu.HBM] * 7,
         scratch=[pltpu.VMEM((slots, cols * nodes), BF16)]
         + [pltpu.SMEM(x.shape, x.dtype) for x in (tile_src, tile_dst, tile_count)]
         + [pltpu.VMEM(x.shape, x.dtype) for x in (tile_vals, cotangent)]
         + [pltpu.VMEM((1, nodes), jnp.int32), pltpu.VMEM((1, slots), jnp.int32)]
-        + [pltpu.SemaphoreType.DMA((10,))],
-    )
-    first = ()
-    if CFG["split"]:
-        first = call(
-            functools.partial(begin, steps[0]),
-            [((slots, width), F32)] * 2,
-            column_picks,
-            feature_parts[steps[0]],
-            near,
-            far,
-        )
-    later = steps[len(first) // 2 :] + (0,)
+        + [pltpu.SemaphoreType.DMA((11,))],
+    )
+    w_self, w_neigh, bias, features = resident
+    feature_parts[0] = features
     sent, part, fixed = call(
-        functools.partial(combine, later),
+        functools.partial(combine, order + (0,)),
         [((half, 3 * width + 128), BF16), ((half, width), F32), ((half, 2 * width + 128), BF16)],
         column_picks,
         known,
-        *[feature_parts[step] for step in later],
+        *[feature_parts[step] for step in order + (0,)],
         near,
         far,
-        *first,
     )
     got = trade(sent, "col", 1)
     sent, part, fixed = call(
@@ -322,10 +305,6 @@
         fixed,
         got,
     )
-    if CFG["a1"] == "sent":
-        sent, far = tie((sent, far))
-    if CFG["dd"] == "sent":
-        sent, feature_parts = tie((sent, feature_parts))
     got = trade(sent, "col", 2)
     found, feature_slots = call(
         slopes,
@@ -337,58 +316,27 @@
         w_neigh,
         bias,
     )
-    if CFG["a1"] == "found":
-        found, far = tie((found, far))
-    if CFG["dd"] == "found":
-        found, feature_parts = tie((found, feature_parts))
-    near_step, far_step = CFG["halves"][1], CFG["halves"][2]
-    columns = near + trade(far, "row", far_step)
-    if CFG["a2"] == "found":
-        found, columns = tie((found, columns))
-
-    def prepare_dense(feature_parts):
-        kept, dense = call(
-            functools.partial(dense_part, steps + (0,)),
-            [((2 * nodes, width), F32), ((2 * nodes, width), BF16)],
-            adjacency,
-            *[feature_parts[step] for step in steps + (0,)],
-            cost=CFG["cd"],
-        )
-        return kept + trade(dense, "col", 1).astype(F32)
-
-    dense = prepare_dense(feature_parts)
-    parts = spread(found, "row", CFG["p3"]) if CFG["p3d"] else None
-    if CFG["p3d"]:
-        if CFG["p3split"]:
-            (found,) = call(merge, [(found.shape, BF16)], parts.pop(CFG["p3"][0]), found)
-    else:
-        (found,) = call(merge, [(found.shape, BF16)], trade(found, "row", CFG["p3"][0]), found)
-    if CFG["a2"] == "found1":
-        found, columns = tie((found, columns))
-    if CFG["fp"] == "found1":
-        found, feature_slots = tie((found, feature_slots))
-    if CFG["dx"] == "found1":
-        found, dense = tie((found, dense))
-    if CFG["p3d"]:
-        (found,) = call(merge, [(found.shape, BF16)], *parts.values(), found)
-    else:
-        (found,) = call(merge, [(found.shape, BF16)], trade(found, "row", CFG["p3"][1]), found)
-    if CFG["dx"] == "merged":
-        found, dense = tie((found, dense))
-    own_columns = columns[:slots] + trade(columns[slots:], "row", near_step)
+    columns = near + trade(far, "row", 2)
+    found, columns = lax.optimization_barrier((found, columns))
+    dense, dense_sent = call(
+        functools.partial(dense_part, order + (0,)),
+        [((2 * nodes, width), F32), ((2 * nodes, width), BF16)],
+        adjacency,
+        *[feature_parts[step] for step in order + (0,)],
+        cost=DENSE_COST,
+    )
+    dense = dense + trade(dense_sent, "col", 1).astype(F32)
+    parts = spread(found, "row", order)
+    (found,) = call(merge, [(found.shape, BF16)], parts.pop(order[0]), found, cost=MERGE_COST)
+    found, feature_slots = lax.optimization_barrier((found, feature_slots))
+    found, dense = lax.optimization_barrier((found, dense))
+    (found,) = call(merge, [(found.shape, BF16)], *parts.values(), found, cost=MERGE_COST)
+    own_columns = columns[:slots] + trade(columns[slots:], "row", 1)
     dense_got = trade(dense[nodes:].astype(BF16), "col", 2)
-    if CFG["fp"] != "none":
-        feature_mine = jnp.concatenate([feature_slots, trade(feature_slots, "col", 2)], axis=0)
-        feature_other = trade(feature_mine, "col", 1)
-        everything = found
-    else:
-        everything = jnp.concatenate([found, feature_slots], axis=1)
-    found_mine = jnp.concatenate([everything, trade(everything, "col", 2)], axis=0)
-    if CFG["hid"] == "mine":
-        found_mine, dense_got = tie((found_mine, dense_got))
+    feature_mine = jnp.concatenate([feature_slots, trade(feature_slots, "col", 2)], axis=0)
+    feature_other = trade(feature_mine, "col", 1)
+    found_mine = jnp.concatenate([found, trade(found, "col", 2)], axis=0)
     found_other = trade(found_mine, "col", 1)
-    if CFG["fp"] == "none":
-        feature_mine, feature_other = found_mine[:, -width:], found_other[:, -width:]
     (hidden,) = call(
         activate,
         [((nodes, width), BF16)],
@@ -558,8 +506,12 @@
         P("groups", None),
         P("groups"),
     )
-    parts = mesh.shape["row"] * mesh.shape["col"]
-    per_device = compact_device if parts <= 16 else dense_device
+    four = mesh.shape["row"] == 4 and mesh.shape["col"] == 4
+
+    def per_device(*args):
+        tiles_are_owned_blocks = args[0].shape[0] == args[4].shape[-1] == 128
+        return (compact_device if four and tiles_are_owned_blocks else dense_device)(*args)
+
     return jax.shard_map(
         per_device, mesh=mesh, in_specs=in_specs, out_specs=out_specs, check_vma=False
     )

time: 36.4 us -> 35.5 us (0.975)
  starting transfers between devices: 21.3 us -> 19.4 us
  waiting for transfers between devices: 8.01 us -> 9.3 us
    ppermute x16, starting transfers between devices: 21.3 us -> 19.4 us  [trade(): lax.ppermute(block, axis, [(i, i ^ step) for i in range(lax.axis_size(axi...]
    ppermute x16, waiting for transfers between devices: 8.01 us -> 9.3 us  [trade(): lax.ppermute(block, axis, [(i, i ^ step) for i in range(lax.axis_size(axi...]
  transfers between devices with their start and end apart: 16 -> 16, of which waited for: 7 -> 8; matrix products, arithmetic and copies ran while one was open for 0% -> 0% of each run, Pallas kernels for 11% -> 11%
where the time goes in v6:
time: 35.5 us; the launch traced here: 35.3 us
  starting transfers between devices  19.4 us (55%)
  waiting for transfers between devices  9.3 us (26%)
  Pallas kernels  5.07 us (14%)
  between operations  1.41 us (4%)
    ppermute x16, starting transfers between devices, trade(): lax.ppermute(block, axis, [(i, i ^ step) for i in range(lax.axis_size(axi...  19.4 us
    ppermute x16, waiting for transfers between devices, trade(): lax.ppermute(block, axis, [(i, i ^ step) for i in range(lax.axis_size(axi...  9.3 us
    pallas_call x9, Pallas kernels, call(): pl.pallas_call(kernel, out_shape=[jax.ShapeDtypeStruct(shape, dtype) for...  5.07 us
  transfers between devices with their start and end apart: 16, of which 8 were waited for; matrix products, arithmetic and copies ran while one was open for 0% of the time, Pallas kernels for 11%

profile of v6, /device:TPU:0, one launch (start us, length us, event | category | flops | bytes accessed | tf_op | source)
XLA Modules:
  0.0 35.3 jit_solution(2845416244385164227)
XLA Ops:
  0.6 5.1 %collective-permute-start = (bf16[128,256]{1,0:T(8,128)(2,1)}, bf16[128,256]{1,0:T(8,128)(2,1)S(1)}, u32[]{:S(2)}, u32[]{:S(2)}) collective-permute-start(bf16[128,256]{1,0:T(8,128)(2,1)} %refs_3_.1), channel_id=1, source_target_pairs={{0,12},{4,8},{8,4},{12,0},{1,13},{5,9},{9,5},{13,1},{2,14},{6,10},... | collective-permute-start | bytes 196616 | tf_op jit(solution)/shard_map/ppermute | solution.py:32
  5.8 0.0 collective-permute-start.2
  5.8 0.6 %collective-permute-start.1 = (bf16[128,256]{1,0:T(8,128)(2,1)}, bf16[128,256]{1,0:T(8,128)(2,1)S(1)}, u32[]{:S(2)}, u32[]{:S(2)}) collective-permute-start(bf16[128,256]{1,0:T(8,128)(2,1)} %refs_3_.1), channel_id=1, source_target_pairs={{0,4},{4,0},{8,12},{12,8},{1,5},{5,1},{9,13},{13,9},{2,6},{6,2},{1... | collective-permute-start | bytes 196616 | tf_op jit(solution)/shard_map/ppermute | solution.py:32
  7.0 1.8 %shard_map.146 = (bf16[4,512,128]{2,1,0:T(8,128)(2,1)S(1)}, bf16[256,512]{1,0:T(8,128)(2,1)S(1)}, bf16[128,256]{1,0:T(8,128)(2,1)S(1)}, bf16[256,384]{1,0:T(8,12...) custom-call(s32[1,256]{1,0:T(1,128)} %bitcast.4, ...), custom_call_target="tpu_custom_call" | custom-call | tf_op jit(solution)/shard_map/pallas_call | solution.py:56
  8.9 2.4 %collective-permute-start.5 = (bf16[512,128]{1,0:T(8,128)(2,1)S(1)}, bf16[512,128]{1,0:T(8,128)(2,1)S(1)}, u32[]{:S(2)}, u32[]{:S(2)}) collective-permute-start(bf16[512,128]{1,0:T(8,128)(2,1)S(1)} %get-tuple-element.40.refs_5_), channel_id=1, source_target_pairs={{0,8},{4,12},{8,0},{12,4},{1,9},{5,13},{9,1},{13,5},{2,10},{6,14},... | collective-permute-start | bytes 393224 | tf_op jit(solution)/shard_map/ppermute | solution.py:32
  11.2 0.0 collective-permute-done.refs_0_
  11.2 0.3 collective-permute-done.2.refs_2_
  11.6 0.0 collective-permute-done.1.refs_1_
  11.6 0.4 %shard_map.147 = (bf16[128,896]{1,0:T(8,128)(2,1)S(1)}, f32[128,256]{1,0:T(8,128)S(1)}, bf16[128,640]{1,0:T(8,128)(2,1)S(1)}) custom-call(bf16[256,512]{1,0:T(8,128)(2,1)S(1)} %get-tuple-element.37.column_picks, bf16[256,384]{1,0:T(8,128)(2,1)S(1)} %get-tuple-element.38.known, bf16[128,256]{1,0:T(8,128)(2,1)S(1)} %collective-permute-done.refs_0_, ...), custom_call_target="tpu_custom_call" | custom-call | tf_op jit(solution)/shard_map/pallas_call | solution.py:56
  12.0 0.1 collective-permute-start.3
  12.1 0.4 %shard_map.151 = (f32[256,256]{1,0:T(8,128)S(1)}, bf16[256,256]{1,0:T(8,128)(2,1)S(1)}) custom-call(bf16[4,512,128]{2,1,0:T(8,128)(2,1)S(1)} %get-tuple-element.54.adjacency, bf16[128,256]{1,0:T(8,128)(2,1)S(1)} %collective-permute-done.refs_0_, bf16[128,256]{1,0:T(8,128)(2,1)S(1)} %collective-permute-done.1.refs_1_, ...), custom_call_target="tpu_custom_call" | custom-call | flops 3000000000 | tf_op jit(solution)/shard_map/pallas_call | solution.py:56
  12.5 0.6 %collective-permute-start.7 = (bf16[256,256]{1,0:T(8,128)(2,1)S(1)}, bf16[256,256]{1,0:T(8,128)(2,1)S(1)}, u32[]{:S(2)}, u32[]{:S(2)}) collective-permute-start(bf16[256,256]{1,0:T(8,128)(2,1)S(1)} %get-tuple-element.56), channel_id=1, source_target_pairs={{0,1},{1,0},{2,3},{3,2},{4,5},{5,4},{6,7},{7,6},{8,9},{9,8},{10,11... | collective-permute-start | bytes 393224 | tf_op jit(solution)/shard_map/ppermute | solution.py:32
  13.1 0.5 %collective-permute-done.3.got = bf16[128,896]{1,0:T(8,128)(2,1)S(1)} collective-permute-done((bf16[128,896]{1,0:T(8,128)(2,1)S(1)}, bf16[128,896]{1,0:T(8,128)(2,1)S(1)}, u32[]{:S(2)}, u32[]{:S(2)}) %collective-permute-start.3) | collective-permute-done | bytes 229408 | tf_op jit(solution)/shard_map/ppermute | solution.py:32
  13.6 1.6 %collective-permute-start.4 = (bf16[64,896]{1,0:T(8,128)(2,1)S(1)}, bf16[64,896]{1,0:T(8,128)(2,1)S(1)}, u32[]{:S(2)}, u32[]{:S(2)}) collective-permute-start(bf16[64,896]{1,0:T(8,128)(2,1)S(1)} %get-tuple-element.46), channel_id=1, source_target_pairs={{0,2},{1,3},{2,0},{3,1},{4,6},{5,7},{6,4},{7,5},{8,10},{9,11},{10,... | collective-permute-start | bytes 344072 | tf_op jit(solution)/shard_map/ppermute | solution.py:32
  15.1 2.2 %collective-permute-done.5 = bf16[512,128]{1,0:T(8,128)(2,1)S(1)} collective-permute-done((bf16[512,128]{1,0:T(8,128)(2,1)S(1)}, bf16[512,128]{1,0:T(8,128)(2,1)S(1)}, u32[]{:S(2)}, u32[]{:S(2)}) %collective-permute-start.5) | collective-permute-done | bytes 131104 | tf_op jit(solution)/shard_map/ppermute | solution.py:32
  17.4 1.4 %collective-permute-done.4.got = bf16[64,896]{1,0:T(8,128)(2,1)S(1)} collective-permute-done((bf16[64,896]{1,0:T(8,128)(2,1)S(1)}, bf16[64,896]{1,0:T(8,128)(2,1)S(1)}, u32[]{:S(2)}, u32[]{:S(2)}) %collective-permute-start.4) | collective-permute-done | bytes 114720 | tf_op jit(solution)/shard_map/ppermute | solution.py:32
  18.8 0.2 shard_map.149
  19.1 2.8 %collective-permute-start.6 = (bf16[272,128]{1,0:T(8,128)(2,1)S(1)}, bf16[272,128]{1,0:T(8,128)(2,1)S(1)}, u32[]{:S(2)}, u32[]{:S(2)}) collective-permute-start(bf16[272,128]{1,0:T(8,128)(2,1)S(1)} %get-tuple-element.51.refs_1_), channel_id=1, source_target_pairs={{0,12},{4,8},{8,4},{12,0},{1,13},{5,9},{9,5},{13,1},{2,14},{6,10},... | collective-permute-start | bytes 208904 | tf_op jit(solution)/shard_map/ppermute | solution.py:32
  21.9 0.0 collective-permute-done.7
  21.9 0.5 %collective-permute-start.10 = (bf16[272,128]{1,0:T(8,128)(2,1)S(1)}, bf16[272,128]{1,0:T(8,128)(2,1)S(1)}, u32[]{:S(2)}, u32[]{:S(2)}) collective-permute-start(bf16[272,128]{1,0:T(8,128)(2,1)S(1)} %get-tuple-element.51.refs_1_), channel_id=1, source_target_pairs={{0,8},{4,12},{8,0},{12,4},{1,9},{5,13},{9,1},{13,5},{2,10},{6,14},... | collective-permute-start | bytes 208904 | tf_op jit(solution)/shard_map/ppermute | solution.py:32
  22.4 1.2 %collective-permute-start.9 = (bf16[272,128]{1,0:T(8,128)(2,1)S(1)}, bf16[272,128]{1,0:T(8,128)(2,1)S(1)}, u32[]{:S(2)}, u32[]{:S(2)}) collective-permute-start(bf16[272,128]{1,0:T(8,128)(2,1)S(1)} %get-tuple-element.51.refs_1_), channel_id=1, source_target_pairs={{0,4},{4,0},{8,12},{12,8},{1,5},{5,1},{9,13},{13,9},{2,6},{6,2},{1... | collective-permute-start | bytes 208904 | tf_op jit(solution)/shard_map/ppermute | solution.py:32
  23.6 0.8 %collective-permute-start.15 = (bf16[256,128]{1,0:T(8,128)(2,1)S(1)}, bf16[256,128]{1,0:T(8,128)(2,1)S(1)}, u32[]{:S(2)}, u32[]{:S(2)}) collective-permute-start(bf16[256,128]{1,0:T(8,128)(2,1)S(1)} %slice.16), channel_id=1, source_target_pairs={{0,4},{4,0},{8,12},{12,8},{1,5},{5,1},{9,13},{13,9},{2,6},{6,2},{1... | collective-permute-start | bytes 196616 | tf_op jit(solution)/shard_map/ppermute | solution.py:32
  24.5 0.9 %collective-permute-done.6.refs_0_ = bf16[272,128]{1,0:T(8,128)(2,1)S(1)} collective-permute-done((bf16[272,128]{1,0:T(8,128)(2,1)S(1)}, bf16[272,128]{1,0:T(8,128)(2,1)S(1)}, u32[]{:S(2)}, u32[]{:S(2)}) %collective-permute-start.6) | collective-permute-done | bytes 69664 | tf_op jit(solution)/shard_map/ppermute | solution.py:32
  25.4 1.5 %collective-permute-start.13 = (bf16[64,256]{1,0:T(8,128)(2,1)S(1)}, bf16[64,256]{1,0:T(8,128)(2,1)S(1)}, u32[]{:S(2)}, u32[]{:S(2)}) collective-permute-start(bf16[64,256]{1,0:T(8,128)(2,1)S(1)} %get-tuple-element.60), channel_id=1, source_target_pairs={{0,2},{1,3},{2,0},{3,1},{4,6},{5,7},{6,4},{7,5},{8,10},{9,11},{10,... | collective-permute-start | bytes 98312 | tf_op jit(solution)/shard_map/ppermute | solution.py:32
  26.9 0.6 %collective-permute-start.8 = (bf16[128,256]{1,0:T(8,128)(2,1)S(1)}, bf16[128,256]{1,0:T(8,128)(2,1)S(1)}, u32[]{:S(2)}, u32[]{:S(2)}) collective-permute-start(bf16[128,256]{1,0:T(8,128)(2,1)S(1)} %slice.20), channel_id=1, source_target_pairs={{0,2},{1,3},{2,0},{3,1},{4,6},{5,7},{6,4},{7,5},{8,10},{9,11},{10,... | collective-permute-start | bytes 196616 | tf_op jit(solution)/shard_map/ppermute | solution.py:32
  27.5 0.7 %collective-permute-done.10.refs_1_ = bf16[272,128]{1,0:T(8,128)(2,1)S(1)} collective-permute-done((bf16[272,128]{1,0:T(8,128)(2,1)S(1)}, bf16[272,128]{1,0:T(8,128)(2,1)S(1)}, u32[]{:S(2)}, u32[]{:S(2)}) %collective-permute-start.10) | collective-permute-done | bytes 69664 | tf_op jit(solution)/shard_map/ppermute | solution.py:32
  28.2 0.0 collective-permute-done.9.refs_0_
  28.3 1.5 %collective-permute-start.11 = (bf16[272,128]{1,0:T(8,128)(2,1)S(1)}, bf16[272,128]{1,0:T(8,128)(2,1)S(1)}, u32[]{:S(2)}, u32[]{:S(2)}) collective-permute-start(bf16[272,128]{1,0:T(8,128)(2,1)S(1)} %shard_map.153), channel_id=1, source_target_pairs={{0,2},{1,3},{2,0},{3,1},{4,6},{5,7},{6,4},{7,5},{8,10},{9,11},{10,... | collective-permute-start | bytes 208904 | tf_op jit(solution)/shard_map/ppermute | solution.py:32
  29.8 0.0 collective-permute-done.13
  29.8 0.0 collective-permute-start.14
  29.8 2.8 %collective-permute-done.11 = bf16[272,128]{1,0:T(8,128)(2,1)S(1)} collective-permute-done((bf16[272,128]{1,0:T(8,128)(2,1)S(1)}, bf16[272,128]{1,0:T(8,128)(2,1)S(1)}, u32[]{:S(2)}, u32[]{:S(2)}) %collective-permute-start.11) | collective-permute-done | bytes 69664 | tf_op jit(solution)/shard_map/ppermute | solution.py:32
  32.7 0.1 collective-permute-start.12
  32.7 0.0 collective-permute-done.15
  32.8 0.0 collective-permute-done.8.got
  32.8 0.9 %shard_map.152 = bf16[128,256]{1,0:T(8,128)(2,1)} custom-call(bf16[128,256]{1,0:T(8,128)(2,1)S(1)} %get-tuple-element.36.refs_3_.features, f32[128,256]{1,0:T(8,128)S(1)} %slice.13.total, bf16[128,256]{1,0:T(8,128)(2,1)S(1)} %collective-permute-done.8.got, f32[128,128]{1,0:T(8,128)S(1)} %get-tuple-element.58.inverse, ...), custom_call_target="tpu_custom_call" | custom-call | tf_op jit(solution)/shard_map/pallas_call | solution.py:56
  33.7 0.0 collective-permute-done.14.refs_3_
  33.7 0.4 %collective-permute-done.12.refs_1_ = bf16[544,128]{1,0:T(8,128)(2,1)S(1)} collective-permute-done((bf16[544,128]{1,0:T(8,128)(2,1)S(1)}, bf16[544,128]{1,0:T(8,128)(2,1)S(1)}, u32[]{:S(2)}, u32[]{:S(2)}) %collective-permute-start.12) | collective-permute-done | bytes 139296 | tf_op jit(solution)/shard_map/ppermute | solution.py:32
  34.1 1.2 %shard_map.154 = (bf16[128,256]{1,0:T(8,128)(2,1)}, f32[256,256]{1,0:T(8,128)}, f32[256,256]{1,0:T(8,128)}, f32[1,256]{1,0:T(1,128)}) custom-call(bf16[544,128]{1,0:T(8,128)(2,1)S(1)} %pad_maximum_fusion.refs_0_, bf16[544,128]{1,0:T(8,128)(2,1)S(1)} %collective-permute-done.12.refs_1_, bf16[128,256]{1,0:T(8,128)(2,1)S(1)} %constant_dynamic-update-slice_fusion.refs_2_, ...), custom_call_target="tpu_custom_call" | custom-call | tf_op jit(solution)/shard_map/pallas_call | solution.py:56
  (12 shorter events, 0.2 us)
Async XLA Ops:
  0.6 10.6 %collective-permute-start = (bf16[128,256]{1,0:T(8,128)(2,1)}, bf16[128,256]{1,0:T(8,128)(2,1)S(1)}, u32[]{:S(2)}, u32[]{:S(2)}) collective-permute-start(bf16[128,256]{1,0:T(8,128)(2,1)} %refs_3_.1), channel_id=1, source_target_pairs={{0,12},{4,8},{8,4},{12,0},{1,13},{5,9},{9,5},{13,1},{2,14},{6,10},... | collective-permute-start | bytes 196616 | tf_op jit(solution)/shard_map/ppermute | solution.py:32
  5.8 5.8 %collective-permute-start.2 = (bf16[128,256]{1,0:T(8,128)(2,1)}, bf16[128,256]{1,0:T(8,128)(2,1)S(1)}, u32[]{:S(2)}, u32[]{:S(2)}) collective-permute-start(bf16[128,256]{1,0:T(8,128)(2,1)} %refs_3_.1), channel_id=1, source_target_pairs={{0,8},{4,12},{8,0},{12,4},{1,9},{5,13},{9,1},{13,5},{2,10},{6,14},... | collective-permute-start | bytes 196616 | tf_op jit(solution)/shard_map/ppermute | solution.py:32
  5.8 5.8 %collective-permute-start.1 = (bf16[128,256]{1,0:T(8,128)(2,1)}, bf16[128,256]{1,0:T(8,128)(2,1)S(1)}, u32[]{:S(2)}, u32[]{:S(2)}) collective-permute-start(bf16[128,256]{1,0:T(8,128)(2,1)} %refs_3_.1), channel_id=1, source_target_pairs={{0,4},{4,0},{8,12},{12,8},{1,5},{5,1},{9,13},{13,9},{2,6},{6,2},{1... | collective-permute-start | bytes 196616 | tf_op jit(solution)/shard_map/ppermute | solution.py:32
  8.9 8.5 %collective-permute-start.5 = (bf16[512,128]{1,0:T(8,128)(2,1)S(1)}, bf16[512,128]{1,0:T(8,128)(2,1)S(1)}, u32[]{:S(2)}, u32[]{:S(2)}) collective-permute-start(bf16[512,128]{1,0:T(8,128)(2,1)S(1)} %get-tuple-element.40.refs_5_), channel_id=1, source_target_pairs={{0,8},{4,12},{8,0},{12,4},{1,9},{5,13},{9,1},{13,5},{2,10},{6,14},... | collective-permute-start | bytes 393224 | tf_op jit(solution)/shard_map/ppermute | solution.py:32
  12.0 1.6 %collective-permute-start.3 = (bf16[128,896]{1,0:T(8,128)(2,1)S(1)}, bf16[128,896]{1,0:T(8,128)(2,1)S(1)}, u32[]{:S(2)}, u32[]{:S(2)}) collective-permute-start(bf16[128,896]{1,0:T(8,128)(2,1)S(1)} %get-tuple-element.43), channel_id=1, source_target_pairs={{0,1},{1,0},{2,3},{3,2},{4,5},{5,4},{6,7},{7,6},{8,9},{9,8},{10,11... | collective-permute-start | bytes 688136 | tf_op jit(solution)/shard_map/ppermute | solution.py:32
  12.5 9.4 %collective-permute-start.7 = (bf16[256,256]{1,0:T(8,128)(2,1)S(1)}, bf16[256,256]{1,0:T(8,128)(2,1)S(1)}, u32[]{:S(2)}, u32[]{:S(2)}) collective-permute-start(bf16[256,256]{1,0:T(8,128)(2,1)S(1)} %get-tuple-element.56), channel_id=1, source_target_pairs={{0,1},{1,0},{2,3},{3,2},{4,5},{5,4},{6,7},{7,6},{8,9},{9,8},{10,11... | collective-permute-start | bytes 393224 | tf_op jit(solution)/shard_map/ppermute | solution.py:32
  13.6 5.3 %collective-permute-start.4 = (bf16[64,896]{1,0:T(8,128)(2,1)S(1)}, bf16[64,896]{1,0:T(8,128)(2,1)S(1)}, u32[]{:S(2)}, u32[]{:S(2)}) collective-permute-start(bf16[64,896]{1,0:T(8,128)(2,1)S(1)} %get-tuple-element.46), channel_id=1, source_target_pairs={{0,2},{1,3},{2,0},{3,1},{4,6},{5,7},{6,4},{7,5},{8,10},{9,11},{10,... | collective-permute-start | bytes 344072 | tf_op jit(solution)/shard_map/ppermute | solution.py:32
  19.1 6.2 %collective-permute-start.6 = (bf16[272,128]{1,0:T(8,128)(2,1)S(1)}, bf16[272,128]{1,0:T(8,128)(2,1)S(1)}, u32[]{:S(2)}, u32[]{:S(2)}) collective-permute-start(bf16[272,128]{1,0:T(8,128)(2,1)S(1)} %get-tuple-element.51.refs_1_), channel_id=1, source_target_pairs={{0,12},{4,8},{8,4},{12,0},{1,13},{5,9},{9,5},{13,1},{2,14},{6,10},... | collective-permute-start | bytes 208904 | tf_op jit(solution)/shard_map/ppermute | solution.py:32
  21.9 6.3 %collective-permute-start.10 = (bf16[272,128]{1,0:T(8,128)(2,1)S(1)}, bf16[272,128]{1,0:T(8,128)(2,1)S(1)}, u32[]{:S(2)}, u32[]{:S(2)}) collective-permute-start(bf16[272,128]{1,0:T(8,128)(2,1)S(1)} %get-tuple-element.51.refs_1_), channel_id=1, source_target_pairs={{0,8},{4,12},{8,0},{12,4},{1,9},{5,13},{9,1},{13,5},{2,10},{6,14},... | collective-permute-start | bytes 208904 | tf_op jit(solution)/shard_map/ppermute | solution.py:32
  22.4 5.8 %collective-permute-start.9 = (bf16[272,128]{1,0:T(8,128)(2,1)S(1)}, bf16[272,128]{1,0:T(8,128)(2,1)S(1)}, u32[]{:S(2)}, u32[]{:S(2)}) collective-permute-start(bf16[272,128]{1,0:T(8,128)(2,1)S(1)} %get-tuple-element.51.refs_1_), channel_id=1, source_target_pairs={{0,4},{4,0},{8,12},{12,8},{1,5},{5,1},{9,13},{13,9},{2,6},{6,2},{1... | collective-permute-start | bytes 208904 | tf_op jit(solution)/shard_map/ppermute | solution.py:32
  23.6 9.1 %collective-permute-start.15 = (bf16[256,128]{1,0:T(8,128)(2,1)S(1)}, bf16[256,128]{1,0:T(8,128)(2,1)S(1)}, u32[]{:S(2)}, u32[]{:S(2)}) collective-permute-start(bf16[256,128]{1,0:T(8,128)(2,1)S(1)} %slice.16), channel_id=1, source_target_pairs={{0,4},{4,0},{8,12},{12,8},{1,5},{5,1},{9,13},{13,9},{2,6},{6,2},{1... | collective-permute-start | bytes 196616 | tf_op jit(solution)/shard_map/ppermute | solution.py:32
  25.4 4.4 %collective-permute-start.13 = (bf16[64,256]{1,0:T(8,128)(2,1)S(1)}, bf16[64,256]{1,0:T(8,128)(2,1)S(1)}, u32[]{:S(2)}, u32[]{:S(2)}) collective-permute-start(bf16[64,256]{1,0:T(8,128)(2,1)S(1)} %get-tuple-element.60), channel_id=1, source_target_pairs={{0,2},{1,3},{2,0},{3,1},{4,6},{5,7},{6,4},{7,5},{8,10},{9,11},{10,... | collective-permute-start | bytes 98312 | tf_op jit(solution)/shard_map/ppermute | solution.py:32
  26.9 5.9 %collective-permute-start.8 = (bf16[128,256]{1,0:T(8,128)(2,1)S(1)}, bf16[128,256]{1,0:T(8,128)(2,1)S(1)}, u32[]{:S(2)}, u32[]{:S(2)}) collective-permute-start(bf16[128,256]{1,0:T(8,128)(2,1)S(1)} %slice.20), channel_id=1, source_target_pairs={{0,2},{1,3},{2,0},{3,1},{4,6},{5,7},{6,4},{7,5},{8,10},{9,11},{10,... | collective-permute-start | bytes 196616 | tf_op jit(solution)/shard_map/ppermute | solution.py:32
  28.3 4.4 %collective-permute-start.11 = (bf16[272,128]{1,0:T(8,128)(2,1)S(1)}, bf16[272,128]{1,0:T(8,128)(2,1)S(1)}, u32[]{:S(2)}, u32[]{:S(2)}) collective-permute-start(bf16[272,128]{1,0:T(8,128)(2,1)S(1)} %shard_map.153), channel_id=1, source_target_pairs={{0,2},{1,3},{2,0},{3,1},{4,6},{5,7},{6,4},{7,5},{8,10},{9,11},{10,... | collective-permute-start | bytes 208904 | tf_op jit(solution)/shard_map/ppermute | solution.py:32
  29.8 3.9 %collective-permute-start.14 = (bf16[128,256]{1,0:T(8,128)(2,1)S(1)}, bf16[128,256]{1,0:T(8,128)(2,1)S(1)}, u32[]{:S(2)}, u32[]{:S(2)}) collective-permute-start(bf16[128,256]{1,0:T(8,128)(2,1)S(1)} %constant_dynamic-update-slice_fusion.refs_2_), channel_id=1, source_target_pairs={{0,1},{1,0},{2,3},{3,2},{4,5},{5,4},{6,7},{7,6},{8,9},{9,8},{10,11... | collective-permute-start | bytes 196616 | tf_op jit(solution)/shard_map/ppermute | solution.py:32
  32.7 1.4 %collective-permute-start.12 = (bf16[544,128]{1,0:T(8,128)(2,1)S(1)}, bf16[544,128]{1,0:T(8,128)(2,1)S(1)}, u32[]{:S(2)}, u32[]{:S(2)}) collective-permute-start(bf16[544,128]{1,0:T(8,128)(2,1)S(1)} %pad_maximum_fusion.refs_0_), channel_id=1, source_target_pairs={{0,1},{1,0},{2,3},{3,2},{4,5},{5,4},{6,7},{7,6},{8,9},{9,8},{10,11... | collective-permute-start | bytes 417800 | tf_op jit(solution)/shard_map/ppermute | solution.py:32

commit v7 on v6

--- a/solution.py
+++ b/solution.py
@@ -114,10 +114,12 @@
         @pl.when(k < count[0, 0])
         def _():
             down = pl.multiple_of(swap_bits(dst[0, 0, k] ^ col) * nodes, nodes)
-            adjacency[src[0, 0, k] ^ row, pl.ds(down, nodes), :] = tiles[0, 0, k]
-
+            across = pl.multiple_of((src[0, 0, k] ^ row) * nodes, nodes)
+            adjacency[pl.ds(down, nodes), pl.ds(across, nodes)] = tiles[0, 0, k]
+
+    picked = dot(picks[...], adjacency[...]).astype(BF16)
     for s in range(rows):
-        block = dot(picks[...], adjacency[s]).astype(BF16)
+        block = picked[:, s * nodes : (s + 1) * nodes]
         (far if s // 2 else near)[s % 2 * slots : (s % 2 + 1) * slots, :] = block
 
 
@@ -127,7 +129,11 @@
 
 def dense_part(steps, adjacency, *refs):
     *features, kept, sent = refs
-    total = sum(dot(adjacency[step], block[...]) for step, block in zip(steps, features))
+    nodes = features[0].shape[0]
+    total = sum(
+        dot(adjacency[:, step * nodes : (step + 1) * nodes], block[...])
+        for step, block in zip(steps, features)
+    )
     half = kept.shape[0]
     kept[...] = total[:half]
     sent[...] = total[half:].astype(BF16)
@@ -259,7 +265,7 @@
     adjacency, column_picks, own_picks, known, near, far, inverse, *resident = call(
         functools.partial(select, rows, cols),
         [
-            ((rows, cols * nodes, nodes), BF16),
+            ((cols * nodes, rows * nodes), BF16),
             ((slots, rows * nodes), BF16),
             ((nodes, slots), BF16),
             ((slots, width + 128), BF16),

time: 35.5 us -> 35.4 us (level)
  transfers between devices with their start and end apart: 16 -> 16, of which waited for: 8 -> 9; matrix products, arithmetic and copies ran while one was open for 0% -> 0% of each run, Pallas kernels for 11% -> 11%
where the time goes in v7:
time: 35.4 us; the launch traced here: 35.2 us
  starting transfers between devices  19.3 us (55%)
  waiting for transfers between devices  9.44 us (27%)
  Pallas kernels  5 us (14%)
  between operations  1.4 us (4%)
    ppermute x16, starting transfers between devices, trade(): lax.ppermute(block, axis, [(i, i ^ step) for i in range(lax.axis_size(axi...  19.3 us
    ppermute x16, waiting for transfers between devices, trade(): lax.ppermute(block, axis, [(i, i ^ step) for i in range(lax.axis_size(axi...  9.44 us
    pallas_call x9, Pallas kernels, call(): pl.pallas_call(kernel, out_shape=[jax.ShapeDtypeStruct(shape, dtype) for...  5 us
  transfers between devices with their start and end apart: 16, of which 9 were waited for; matrix products, arithmetic and copies ran while one was open for 0% of the time, Pallas kernels for 11%

profile of v7, /device:TPU:0, one launch (start us, length us, event | category | flops | bytes accessed | tf_op | source)
XLA Modules:
  0.0 35.2 jit_solution(4293854190392596025)
XLA Ops:
  0.6 5.1 %collective-permute-start = (bf16[128,256]{1,0:T(8,128)(2,1)}, bf16[128,256]{1,0:T(8,128)(2,1)S(1)}, u32[]{:S(2)}, u32[]{:S(2)}) collective-permute-start(bf16[128,256]{1,0:T(8,128)(2,1)} %refs_3_.1), channel_id=1, source_target_pairs={{0,12},{4,8},{8,4},{12,0},{1,13},{5,9},{9,5},{13,1},{2,14},{6,10},... | collective-permute-start | bytes 196616 | tf_op jit(solution)/shard_map/ppermute | solution.py:32
  5.8 0.0 collective-permute-start.2
  5.8 0.6 %collective-permute-start.1 = (bf16[128,256]{1,0:T(8,128)(2,1)}, bf16[128,256]{1,0:T(8,128)(2,1)S(1)}, u32[]{:S(2)}, u32[]{:S(2)}) collective-permute-start(bf16[128,256]{1,0:T(8,128)(2,1)} %refs_3_.1), channel_id=1, source_target_pairs={{0,4},{4,0},{8,12},{12,8},{1,5},{5,1},{9,13},{13,9},{2,6},{6,2},{1... | collective-permute-start | bytes 196616 | tf_op jit(solution)/shard_map/ppermute | solution.py:32
  7.0 1.8 %shard_map.146 = (bf16[512,512]{1,0:T(8,128)(2,1)S(1)}, bf16[256,512]{1,0:T(8,128)(2,1)S(1)}, bf16[128,256]{1,0:T(8,128)(2,1)S(1)}, bf16[256,384]{1,0:T(8,128)(2...) custom-call(s32[1,256]{1,0:T(1,128)} %bitcast.4, ...), custom_call_target="tpu_custom_call" | custom-call | tf_op jit(solution)/shard_map/pallas_call | solution.py:56
  8.8 2.4 %collective-permute-start.5 = (bf16[512,128]{1,0:T(8,128)(2,1)S(1)}, bf16[512,128]{1,0:T(8,128)(2,1)S(1)}, u32[]{:S(2)}, u32[]{:S(2)}) collective-permute-start(bf16[512,128]{1,0:T(8,128)(2,1)S(1)} %get-tuple-element.40.refs_5_), channel_id=1, source_target_pairs={{0,8},{4,12},{8,0},{12,4},{1,9},{5,13},{9,1},{13,5},{2,10},{6,14},... | collective-permute-start | bytes 393224 | tf_op jit(solution)/shard_map/ppermute | solution.py:32
  11.2 0.0 collective-permute-done.refs_0_
  11.2 0.4 %collective-permute-done.2.refs_2_ = bf16[128,256]{1,0:T(8,128)(2,1)S(1)} collective-permute-done((bf16[128,256]{1,0:T(8,128)(2,1)}, bf16[128,256]{1,0:T(8,128)(2,1)S(1)}, u32[]{:S(2)}, u32[]{:S(2)}) %collective-permute-start.2) | collective-permute-done | bytes 65568 | tf_op jit(solution)/shard_map/ppermute | solution.py:32
  11.6 0.0 collective-permute-done.1.refs_1_
  11.6 0.4 %shard_map.147 = (bf16[128,896]{1,0:T(8,128)(2,1)S(1)}, f32[128,256]{1,0:T(8,128)S(1)}, bf16[128,640]{1,0:T(8,128)(2,1)S(1)}) custom-call(bf16[256,512]{1,0:T(8,128)(2,1)S(1)} %get-tuple-element.37.column_picks, bf16[256,384]{1,0:T(8,128)(2,1)S(1)} %get-tuple-element.38.known, bf16[128,256]{1,0:T(8,128)(2,1)S(1)} %collective-permute-done.refs_0_, ...), custom_call_target="tpu_custom_call" | custom-call | tf_op jit(solution)/shard_map/pallas_call | solution.py:56
  12.0 0.1 collective-permute-start.3
  12.1 0.4 %shard_map.151 = (f32[256,256]{1,0:T(8,128)S(1)}, bf16[256,256]{1,0:T(8,128)(2,1)S(1)}) custom-call(bf16[512,512]{1,0:T(8,128)(2,1)S(1)} %get-tuple-element.54.adjacency, bf16[128,256]{1,0:T(8,128)(2,1)S(1)} %collective-permute-done.refs_0_, bf16[128,256]{1,0:T(8,128)(2,1)S(1)} %collective-permute-done.1.refs_1_, ...), custom_call_target="tpu_custom_call" | custom-call | flops 3000000000 | tf_op jit(solution)/shard_map/pallas_call | solution.py:56
  12.5 0.6 %collective-permute-start.7 = (bf16[256,256]{1,0:T(8,128)(2,1)S(1)}, bf16[256,256]{1,0:T(8,128)(2,1)S(1)}, u32[]{:S(2)}, u32[]{:S(2)}) collective-permute-start(bf16[256,256]{1,0:T(8,128)(2,1)S(1)} %get-tuple-element.56), channel_id=1, source_target_pairs={{0,1},{1,0},{2,3},{3,2},{4,5},{5,4},{6,7},{7,6},{8,9},{9,8},{10,11... | collective-permute-start | bytes 393224 | tf_op jit(solution)/shard_map/ppermute | solution.py:32
  13.1 0.5 %collective-permute-done.3.got = bf16[128,896]{1,0:T(8,128)(2,1)S(1)} collective-permute-done((bf16[128,896]{1,0:T(8,128)(2,1)S(1)}, bf16[128,896]{1,0:T(8,128)(2,1)S(1)}, u32[]{:S(2)}, u32[]{:S(2)}) %collective-permute-start.3) | collective-permute-done | bytes 229408 | tf_op jit(solution)/shard_map/ppermute | solution.py:32
  13.6 1.6 %collective-permute-start.4 = (bf16[64,896]{1,0:T(8,128)(2,1)S(1)}, bf16[64,896]{1,0:T(8,128)(2,1)S(1)}, u32[]{:S(2)}, u32[]{:S(2)}) collective-permute-start(bf16[64,896]{1,0:T(8,128)(2,1)S(1)} %get-tuple-element.46), channel_id=1, source_target_pairs={{0,2},{1,3},{2,0},{3,1},{4,6},{5,7},{6,4},{7,5},{8,10},{9,11},{10,... | collective-permute-start | bytes 344072 | tf_op jit(solution)/shard_map/ppermute | solution.py:32
  15.1 2.1 %collective-permute-done.5 = bf16[512,128]{1,0:T(8,128)(2,1)S(1)} collective-permute-done((bf16[512,128]{1,0:T(8,128)(2,1)S(1)}, bf16[512,128]{1,0:T(8,128)(2,1)S(1)}, u32[]{:S(2)}, u32[]{:S(2)}) %collective-permute-start.5) | collective-permute-done | bytes 131104 | tf_op jit(solution)/shard_map/ppermute | solution.py:32
  17.3 1.6 %collective-permute-done.4.got = bf16[64,896]{1,0:T(8,128)(2,1)S(1)} collective-permute-done((bf16[64,896]{1,0:T(8,128)(2,1)S(1)}, bf16[64,896]{1,0:T(8,128)(2,1)S(1)}, u32[]{:S(2)}, u32[]{:S(2)}) %collective-permute-start.4) | collective-permute-done | bytes 114720 | tf_op jit(solution)/shard_map/ppermute | solution.py:32
  18.8 0.2 shard_map.149
  19.1 2.8 %collective-permute-start.6 = (bf16[272,128]{1,0:T(8,128)(2,1)S(1)}, bf16[272,128]{1,0:T(8,128)(2,1)S(1)}, u32[]{:S(2)}, u32[]{:S(2)}) collective-permute-start(bf16[272,128]{1,0:T(8,128)(2,1)S(1)} %get-tuple-element.51.refs_1_), channel_id=1, source_target_pairs={{0,12},{4,8},{8,4},{12,0},{1,13},{5,9},{9,5},{13,1},{2,14},{6,10},... | collective-permute-start | bytes 208904 | tf_op jit(solution)/shard_map/ppermute | solution.py:32
  21.9 0.0 collective-permute-done.7
  21.9 0.4 %collective-permute-start.10 = (bf16[272,128]{1,0:T(8,128)(2,1)S(1)}, bf16[272,128]{1,0:T(8,128)(2,1)S(1)}, u32[]{:S(2)}, u32[]{:S(2)}) collective-permute-start(bf16[272,128]{1,0:T(8,128)(2,1)S(1)} %get-tuple-element.51.refs_1_), channel_id=1, source_target_pairs={{0,8},{4,12},{8,0},{12,4},{1,9},{5,13},{9,1},{13,5},{2,10},{6,14},... | collective-permute-start | bytes 208904 | tf_op jit(solution)/shard_map/ppermute | solution.py:32
  22.3 1.4 %collective-permute-start.9 = (bf16[272,128]{1,0:T(8,128)(2,1)S(1)}, bf16[272,128]{1,0:T(8,128)(2,1)S(1)}, u32[]{:S(2)}, u32[]{:S(2)}) collective-permute-start(bf16[272,128]{1,0:T(8,128)(2,1)S(1)} %get-tuple-element.51.refs_1_), channel_id=1, source_target_pairs={{0,4},{4,0},{8,12},{12,8},{1,5},{5,1},{9,13},{13,9},{2,6},{6,2},{1... | collective-permute-start | bytes 208904 | tf_op jit(solution)/shard_map/ppermute | solution.py:32
  23.6 0.7 %collective-permute-start.15 = (bf16[256,128]{1,0:T(8,128)(2,1)S(1)}, bf16[256,128]{1,0:T(8,128)(2,1)S(1)}, u32[]{:S(2)}, u32[]{:S(2)}) collective-permute-start(bf16[256,128]{1,0:T(8,128)(2,1)S(1)} %slice.16), channel_id=1, source_target_pairs={{0,4},{4,0},{8,12},{12,8},{1,5},{5,1},{9,13},{13,9},{2,6},{6,2},{1... | collective-permute-start | bytes 196616 | tf_op jit(solution)/shard_map/ppermute | solution.py:32
  24.3 1.0 %collective-permute-done.6.refs_0_ = bf16[272,128]{1,0:T(8,128)(2,1)S(1)} collective-permute-done((bf16[272,128]{1,0:T(8,128)(2,1)S(1)}, bf16[272,128]{1,0:T(8,128)(2,1)S(1)}, u32[]{:S(2)}, u32[]{:S(2)}) %collective-permute-start.6) | collective-permute-done | bytes 69664 | tf_op jit(solution)/shard_map/ppermute | solution.py:32
  25.3 1.6 %collective-permute-start.13 = (bf16[64,256]{1,0:T(8,128)(2,1)S(1)}, bf16[64,256]{1,0:T(8,128)(2,1)S(1)}, u32[]{:S(2)}, u32[]{:S(2)}) collective-permute-start(bf16[64,256]{1,0:T(8,128)(2,1)S(1)} %get-tuple-element.60), channel_id=1, source_target_pairs={{0,2},{1,3},{2,0},{3,1},{4,6},{5,7},{6,4},{7,5},{8,10},{9,11},{10,... | collective-permute-start | bytes 98312 | tf_op jit(solution)/shard_map/ppermute | solution.py:32
  26.9 0.6 %collective-permute-start.8 = (bf16[128,256]{1,0:T(8,128)(2,1)S(1)}, bf16[128,256]{1,0:T(8,128)(2,1)S(1)}, u32[]{:S(2)}, u32[]{:S(2)}) collective-permute-start(bf16[128,256]{1,0:T(8,128)(2,1)S(1)} %slice.20), channel_id=1, source_target_pairs={{0,2},{1,3},{2,0},{3,1},{4,6},{5,7},{6,4},{7,5},{8,10},{9,11},{10,... | collective-permute-start | bytes 196616 | tf_op jit(solution)/shard_map/ppermute | solution.py:32
  27.5 0.6 %collective-permute-done.10.refs_1_ = bf16[272,128]{1,0:T(8,128)(2,1)S(1)} collective-permute-done((bf16[272,128]{1,0:T(8,128)(2,1)S(1)}, bf16[272,128]{1,0:T(8,128)(2,1)S(1)}, u32[]{:S(2)}, u32[]{:S(2)}) %collective-permute-start.10) | collective-permute-done | bytes 69664 | tf_op jit(solution)/shard_map/ppermute | solution.py:32
  28.1 0.1 collective-permute-done.9.refs_0_
  28.2 1.6 %collective-permute-start.11 = (bf16[272,128]{1,0:T(8,128)(2,1)S(1)}, bf16[272,128]{1,0:T(8,128)(2,1)S(1)}, u32[]{:S(2)}, u32[]{:S(2)}) collective-permute-start(bf16[272,128]{1,0:T(8,128)(2,1)S(1)} %shard_map.153), channel_id=1, source_target_pairs={{0,2},{1,3},{2,0},{3,1},{4,6},{5,7},{6,4},{7,5},{8,10},{9,11},{10,... | collective-permute-start | bytes 208904 | tf_op jit(solution)/shard_map/ppermute | solution.py:32
  29.8 0.0 collective-permute-done.13
  29.8 0.0 collective-permute-start.14
  29.8 2.8 %collective-permute-done.11 = bf16[272,128]{1,0:T(8,128)(2,1)S(1)} collective-permute-done((bf16[272,128]{1,0:T(8,128)(2,1)S(1)}, bf16[272,128]{1,0:T(8,128)(2,1)S(1)}, u32[]{:S(2)}, u32[]{:S(2)}) %collective-permute-start.11) | collective-permute-done | bytes 69664 | tf_op jit(solution)/shard_map/ppermute | solution.py:32
  32.6 0.1 collective-permute-start.12
  32.7 0.0 collective-permute-done.15
  32.7 0.0 collective-permute-done.8.got
  32.7 0.9 %shard_map.152 = bf16[128,256]{1,0:T(8,128)(2,1)} custom-call(bf16[128,256]{1,0:T(8,128)(2,1)S(1)} %get-tuple-element.36.refs_3_.features, f32[128,256]{1,0:T(8,128)S(1)} %slice.13.total, bf16[128,256]{1,0:T(8,128)(2,1)S(1)} %collective-permute-done.8.got, f32[128,128]{1,0:T(8,128)S(1)} %get-tuple-element.58.inverse, ...), custom_call_target="tpu_custom_call" | custom-call | tf_op jit(solution)/shard_map/pallas_call | solution.py:56
  33.6 0.0 collective-permute-done.14.refs_3_
  33.6 0.4 %collective-permute-done.12.refs_1_ = bf16[544,128]{1,0:T(8,128)(2,1)S(1)} collective-permute-done((bf16[544,128]{1,0:T(8,128)(2,1)S(1)}, bf16[544,128]{1,0:T(8,128)(2,1)S(1)}, u32[]{:S(2)}, u32[]{:S(2)}) %collective-permute-start.12) | collective-permute-done | bytes 139296 | tf_op jit(solution)/shard_map/ppermute | solution.py:32
  34.0 1.2 %shard_map.154 = (bf16[128,256]{1,0:T(8,128)(2,1)}, f32[256,256]{1,0:T(8,128)}, f32[256,256]{1,0:T(8,128)}, f32[1,256]{1,0:T(1,128)}) custom-call(bf16[544,128]{1,0:T(8,128)(2,1)S(1)} %pad_maximum_fusion.refs_0_, bf16[544,128]{1,0:T(8,128)(2,1)S(1)} %collective-permute-done.12.refs_1_, bf16[128,256]{1,0:T(8,128)(2,1)S(1)} %constant_dynamic-update-slice_fusion.refs_2_, ...), custom_call_target="tpu_custom_call" | custom-call | tf_op jit(solution)/shard_map/pallas_call | solution.py:56
  (12 shorter events, 0.2 us)
Async XLA Ops:
  0.6 10.5 %collective-permute-start = (bf16[128,256]{1,0:T(8,128)(2,1)}, bf16[128,256]{1,0:T(8,128)(2,1)S(1)}, u32[]{:S(2)}, u32[]{:S(2)}) collective-permute-start(bf16[128,256]{1,0:T(8,128)(2,1)} %refs_3_.1), channel_id=1, source_target_pairs={{0,12},{4,8},{8,4},{12,0},{1,13},{5,9},{9,5},{13,1},{2,14},{6,10},... | collective-permute-start | bytes 196616 | tf_op jit(solution)/shard_map/ppermute | solution.py:32
  5.8 5.8 %collective-permute-start.2 = (bf16[128,256]{1,0:T(8,128)(2,1)}, bf16[128,256]{1,0:T(8,128)(2,1)S(1)}, u32[]{:S(2)}, u32[]{:S(2)}) collective-permute-start(bf16[128,256]{1,0:T(8,128)(2,1)} %refs_3_.1), channel_id=1, source_target_pairs={{0,8},{4,12},{8,0},{12,4},{1,9},{5,13},{9,1},{13,5},{2,10},{6,14},... | collective-permute-start | bytes 196616 | tf_op jit(solution)/shard_map/ppermute | solution.py:32
  5.8 5.8 %collective-permute-start.1 = (bf16[128,256]{1,0:T(8,128)(2,1)}, bf16[128,256]{1,0:T(8,128)(2,1)S(1)}, u32[]{:S(2)}, u32[]{:S(2)}) collective-permute-start(bf16[128,256]{1,0:T(8,128)(2,1)} %refs_3_.1), channel_id=1, source_target_pairs={{0,4},{4,0},{8,12},{12,8},{1,5},{5,1},{9,13},{13,9},{2,6},{6,2},{1... | collective-permute-start | bytes 196616 | tf_op jit(solution)/shard_map/ppermute | solution.py:32
  8.8 8.4 %collective-permute-start.5 = (bf16[512,128]{1,0:T(8,128)(2,1)S(1)}, bf16[512,128]{1,0:T(8,128)(2,1)S(1)}, u32[]{:S(2)}, u32[]{:S(2)}) collective-permute-start(bf16[512,128]{1,0:T(8,128)(2,1)S(1)} %get-tuple-element.40.refs_5_), channel_id=1, source_target_pairs={{0,8},{4,12},{8,0},{12,4},{1,9},{5,13},{9,1},{13,5},{2,10},{6,14},... | collective-permute-start | bytes 393224 | tf_op jit(solution)/shard_map/ppermute | solution.py:32
  12.0 1.6 %collective-permute-start.3 = (bf16[128,896]{1,0:T(8,128)(2,1)S(1)}, bf16[128,896]{1,0:T(8,128)(2,1)S(1)}, u32[]{:S(2)}, u32[]{:S(2)}) collective-permute-start(bf16[128,896]{1,0:T(8,128)(2,1)S(1)} %get-tuple-element.43), channel_id=1, source_target_pairs={{0,1},{1,0},{2,3},{3,2},{4,5},{5,4},{6,7},{7,6},{8,9},{9,8},{10,11... | collective-permute-start | bytes 688136 | tf_op jit(solution)/shard_map/ppermute | solution.py:32
  12.5 9.4 %collective-permute-start.7 = (bf16[256,256]{1,0:T(8,128)(2,1)S(1)}, bf16[256,256]{1,0:T(8,128)(2,1)S(1)}, u32[]{:S(2)}, u32[]{:S(2)}) collective-permute-start(bf16[256,256]{1,0:T(8,128)(2,1)S(1)} %get-tuple-element.56), channel_id=1, source_target_pairs={{0,1},{1,0},{2,3},{3,2},{4,5},{5,4},{6,7},{7,6},{8,9},{9,8},{10,11... | collective-permute-start | bytes 393224 | tf_op jit(solution)/shard_map/ppermute | solution.py:32
  13.6 5.3 %collective-permute-start.4 = (bf16[64,896]{1,0:T(8,128)(2,1)S(1)}, bf16[64,896]{1,0:T(8,128)(2,1)S(1)}, u32[]{:S(2)}, u32[]{:S(2)}) collective-permute-start(bf16[64,896]{1,0:T(8,128)(2,1)S(1)} %get-tuple-element.46), channel_id=1, source_target_pairs={{0,2},{1,3},{2,0},{3,1},{4,6},{5,7},{6,4},{7,5},{8,10},{9,11},{10,... | collective-permute-start | bytes 344072 | tf_op jit(solution)/shard_map/ppermute | solution.py:32
  19.1 6.2 %collective-permute-start.6 = (bf16[272,128]{1,0:T(8,128)(2,1)S(1)}, bf16[272,128]{1,0:T(8,128)(2,1)S(1)}, u32[]{:S(2)}, u32[]{:S(2)}) collective-permute-start(bf16[272,128]{1,0:T(8,128)(2,1)S(1)} %get-tuple-element.51.refs_1_), channel_id=1, source_target_pairs={{0,12},{4,8},{8,4},{12,0},{1,13},{5,9},{9,5},{13,1},{2,14},{6,10},... | collective-permute-start | bytes 208904 | tf_op jit(solution)/shard_map/ppermute | solution.py:32
  21.9 6.2 %collective-permute-start.10 = (bf16[272,128]{1,0:T(8,128)(2,1)S(1)}, bf16[272,128]{1,0:T(8,128)(2,1)S(1)}, u32[]{:S(2)}, u32[]{:S(2)}) collective-permute-start(bf16[272,128]{1,0:T(8,128)(2,1)S(1)} %get-tuple-element.51.refs_1_), channel_id=1, source_target_pairs={{0,8},{4,12},{8,0},{12,4},{1,9},{5,13},{9,1},{13,5},{2,10},{6,14},... | collective-permute-start | bytes 208904 | tf_op jit(solution)/shard_map/ppermute | solution.py:32
  22.3 5.9 %collective-permute-start.9 = (bf16[272,128]{1,0:T(8,128)(2,1)S(1)}, bf16[272,128]{1,0:T(8,128)(2,1)S(1)}, u32[]{:S(2)}, u32[]{:S(2)}) collective-permute-start(bf16[272,128]{1,0:T(8,128)(2,1)S(1)} %get-tuple-element.51.refs_1_), channel_id=1, source_target_pairs={{0,4},{4,0},{8,12},{12,8},{1,5},{5,1},{9,13},{13,9},{2,6},{6,2},{1... | collective-permute-start | bytes 208904 | tf_op jit(solution)/shard_map/ppermute | solution.py:32
  23.6 9.1 %collective-permute-start.15 = (bf16[256,128]{1,0:T(8,128)(2,1)S(1)}, bf16[256,128]{1,0:T(8,128)(2,1)S(1)}, u32[]{:S(2)}, u32[]{:S(2)}) collective-permute-start(bf16[256,128]{1,0:T(8,128)(2,1)S(1)} %slice.16), channel_id=1, source_target_pairs={{0,4},{4,0},{8,12},{12,8},{1,5},{5,1},{9,13},{13,9},{2,6},{6,2},{1... | collective-permute-start | bytes 196616 | tf_op jit(solution)/shard_map/ppermute | solution.py:32
  25.3 4.4 %collective-permute-start.13 = (bf16[64,256]{1,0:T(8,128)(2,1)S(1)}, bf16[64,256]{1,0:T(8,128)(2,1)S(1)}, u32[]{:S(2)}, u32[]{:S(2)}) collective-permute-start(bf16[64,256]{1,0:T(8,128)(2,1)S(1)} %get-tuple-element.60), channel_id=1, source_target_pairs={{0,2},{1,3},{2,0},{3,1},{4,6},{5,7},{6,4},{7,5},{8,10},{9,11},{10,... | collective-permute-start | bytes 98312 | tf_op jit(solution)/shard_map/ppermute | solution.py:32
  26.9 5.8 %collective-permute-start.8 = (bf16[128,256]{1,0:T(8,128)(2,1)S(1)}, bf16[128,256]{1,0:T(8,128)(2,1)S(1)}, u32[]{:S(2)}, u32[]{:S(2)}) collective-permute-start(bf16[128,256]{1,0:T(8,128)(2,1)S(1)} %slice.20), channel_id=1, source_target_pairs={{0,2},{1,3},{2,0},{3,1},{4,6},{5,7},{6,4},{7,5},{8,10},{9,11},{10,... | collective-permute-start | bytes 196616 | tf_op jit(solution)/shard_map/ppermute | solution.py:32
  28.2 4.4 %collective-permute-start.11 = (bf16[272,128]{1,0:T(8,128)(2,1)S(1)}, bf16[272,128]{1,0:T(8,128)(2,1)S(1)}, u32[]{:S(2)}, u32[]{:S(2)}) collective-permute-start(bf16[272,128]{1,0:T(8,128)(2,1)S(1)} %shard_map.153), channel_id=1, source_target_pairs={{0,2},{1,3},{2,0},{3,1},{4,6},{5,7},{6,4},{7,5},{8,10},{9,11},{10,... | collective-permute-start | bytes 208904 | tf_op jit(solution)/shard_map/ppermute | solution.py:32
  29.8 3.8 %collective-permute-start.14 = (bf16[128,256]{1,0:T(8,128)(2,1)S(1)}, bf16[128,256]{1,0:T(8,128)(2,1)S(1)}, u32[]{:S(2)}, u32[]{:S(2)}) collective-permute-start(bf16[128,256]{1,0:T(8,128)(2,1)S(1)} %constant_dynamic-update-slice_fusion.refs_2_), channel_id=1, source_target_pairs={{0,1},{1,0},{2,3},{3,2},{4,5},{5,4},{6,7},{7,6},{8,9},{9,8},{10,11... | collective-permute-start | bytes 196616 | tf_op jit(solution)/shard_map/ppermute | solution.py:32
  32.6 1.4 %collective-permute-start.12 = (bf16[544,128]{1,0:T(8,128)(2,1)S(1)}, bf16[544,128]{1,0:T(8,128)(2,1)S(1)}, u32[]{:S(2)}, u32[]{:S(2)}) collective-permute-start(bf16[544,128]{1,0:T(8,128)(2,1)S(1)} %pad_maximum_fusion.refs_0_), channel_id=1, source_target_pairs={{0,1},{1,0},{2,3},{3,2},{4,5},{5,4},{6,7},{7,6},{8,9},{9,8},{10,11... | collective-permute-start | bytes 417800 | tf_op jit(solution)/shard_map/ppermute | solution.py:32

commit v8 on v7

--- a/solution.py
+++ b/solution.py
@@ -107,7 +107,7 @@
     inverse[...] = 1.0 / jnp.broadcast_to(counts, (nodes, nodes)).T
     counts = jnp.sum(own.astype(F32) * counts, axis=1, keepdims=True)
     known[:, width:] = jnp.broadcast_to(counts, (slots, 128)).astype(BF16)
-    for copy in copies[3:]:
+    for copy in copies[3:7]:
         copy.wait()
     for k in range(tiles.shape[2]):
 
@@ -121,6 +121,8 @@
     for s in range(rows):
         block = picked[:, s * nodes : (s + 1) * nodes]
         (far if s // 2 else near)[s % 2 * slots : (s % 2 + 1) * slots, :] = block
+    for copy in copies[7:]:
+        copy.wait()
 
 
 def block_of(step, near, far, slots):

time: 35.4 us -> 35.4 us (level)
  no operation moved by 1% of the time
where the time goes in v8:
time: 35.4 us; the launch traced here: 35.2 us
  starting transfers between devices  19.3 us (55%)
  waiting for transfers between devices  9.4 us (27%)
  Pallas kernels  4.97 us (14%)
  between operations  1.4 us (4%)
    ppermute x16, starting transfers between devices, trade(): lax.ppermute(block, axis, [(i, i ^ step) for i in range(lax.axis_size(axi...  19.3 us
    ppermute x16, waiting for transfers between devices, trade(): lax.ppermute(block, axis, [(i, i ^ step) for i in range(lax.axis_size(axi...  9.4 us
    pallas_call x9, Pallas kernels, call(): pl.pallas_call(kernel, out_shape=[jax.ShapeDtypeStruct(shape, dtype) for...  4.97 us
  transfers between devices with their start and end apart: 16, of which 9 were waited for; matrix products, arithmetic and copies ran while one was open for 0% of the time, Pallas kernels for 11%

profile of v8, /device:TPU:0, one launch (start us, length us, event | category | flops | bytes accessed | tf_op | source)
XLA Modules:
  0.0 35.2 jit_solution(7286419637463402873)
XLA Ops:
  0.6 5.1 %collective-permute-start = (bf16[128,256]{1,0:T(8,128)(2,1)}, bf16[128,256]{1,0:T(8,128)(2,1)S(1)}, u32[]{:S(2)}, u32[]{:S(2)}) collective-permute-start(bf16[128,256]{1,0:T(8,128)(2,1)} %refs_3_.1), channel_id=1, source_target_pairs={{0,12},{4,8},{8,4},{12,0},{1,13},{5,9},{9,5},{13,1},{2,14},{6,10},... | collective-permute-start | bytes 196616 | tf_op jit(solution)/shard_map/ppermute | solution.py:32
  5.8 0.0 collective-permute-start.2
  5.8 0.6 %collective-permute-start.1 = (bf16[128,256]{1,0:T(8,128)(2,1)}, bf16[128,256]{1,0:T(8,128)(2,1)S(1)}, u32[]{:S(2)}, u32[]{:S(2)}) collective-permute-start(bf16[128,256]{1,0:T(8,128)(2,1)} %refs_3_.1), channel_id=1, source_target_pairs={{0,4},{4,0},{8,12},{12,8},{1,5},{5,1},{9,13},{13,9},{2,6},{6,2},{1... | collective-permute-start | bytes 196616 | tf_op jit(solution)/shard_map/ppermute | solution.py:32
  7.0 1.7 %shard_map.146 = (bf16[512,512]{1,0:T(8,128)(2,1)S(1)}, bf16[256,512]{1,0:T(8,128)(2,1)S(1)}, bf16[128,256]{1,0:T(8,128)(2,1)S(1)}, bf16[256,384]{1,0:T(8,128)(2...) custom-call(s32[1,256]{1,0:T(1,128)} %bitcast.4, ...), custom_call_target="tpu_custom_call" | custom-call | tf_op jit(solution)/shard_map/pallas_call | solution.py:56
  8.8 2.4 %collective-permute-start.5 = (bf16[512,128]{1,0:T(8,128)(2,1)S(1)}, bf16[512,128]{1,0:T(8,128)(2,1)S(1)}, u32[]{:S(2)}, u32[]{:S(2)}) collective-permute-start(bf16[512,128]{1,0:T(8,128)(2,1)S(1)} %get-tuple-element.40.refs_5_), channel_id=1, source_target_pairs={{0,8},{4,12},{8,0},{12,4},{1,9},{5,13},{9,1},{13,5},{2,10},{6,14},... | collective-permute-start | bytes 393224 | tf_op jit(solution)/shard_map/ppermute | solution.py:32
  11.2 0.0 collective-permute-done.refs_0_
  11.2 0.4 %collective-permute-done.2.refs_2_ = bf16[128,256]{1,0:T(8,128)(2,1)S(1)} collective-permute-done((bf16[128,256]{1,0:T(8,128)(2,1)}, bf16[128,256]{1,0:T(8,128)(2,1)S(1)}, u32[]{:S(2)}, u32[]{:S(2)}) %collective-permute-start.2) | collective-permute-done | bytes 65568 | tf_op jit(solution)/shard_map/ppermute | solution.py:32
  11.6 0.0 collective-permute-done.1.refs_1_
  11.6 0.4 %shard_map.147 = (bf16[128,896]{1,0:T(8,128)(2,1)S(1)}, f32[128,256]{1,0:T(8,128)S(1)}, bf16[128,640]{1,0:T(8,128)(2,1)S(1)}) custom-call(bf16[256,512]{1,0:T(8,128)(2,1)S(1)} %get-tuple-element.37.column_picks, bf16[256,384]{1,0:T(8,128)(2,1)S(1)} %get-tuple-element.38.known, bf16[128,256]{1,0:T(8,128)(2,1)S(1)} %collective-permute-done.refs_0_, ...), custom_call_target="tpu_custom_call" | custom-call | tf_op jit(solution)/shard_map/pallas_call | solution.py:56
  12.0 0.1 collective-permute-start.3
  12.1 0.4 %shard_map.151 = (f32[256,256]{1,0:T(8,128)S(1)}, bf16[256,256]{1,0:T(8,128)(2,1)S(1)}) custom-call(bf16[512,512]{1,0:T(8,128)(2,1)S(1)} %get-tuple-element.54.adjacency, bf16[128,256]{1,0:T(8,128)(2,1)S(1)} %collective-permute-done.refs_0_, bf16[128,256]{1,0:T(8,128)(2,1)S(1)} %collective-permute-done.1.refs_1_, ...), custom_call_target="tpu_custom_call" | custom-call | flops 3000000000 | tf_op jit(solution)/shard_map/pallas_call | solution.py:56
  12.5 0.6 %collective-permute-start.7 = (bf16[256,256]{1,0:T(8,128)(2,1)S(1)}, bf16[256,256]{1,0:T(8,128)(2,1)S(1)}, u32[]{:S(2)}, u32[]{:S(2)}) collective-permute-start(bf16[256,256]{1,0:T(8,128)(2,1)S(1)} %get-tuple-element.56), channel_id=1, source_target_pairs={{0,1},{1,0},{2,3},{3,2},{4,5},{5,4},{6,7},{7,6},{8,9},{9,8},{10,11... | collective-permute-start | bytes 393224 | tf_op jit(solution)/shard_map/ppermute | solution.py:32
  13.1 0.5 %collective-permute-done.3.got = bf16[128,896]{1,0:T(8,128)(2,1)S(1)} collective-permute-done((bf16[128,896]{1,0:T(8,128)(2,1)S(1)}, bf16[128,896]{1,0:T(8,128)(2,1)S(1)}, u32[]{:S(2)}, u32[]{:S(2)}) %collective-permute-start.3) | collective-permute-done | bytes 229408 | tf_op jit(solution)/shard_map/ppermute | solution.py:32
  13.6 1.6 %collective-permute-start.4 = (bf16[64,896]{1,0:T(8,128)(2,1)S(1)}, bf16[64,896]{1,0:T(8,128)(2,1)S(1)}, u32[]{:S(2)}, u32[]{:S(2)}) collective-permute-start(bf16[64,896]{1,0:T(8,128)(2,1)S(1)} %get-tuple-element.46), channel_id=1, source_target_pairs={{0,2},{1,3},{2,0},{3,1},{4,6},{5,7},{6,4},{7,5},{8,10},{9,11},{10,... | collective-permute-start | bytes 344072 | tf_op jit(solution)/shard_map/ppermute | solution.py:32
  15.1 2.1 %collective-permute-done.5 = bf16[512,128]{1,0:T(8,128)(2,1)S(1)} collective-permute-done((bf16[512,128]{1,0:T(8,128)(2,1)S(1)}, bf16[512,128]{1,0:T(8,128)(2,1)S(1)}, u32[]{:S(2)}, u32[]{:S(2)}) %collective-permute-start.5) | collective-permute-done | bytes 131104 | tf_op jit(solution)/shard_map/ppermute | solution.py:32
  17.3 1.5 %collective-permute-done.4.got = bf16[64,896]{1,0:T(8,128)(2,1)S(1)} collective-permute-done((bf16[64,896]{1,0:T(8,128)(2,1)S(1)}, bf16[64,896]{1,0:T(8,128)(2,1)S(1)}, u32[]{:S(2)}, u32[]{:S(2)}) %collective-permute-start.4) | collective-permute-done | bytes 114720 | tf_op jit(solution)/shard_map/ppermute | solution.py:32
  18.8 0.2 shard_map.149
  19.1 2.8 %collective-permute-start.6 = (bf16[272,128]{1,0:T(8,128)(2,1)S(1)}, bf16[272,128]{1,0:T(8,128)(2,1)S(1)}, u32[]{:S(2)}, u32[]{:S(2)}) collective-permute-start(bf16[272,128]{1,0:T(8,128)(2,1)S(1)} %get-tuple-element.51.refs_1_), channel_id=1, source_target_pairs={{0,12},{4,8},{8,4},{12,0},{1,13},{5,9},{9,5},{13,1},{2,14},{6,10},... | collective-permute-start | bytes 208904 | tf_op jit(solution)/shard_map/ppermute | solution.py:32
  21.9 0.0 collective-permute-done.7
  21.9 0.4 %collective-permute-start.10 = (bf16[272,128]{1,0:T(8,128)(2,1)S(1)}, bf16[272,128]{1,0:T(8,128)(2,1)S(1)}, u32[]{:S(2)}, u32[]{:S(2)}) collective-permute-start(bf16[272,128]{1,0:T(8,128)(2,1)S(1)} %get-tuple-element.51.refs_1_), channel_id=1, source_target_pairs={{0,8},{4,12},{8,0},{12,4},{1,9},{5,13},{9,1},{13,5},{2,10},{6,14},... | collective-permute-start | bytes 208904 | tf_op jit(solution)/shard_map/ppermute | solution.py:32
  22.3 1.3 %collective-permute-start.9 = (bf16[272,128]{1,0:T(8,128)(2,1)S(1)}, bf16[272,128]{1,0:T(8,128)(2,1)S(1)}, u32[]{:S(2)}, u32[]{:S(2)}) collective-permute-start(bf16[272,128]{1,0:T(8,128)(2,1)S(1)} %get-tuple-element.51.refs_1_), channel_id=1, source_target_pairs={{0,4},{4,0},{8,12},{12,8},{1,5},{5,1},{9,13},{13,9},{2,6},{6,2},{1... | collective-permute-start | bytes 208904 | tf_op jit(solution)/shard_map/ppermute | solution.py:32
  23.6 0.7 %collective-permute-start.15 = (bf16[256,128]{1,0:T(8,128)(2,1)S(1)}, bf16[256,128]{1,0:T(8,128)(2,1)S(1)}, u32[]{:S(2)}, u32[]{:S(2)}) collective-permute-start(bf16[256,128]{1,0:T(8,128)(2,1)S(1)} %slice.16), channel_id=1, source_target_pairs={{0,4},{4,0},{8,12},{12,8},{1,5},{5,1},{9,13},{13,9},{2,6},{6,2},{1... | collective-permute-start | bytes 196616 | tf_op jit(solution)/shard_map/ppermute | solution.py:32
  24.4 1.0 %collective-permute-done.6.refs_0_ = bf16[272,128]{1,0:T(8,128)(2,1)S(1)} collective-permute-done((bf16[272,128]{1,0:T(8,128)(2,1)S(1)}, bf16[272,128]{1,0:T(8,128)(2,1)S(1)}, u32[]{:S(2)}, u32[]{:S(2)}) %collective-permute-start.6) | collective-permute-done | bytes 69664 | tf_op jit(solution)/shard_map/ppermute | solution.py:32
  25.3 1.6 %collective-permute-start.13 = (bf16[64,256]{1,0:T(8,128)(2,1)S(1)}, bf16[64,256]{1,0:T(8,128)(2,1)S(1)}, u32[]{:S(2)}, u32[]{:S(2)}) collective-permute-start(bf16[64,256]{1,0:T(8,128)(2,1)S(1)} %get-tuple-element.60), channel_id=1, source_target_pairs={{0,2},{1,3},{2,0},{3,1},{4,6},{5,7},{6,4},{7,5},{8,10},{9,11},{10,... | collective-permute-start | bytes 98312 | tf_op jit(solution)/shard_map/ppermute | solution.py:32
  26.9 0.6 %collective-permute-start.8 = (bf16[128,256]{1,0:T(8,128)(2,1)S(1)}, bf16[128,256]{1,0:T(8,128)(2,1)S(1)}, u32[]{:S(2)}, u32[]{:S(2)}) collective-permute-start(bf16[128,256]{1,0:T(8,128)(2,1)S(1)} %slice.20), channel_id=1, source_target_pairs={{0,2},{1,3},{2,0},{3,1},{4,6},{5,7},{6,4},{7,5},{8,10},{9,11},{10,... | collective-permute-start | bytes 196616 | tf_op jit(solution)/shard_map/ppermute | solution.py:32
  27.5 0.6 %collective-permute-done.10.refs_1_ = bf16[272,128]{1,0:T(8,128)(2,1)S(1)} collective-permute-done((bf16[272,128]{1,0:T(8,128)(2,1)S(1)}, bf16[272,128]{1,0:T(8,128)(2,1)S(1)}, u32[]{:S(2)}, u32[]{:S(2)}) %collective-permute-start.10) | collective-permute-done | bytes 69664 | tf_op jit(solution)/shard_map/ppermute | solution.py:32
  28.1 0.1 collective-permute-done.9.refs_0_
  28.2 1.6 %collective-permute-start.11 = (bf16[272,128]{1,0:T(8,128)(2,1)S(1)}, bf16[272,128]{1,0:T(8,128)(2,1)S(1)}, u32[]{:S(2)}, u32[]{:S(2)}) collective-permute-start(bf16[272,128]{1,0:T(8,128)(2,1)S(1)} %shard_map.153), channel_id=1, source_target_pairs={{0,2},{1,3},{2,0},{3,1},{4,6},{5,7},{6,4},{7,5},{8,10},{9,11},{10,... | collective-permute-start | bytes 208904 | tf_op jit(solution)/shard_map/ppermute | solution.py:32
  29.8 0.0 collective-permute-done.13
  29.8 0.0 collective-permute-start.14
  29.8 2.8 %collective-permute-done.11 = bf16[272,128]{1,0:T(8,128)(2,1)S(1)} collective-permute-done((bf16[272,128]{1,0:T(8,128)(2,1)S(1)}, bf16[272,128]{1,0:T(8,128)(2,1)S(1)}, u32[]{:S(2)}, u32[]{:S(2)}) %collective-permute-start.11) | collective-permute-done | bytes 69664 | tf_op jit(solution)/shard_map/ppermute | solution.py:32
  32.6 0.1 collective-permute-start.12
  32.7 0.0 collective-permute-done.15
  32.7 0.0 collective-permute-done.8.got
  32.7 0.9 %shard_map.152 = bf16[128,256]{1,0:T(8,128)(2,1)} custom-call(bf16[128,256]{1,0:T(8,128)(2,1)S(1)} %get-tuple-element.36.refs_3_.features, f32[128,256]{1,0:T(8,128)S(1)} %slice.13.total, bf16[128,256]{1,0:T(8,128)(2,1)S(1)} %collective-permute-done.8.got, f32[128,128]{1,0:T(8,128)S(1)} %get-tuple-element.58.inverse, ...), custom_call_target="tpu_custom_call" | custom-call | tf_op jit(solution)/shard_map/pallas_call | solution.py:56
  33.6 0.0 collective-permute-done.14.refs_3_
  33.6 0.4 %collective-permute-done.12.refs_1_ = bf16[544,128]{1,0:T(8,128)(2,1)S(1)} collective-permute-done((bf16[544,128]{1,0:T(8,128)(2,1)S(1)}, bf16[544,128]{1,0:T(8,128)(2,1)S(1)}, u32[]{:S(2)}, u32[]{:S(2)}) %collective-permute-start.12) | collective-permute-done | bytes 139296 | tf_op jit(solution)/shard_map/ppermute | solution.py:32
  34.0 1.2 %shard_map.154 = (bf16[128,256]{1,0:T(8,128)(2,1)}, f32[256,256]{1,0:T(8,128)}, f32[256,256]{1,0:T(8,128)}, f32[1,256]{1,0:T(1,128)}) custom-call(bf16[544,128]{1,0:T(8,128)(2,1)S(1)} %pad_maximum_fusion.refs_0_, bf16[544,128]{1,0:T(8,128)(2,1)S(1)} %collective-permute-done.12.refs_1_, bf16[128,256]{1,0:T(8,128)(2,1)S(1)} %constant_dynamic-update-slice_fusion.refs_2_, ...), custom_call_target="tpu_custom_call" | custom-call | tf_op jit(solution)/shard_map/pallas_call | solution.py:56
  (12 shorter events, 0.2 us)
Async XLA Ops:
  0.6 10.5 %collective-permute-start = (bf16[128,256]{1,0:T(8,128)(2,1)}, bf16[128,256]{1,0:T(8,128)(2,1)S(1)}, u32[]{:S(2)}, u32[]{:S(2)}) collective-permute-start(bf16[128,256]{1,0:T(8,128)(2,1)} %refs_3_.1), channel_id=1, source_target_pairs={{0,12},{4,8},{8,4},{12,0},{1,13},{5,9},{9,5},{13,1},{2,14},{6,10},... | collective-permute-start | bytes 196616 | tf_op jit(solution)/shard_map/ppermute | solution.py:32
  5.8 5.8 %collective-permute-start.2 = (bf16[128,256]{1,0:T(8,128)(2,1)}, bf16[128,256]{1,0:T(8,128)(2,1)S(1)}, u32[]{:S(2)}, u32[]{:S(2)}) collective-permute-start(bf16[128,256]{1,0:T(8,128)(2,1)} %refs_3_.1), channel_id=1, source_target_pairs={{0,8},{4,12},{8,0},{12,4},{1,9},{5,13},{9,1},{13,5},{2,10},{6,14},... | collective-permute-start | bytes 196616 | tf_op jit(solution)/shard_map/ppermute | solution.py:32
  5.8 5.8 %collective-permute-start.1 = (bf16[128,256]{1,0:T(8,128)(2,1)}, bf16[128,256]{1,0:T(8,128)(2,1)S(1)}, u32[]{:S(2)}, u32[]{:S(2)}) collective-permute-start(bf16[128,256]{1,0:T(8,128)(2,1)} %refs_3_.1), channel_id=1, source_target_pairs={{0,4},{4,0},{8,12},{12,8},{1,5},{5,1},{9,13},{13,9},{2,6},{6,2},{1... | collective-permute-start | bytes 196616 | tf_op jit(solution)/shard_map/ppermute | solution.py:32
  8.8 8.5 %collective-permute-start.5 = (bf16[512,128]{1,0:T(8,128)(2,1)S(1)}, bf16[512,128]{1,0:T(8,128)(2,1)S(1)}, u32[]{:S(2)}, u32[]{:S(2)}) collective-permute-start(bf16[512,128]{1,0:T(8,128)(2,1)S(1)} %get-tuple-element.40.refs_5_), channel_id=1, source_target_pairs={{0,8},{4,12},{8,0},{12,4},{1,9},{5,13},{9,1},{13,5},{2,10},{6,14},... | collective-permute-start | bytes 393224 | tf_op jit(solution)/shard_map/ppermute | solution.py:32
  12.0 1.6 %collective-permute-start.3 = (bf16[128,896]{1,0:T(8,128)(2,1)S(1)}, bf16[128,896]{1,0:T(8,128)(2,1)S(1)}, u32[]{:S(2)}, u32[]{:S(2)}) collective-permute-start(bf16[128,896]{1,0:T(8,128)(2,1)S(1)} %get-tuple-element.43), channel_id=1, source_target_pairs={{0,1},{1,0},{2,3},{3,2},{4,5},{5,4},{6,7},{7,6},{8,9},{9,8},{10,11... | collective-permute-start | bytes 688136 | tf_op jit(solution)/shard_map/ppermute | solution.py:32
  12.5 9.4 %collective-permute-start.7 = (bf16[256,256]{1,0:T(8,128)(2,1)S(1)}, bf16[256,256]{1,0:T(8,128)(2,1)S(1)}, u32[]{:S(2)}, u32[]{:S(2)}) collective-permute-start(bf16[256,256]{1,0:T(8,128)(2,1)S(1)} %get-tuple-element.56), channel_id=1, source_target_pairs={{0,1},{1,0},{2,3},{3,2},{4,5},{5,4},{6,7},{7,6},{8,9},{9,8},{10,11... | collective-permute-start | bytes 393224 | tf_op jit(solution)/shard_map/ppermute | solution.py:32
  13.6 5.3 %collective-permute-start.4 = (bf16[64,896]{1,0:T(8,128)(2,1)S(1)}, bf16[64,896]{1,0:T(8,128)(2,1)S(1)}, u32[]{:S(2)}, u32[]{:S(2)}) collective-permute-start(bf16[64,896]{1,0:T(8,128)(2,1)S(1)} %get-tuple-element.46), channel_id=1, source_target_pairs={{0,2},{1,3},{2,0},{3,1},{4,6},{5,7},{6,4},{7,5},{8,10},{9,11},{10,... | collective-permute-start | bytes 344072 | tf_op jit(solution)/shard_map/ppermute | solution.py:32
  19.1 6.2 %collective-permute-start.6 = (bf16[272,128]{1,0:T(8,128)(2,1)S(1)}, bf16[272,128]{1,0:T(8,128)(2,1)S(1)}, u32[]{:S(2)}, u32[]{:S(2)}) collective-permute-start(bf16[272,128]{1,0:T(8,128)(2,1)S(1)} %get-tuple-element.51.refs_1_), channel_id=1, source_target_pairs={{0,12},{4,8},{8,4},{12,0},{1,13},{5,9},{9,5},{13,1},{2,14},{6,10},... | collective-permute-start | bytes 208904 | tf_op jit(solution)/shard_map/ppermute | solution.py:32
  21.9 6.2 %collective-permute-start.10 = (bf16[272,128]{1,0:T(8,128)(2,1)S(1)}, bf16[272,128]{1,0:T(8,128)(2,1)S(1)}, u32[]{:S(2)}, u32[]{:S(2)}) collective-permute-start(bf16[272,128]{1,0:T(8,128)(2,1)S(1)} %get-tuple-element.51.refs_1_), channel_id=1, source_target_pairs={{0,8},{4,12},{8,0},{12,4},{1,9},{5,13},{9,1},{13,5},{2,10},{6,14},... | collective-permute-start | bytes 208904 | tf_op jit(solution)/shard_map/ppermute | solution.py:32
  22.3 5.9 %collective-permute-start.9 = (bf16[272,128]{1,0:T(8,128)(2,1)S(1)}, bf16[272,128]{1,0:T(8,128)(2,1)S(1)}, u32[]{:S(2)}, u32[]{:S(2)}) collective-permute-start(bf16[272,128]{1,0:T(8,128)(2,1)S(1)} %get-tuple-element.51.refs_1_), channel_id=1, source_target_pairs={{0,4},{4,0},{8,12},{12,8},{1,5},{5,1},{9,13},{13,9},{2,6},{6,2},{1... | collective-permute-start | bytes 208904 | tf_op jit(solution)/shard_map/ppermute | solution.py:32
  23.6 9.1 %collective-permute-start.15 = (bf16[256,128]{1,0:T(8,128)(2,1)S(1)}, bf16[256,128]{1,0:T(8,128)(2,1)S(1)}, u32[]{:S(2)}, u32[]{:S(2)}) collective-permute-start(bf16[256,128]{1,0:T(8,128)(2,1)S(1)} %slice.16), channel_id=1, source_target_pairs={{0,4},{4,0},{8,12},{12,8},{1,5},{5,1},{9,13},{13,9},{2,6},{6,2},{1... | collective-permute-start | bytes 196616 | tf_op jit(solution)/shard_map/ppermute | solution.py:32
  25.3 4.4 %collective-permute-start.13 = (bf16[64,256]{1,0:T(8,128)(2,1)S(1)}, bf16[64,256]{1,0:T(8,128)(2,1)S(1)}, u32[]{:S(2)}, u32[]{:S(2)}) collective-permute-start(bf16[64,256]{1,0:T(8,128)(2,1)S(1)} %get-tuple-element.60), channel_id=1, source_target_pairs={{0,2},{1,3},{2,0},{3,1},{4,6},{5,7},{6,4},{7,5},{8,10},{9,11},{10,... | collective-permute-start | bytes 98312 | tf_op jit(solution)/shard_map/ppermute | solution.py:32
  26.9 5.8 %collective-permute-start.8 = (bf16[128,256]{1,0:T(8,128)(2,1)S(1)}, bf16[128,256]{1,0:T(8,128)(2,1)S(1)}, u32[]{:S(2)}, u32[]{:S(2)}) collective-permute-start(bf16[128,256]{1,0:T(8,128)(2,1)S(1)} %slice.20), channel_id=1, source_target_pairs={{0,2},{1,3},{2,0},{3,1},{4,6},{5,7},{6,4},{7,5},{8,10},{9,11},{10,... | collective-permute-start | bytes 196616 | tf_op jit(solution)/shard_map/ppermute | solution.py:32
  28.2 4.4 %collective-permute-start.11 = (bf16[272,128]{1,0:T(8,128)(2,1)S(1)}, bf16[272,128]{1,0:T(8,128)(2,1)S(1)}, u32[]{:S(2)}, u32[]{:S(2)}) collective-permute-start(bf16[272,128]{1,0:T(8,128)(2,1)S(1)} %shard_map.153), channel_id=1, source_target_pairs={{0,2},{1,3},{2,0},{3,1},{4,6},{5,7},{6,4},{7,5},{8,10},{9,11},{10,... | collective-permute-start | bytes 208904 | tf_op jit(solution)/shard_map/ppermute | solution.py:32
  29.8 3.8 %collective-permute-start.14 = (bf16[128,256]{1,0:T(8,128)(2,1)S(1)}, bf16[128,256]{1,0:T(8,128)(2,1)S(1)}, u32[]{:S(2)}, u32[]{:S(2)}) collective-permute-start(bf16[128,256]{1,0:T(8,128)(2,1)S(1)} %constant_dynamic-update-slice_fusion.refs_2_), channel_id=1, source_target_pairs={{0,1},{1,0},{2,3},{3,2},{4,5},{5,4},{6,7},{7,6},{8,9},{9,8},{10,11... | collective-permute-start | bytes 196616 | tf_op jit(solution)/shard_map/ppermute | solution.py:32
  32.6 1.4 %collective-permute-start.12 = (bf16[544,128]{1,0:T(8,128)(2,1)S(1)}, bf16[544,128]{1,0:T(8,128)(2,1)S(1)}, u32[]{:S(2)}, u32[]{:S(2)}) collective-permute-start(bf16[544,128]{1,0:T(8,128)(2,1)S(1)} %pad_maximum_fusion.refs_0_), channel_id=1, source_target_pairs={{0,1},{1,0},{2,3},{3,2},{4,5},{5,4},{6,7},{7,6},{8,9},{9,8},{10,11... | collective-permute-start | bytes 417800 | tf_op jit(solution)/shard_map/ppermute | solution.py:32

commit v9 on v6

--- a/solution.py
+++ b/solution.py
@@ -107,7 +107,7 @@
     inverse[...] = 1.0 / jnp.broadcast_to(counts, (nodes, nodes)).T
     counts = jnp.sum(own.astype(F32) * counts, axis=1, keepdims=True)
     known[:, width:] = jnp.broadcast_to(counts, (slots, 128)).astype(BF16)
-    for copy in copies[3:]:
+    for copy in copies[3:7]:
         copy.wait()
     for k in range(tiles.shape[2]):
 
@@ -119,6 +119,8 @@
     for s in range(rows):
         block = dot(picks[...], adjacency[s]).astype(BF16)
         (far if s // 2 else near)[s % 2 * slots : (s % 2 + 1) * slots, :] = block
+    for copy in copies[7:]:
+        copy.wait()
 
 
 def block_of(step, near, far, slots):

time: 35.5 us -> 35.4 us (level)
  no operation moved by 1% of the time
where the time goes in v9:
time: 35.4 us; the launch traced here: 35.3 us
  starting transfers between devices  19.4 us (55%)
  waiting for transfers between devices  9.21 us (26%)
  Pallas kernels  5.11 us (14%)
  between operations  1.41 us (4%)
    ppermute x16, starting transfers between devices, trade(): lax.ppermute(block, axis, [(i, i ^ step) for i in range(lax.axis_size(axi...  19.4 us
    ppermute x16, waiting for transfers between devices, trade(): lax.ppermute(block, axis, [(i, i ^ step) for i in range(lax.axis_size(axi...  9.21 us
    pallas_call x9, Pallas kernels, call(): pl.pallas_call(kernel, out_shape=[jax.ShapeDtypeStruct(shape, dtype) for...  5.11 us
  transfers between devices with their start and end apart: 16, of which 8 were waited for; matrix products, arithmetic and copies ran while one was open for 0% of the time, Pallas kernels for 11%

profile of v9, /device:TPU:0, one launch (start us, length us, event | category | flops | bytes accessed | tf_op | source)
XLA Modules:
  0.0 35.3 jit_solution(11785987294934382163)
XLA Ops:
  0.6 5.1 %collective-permute-start = (bf16[128,256]{1,0:T(8,128)(2,1)}, bf16[128,256]{1,0:T(8,128)(2,1)S(1)}, u32[]{:S(2)}, u32[]{:S(2)}) collective-permute-start(bf16[128,256]{1,0:T(8,128)(2,1)} %refs_3_.1), channel_id=1, source_target_pairs={{0,12},{4,8},{8,4},{12,0},{1,13},{5,9},{9,5},{13,1},{2,14},{6,10},... | collective-permute-start | bytes 196616 | tf_op jit(solution)/shard_map/ppermute | solution.py:32
  5.8 0.0 collective-permute-start.2
  5.8 0.6 %collective-permute-start.1 = (bf16[128,256]{1,0:T(8,128)(2,1)}, bf16[128,256]{1,0:T(8,128)(2,1)S(1)}, u32[]{:S(2)}, u32[]{:S(2)}) collective-permute-start(bf16[128,256]{1,0:T(8,128)(2,1)} %refs_3_.1), channel_id=1, source_target_pairs={{0,4},{4,0},{8,12},{12,8},{1,5},{5,1},{9,13},{13,9},{2,6},{6,2},{1... | collective-permute-start | bytes 196616 | tf_op jit(solution)/shard_map/ppermute | solution.py:32
  7.0 1.9 %shard_map.146 = (bf16[4,512,128]{2,1,0:T(8,128)(2,1)S(1)}, bf16[256,512]{1,0:T(8,128)(2,1)S(1)}, bf16[128,256]{1,0:T(8,128)(2,1)S(1)}, bf16[256,384]{1,0:T(8,12...) custom-call(s32[1,256]{1,0:T(1,128)} %bitcast.4, ...), custom_call_target="tpu_custom_call" | custom-call | tf_op jit(solution)/shard_map/pallas_call | solution.py:56
  8.9 2.3 %collective-permute-start.5 = (bf16[512,128]{1,0:T(8,128)(2,1)S(1)}, bf16[512,128]{1,0:T(8,128)(2,1)S(1)}, u32[]{:S(2)}, u32[]{:S(2)}) collective-permute-start(bf16[512,128]{1,0:T(8,128)(2,1)S(1)} %get-tuple-element.40.refs_5_), channel_id=1, source_target_pairs={{0,8},{4,12},{8,0},{12,4},{1,9},{5,13},{9,1},{13,5},{2,10},{6,14},... | collective-permute-start | bytes 393224 | tf_op jit(solution)/shard_map/ppermute | solution.py:32
  11.3 0.0 collective-permute-done.refs_0_
  11.3 0.3 collective-permute-done.2.refs_2_
  11.6 0.0 collective-permute-done.1.refs_1_
  11.6 0.4 %shard_map.147 = (bf16[128,896]{1,0:T(8,128)(2,1)S(1)}, f32[128,256]{1,0:T(8,128)S(1)}, bf16[128,640]{1,0:T(8,128)(2,1)S(1)}) custom-call(bf16[256,512]{1,0:T(8,128)(2,1)S(1)} %get-tuple-element.37.column_picks, bf16[256,384]{1,0:T(8,128)(2,1)S(1)} %get-tuple-element.38.known, bf16[128,256]{1,0:T(8,128)(2,1)S(1)} %collective-permute-done.refs_0_, ...), custom_call_target="tpu_custom_call" | custom-call | tf_op jit(solution)/shard_map/pallas_call | solution.py:56
  12.0 0.1 collective-permute-start.3
  12.1 0.4 %shard_map.151 = (f32[256,256]{1,0:T(8,128)S(1)}, bf16[256,256]{1,0:T(8,128)(2,1)S(1)}) custom-call(bf16[4,512,128]{2,1,0:T(8,128)(2,1)S(1)} %get-tuple-element.54.adjacency, bf16[128,256]{1,0:T(8,128)(2,1)S(1)} %collective-permute-done.refs_0_, bf16[128,256]{1,0:T(8,128)(2,1)S(1)} %collective-permute-done.1.refs_1_, ...), custom_call_target="tpu_custom_call" | custom-call | flops 3000000000 | tf_op jit(solution)/shard_map/pallas_call | solution.py:56
  12.5 0.6 %collective-permute-start.7 = (bf16[256,256]{1,0:T(8,128)(2,1)S(1)}, bf16[256,256]{1,0:T(8,128)(2,1)S(1)}, u32[]{:S(2)}, u32[]{:S(2)}) collective-permute-start(bf16[256,256]{1,0:T(8,128)(2,1)S(1)} %get-tuple-element.56), channel_id=1, source_target_pairs={{0,1},{1,0},{2,3},{3,2},{4,5},{5,4},{6,7},{7,6},{8,9},{9,8},{10,11... | collective-permute-start | bytes 393224 | tf_op jit(solution)/shard_map/ppermute | solution.py:32
  13.1 0.5 %collective-permute-done.3.got = bf16[128,896]{1,0:T(8,128)(2,1)S(1)} collective-permute-done((bf16[128,896]{1,0:T(8,128)(2,1)S(1)}, bf16[128,896]{1,0:T(8,128)(2,1)S(1)}, u32[]{:S(2)}, u32[]{:S(2)}) %collective-permute-start.3) | collective-permute-done | bytes 229408 | tf_op jit(solution)/shard_map/ppermute | solution.py:32
  13.6 1.6 %collective-permute-start.4 = (bf16[64,896]{1,0:T(8,128)(2,1)S(1)}, bf16[64,896]{1,0:T(8,128)(2,1)S(1)}, u32[]{:S(2)}, u32[]{:S(2)}) collective-permute-start(bf16[64,896]{1,0:T(8,128)(2,1)S(1)} %get-tuple-element.46), channel_id=1, source_target_pairs={{0,2},{1,3},{2,0},{3,1},{4,6},{5,7},{6,4},{7,5},{8,10},{9,11},{10,... | collective-permute-start | bytes 344072 | tf_op jit(solution)/shard_map/ppermute | solution.py:32
  15.1 2.2 %collective-permute-done.5 = bf16[512,128]{1,0:T(8,128)(2,1)S(1)} collective-permute-done((bf16[512,128]{1,0:T(8,128)(2,1)S(1)}, bf16[512,128]{1,0:T(8,128)(2,1)S(1)}, u32[]{:S(2)}, u32[]{:S(2)}) %collective-permute-start.5) | collective-permute-done | bytes 131104 | tf_op jit(solution)/shard_map/ppermute | solution.py:32
  17.4 1.4 %collective-permute-done.4.got = bf16[64,896]{1,0:T(8,128)(2,1)S(1)} collective-permute-done((bf16[64,896]{1,0:T(8,128)(2,1)S(1)}, bf16[64,896]{1,0:T(8,128)(2,1)S(1)}, u32[]{:S(2)}, u32[]{:S(2)}) %collective-permute-start.4) | collective-permute-done | bytes 114720 | tf_op jit(solution)/shard_map/ppermute | solution.py:32
  18.8 0.2 shard_map.149
  19.1 2.8 %collective-permute-start.6 = (bf16[272,128]{1,0:T(8,128)(2,1)S(1)}, bf16[272,128]{1,0:T(8,128)(2,1)S(1)}, u32[]{:S(2)}, u32[]{:S(2)}) collective-permute-start(bf16[272,128]{1,0:T(8,128)(2,1)S(1)} %get-tuple-element.51.refs_1_), channel_id=1, source_target_pairs={{0,12},{4,8},{8,4},{12,0},{1,13},{5,9},{9,5},{13,1},{2,14},{6,10},... | collective-permute-start | bytes 208904 | tf_op jit(solution)/shard_map/ppermute | solution.py:32
  21.9 0.0 collective-permute-done.7
  21.9 0.5 %collective-permute-start.10 = (bf16[272,128]{1,0:T(8,128)(2,1)S(1)}, bf16[272,128]{1,0:T(8,128)(2,1)S(1)}, u32[]{:S(2)}, u32[]{:S(2)}) collective-permute-start(bf16[272,128]{1,0:T(8,128)(2,1)S(1)} %get-tuple-element.51.refs_1_), channel_id=1, source_target_pairs={{0,8},{4,12},{8,0},{12,4},{1,9},{5,13},{9,1},{13,5},{2,10},{6,14},... | collective-permute-start | bytes 208904 | tf_op jit(solution)/shard_map/ppermute | solution.py:32
  22.4 1.2 %collective-permute-start.9 = (bf16[272,128]{1,0:T(8,128)(2,1)S(1)}, bf16[272,128]{1,0:T(8,128)(2,1)S(1)}, u32[]{:S(2)}, u32[]{:S(2)}) collective-permute-start(bf16[272,128]{1,0:T(8,128)(2,1)S(1)} %get-tuple-element.51.refs_1_), channel_id=1, source_target_pairs={{0,4},{4,0},{8,12},{12,8},{1,5},{5,1},{9,13},{13,9},{2,6},{6,2},{1... | collective-permute-start | bytes 208904 | tf_op jit(solution)/shard_map/ppermute | solution.py:32
  23.6 0.8 %collective-permute-start.15 = (bf16[256,128]{1,0:T(8,128)(2,1)S(1)}, bf16[256,128]{1,0:T(8,128)(2,1)S(1)}, u32[]{:S(2)}, u32[]{:S(2)}) collective-permute-start(bf16[256,128]{1,0:T(8,128)(2,1)S(1)} %slice.16), channel_id=1, source_target_pairs={{0,4},{4,0},{8,12},{12,8},{1,5},{5,1},{9,13},{13,9},{2,6},{6,2},{1... | collective-permute-start | bytes 196616 | tf_op jit(solution)/shard_map/ppermute | solution.py:32
  24.4 0.9 %collective-permute-done.6.refs_0_ = bf16[272,128]{1,0:T(8,128)(2,1)S(1)} collective-permute-done((bf16[272,128]{1,0:T(8,128)(2,1)S(1)}, bf16[272,128]{1,0:T(8,128)(2,1)S(1)}, u32[]{:S(2)}, u32[]{:S(2)}) %collective-permute-start.6) | collective-permute-done | bytes 69664 | tf_op jit(solution)/shard_map/ppermute | solution.py:32
  25.3 1.6 %collective-permute-start.13 = (bf16[64,256]{1,0:T(8,128)(2,1)S(1)}, bf16[64,256]{1,0:T(8,128)(2,1)S(1)}, u32[]{:S(2)}, u32[]{:S(2)}) collective-permute-start(bf16[64,256]{1,0:T(8,128)(2,1)S(1)} %get-tuple-element.60), channel_id=1, source_target_pairs={{0,2},{1,3},{2,0},{3,1},{4,6},{5,7},{6,4},{7,5},{8,10},{9,11},{10,... | collective-permute-start | bytes 98312 | tf_op jit(solution)/shard_map/ppermute | solution.py:32
  26.9 0.6 %collective-permute-start.8 = (bf16[128,256]{1,0:T(8,128)(2,1)S(1)}, bf16[128,256]{1,0:T(8,128)(2,1)S(1)}, u32[]{:S(2)}, u32[]{:S(2)}) collective-permute-start(bf16[128,256]{1,0:T(8,128)(2,1)S(1)} %slice.20), channel_id=1, source_target_pairs={{0,2},{1,3},{2,0},{3,1},{4,6},{5,7},{6,4},{7,5},{8,10},{9,11},{10,... | collective-permute-start | bytes 196616 | tf_op jit(solution)/shard_map/ppermute | solution.py:32
  27.5 0.7 %collective-permute-done.10.refs_1_ = bf16[272,128]{1,0:T(8,128)(2,1)S(1)} collective-permute-done((bf16[272,128]{1,0:T(8,128)(2,1)S(1)}, bf16[272,128]{1,0:T(8,128)(2,1)S(1)}, u32[]{:S(2)}, u32[]{:S(2)}) %collective-permute-start.10) | collective-permute-done | bytes 69664 | tf_op jit(solution)/shard_map/ppermute | solution.py:32
  28.2 0.0 collective-permute-done.9.refs_0_
  28.3 1.6 %collective-permute-start.11 = (bf16[272,128]{1,0:T(8,128)(2,1)S(1)}, bf16[272,128]{1,0:T(8,128)(2,1)S(1)}, u32[]{:S(2)}, u32[]{:S(2)}) collective-permute-start(bf16[272,128]{1,0:T(8,128)(2,1)S(1)} %shard_map.153), channel_id=1, source_target_pairs={{0,2},{1,3},{2,0},{3,1},{4,6},{5,7},{6,4},{7,5},{8,10},{9,11},{10,... | collective-permute-start | bytes 208904 | tf_op jit(solution)/shard_map/ppermute | solution.py:32
  29.8 0.0 collective-permute-done.13
  29.8 0.0 collective-permute-start.14
  29.9 2.8 %collective-permute-done.11 = bf16[272,128]{1,0:T(8,128)(2,1)S(1)} collective-permute-done((bf16[272,128]{1,0:T(8,128)(2,1)S(1)}, bf16[272,128]{1,0:T(8,128)(2,1)S(1)}, u32[]{:S(2)}, u32[]{:S(2)}) %collective-permute-start.11) | collective-permute-done | bytes 69664 | tf_op jit(solution)/shard_map/ppermute | solution.py:32
  32.6 0.1 collective-permute-start.12
  32.7 0.0 collective-permute-done.15
  32.8 0.0 collective-permute-done.8.got
  32.8 0.9 %shard_map.152 = bf16[128,256]{1,0:T(8,128)(2,1)} custom-call(bf16[128,256]{1,0:T(8,128)(2,1)S(1)} %get-tuple-element.36.refs_3_.features, f32[128,256]{1,0:T(8,128)S(1)} %slice.13.total, bf16[128,256]{1,0:T(8,128)(2,1)S(1)} %collective-permute-done.8.got, f32[128,128]{1,0:T(8,128)S(1)} %get-tuple-element.58.inverse, ...), custom_call_target="tpu_custom_call" | custom-call | tf_op jit(solution)/shard_map/pallas_call | solution.py:56
  33.6 0.0 collective-permute-done.14.refs_3_
  33.6 0.4 %collective-permute-done.12.refs_1_ = bf16[544,128]{1,0:T(8,128)(2,1)S(1)} collective-permute-done((bf16[544,128]{1,0:T(8,128)(2,1)S(1)}, bf16[544,128]{1,0:T(8,128)(2,1)S(1)}, u32[]{:S(2)}, u32[]{:S(2)}) %collective-permute-start.12) | collective-permute-done | bytes 139296 | tf_op jit(solution)/shard_map/ppermute | solution.py:32
  34.1 1.2 %shard_map.154 = (bf16[128,256]{1,0:T(8,128)(2,1)}, f32[256,256]{1,0:T(8,128)}, f32[256,256]{1,0:T(8,128)}, f32[1,256]{1,0:T(1,128)}) custom-call(bf16[544,128]{1,0:T(8,128)(2,1)S(1)} %pad_maximum_fusion.refs_0_, bf16[544,128]{1,0:T(8,128)(2,1)S(1)} %collective-permute-done.12.refs_1_, bf16[128,256]{1,0:T(8,128)(2,1)S(1)} %constant_dynamic-update-slice_fusion.refs_2_, ...), custom_call_target="tpu_custom_call" | custom-call | tf_op jit(solution)/shard_map/pallas_call | solution.py:56
  (12 shorter events, 0.2 us)
Async XLA Ops:
  0.6 10.6 %collective-permute-start = (bf16[128,256]{1,0:T(8,128)(2,1)}, bf16[128,256]{1,0:T(8,128)(2,1)S(1)}, u32[]{:S(2)}, u32[]{:S(2)}) collective-permute-start(bf16[128,256]{1,0:T(8,128)(2,1)} %refs_3_.1), channel_id=1, source_target_pairs={{0,12},{4,8},{8,4},{12,0},{1,13},{5,9},{9,5},{13,1},{2,14},{6,10},... | collective-permute-start | bytes 196616 | tf_op jit(solution)/shard_map/ppermute | solution.py:32
  5.8 5.8 %collective-permute-start.2 = (bf16[128,256]{1,0:T(8,128)(2,1)}, bf16[128,256]{1,0:T(8,128)(2,1)S(1)}, u32[]{:S(2)}, u32[]{:S(2)}) collective-permute-start(bf16[128,256]{1,0:T(8,128)(2,1)} %refs_3_.1), channel_id=1, source_target_pairs={{0,8},{4,12},{8,0},{12,4},{1,9},{5,13},{9,1},{13,5},{2,10},{6,14},... | collective-permute-start | bytes 196616 | tf_op jit(solution)/shard_map/ppermute | solution.py:32
  5.8 5.8 %collective-permute-start.1 = (bf16[128,256]{1,0:T(8,128)(2,1)}, bf16[128,256]{1,0:T(8,128)(2,1)S(1)}, u32[]{:S(2)}, u32[]{:S(2)}) collective-permute-start(bf16[128,256]{1,0:T(8,128)(2,1)} %refs_3_.1), channel_id=1, source_target_pairs={{0,4},{4,0},{8,12},{12,8},{1,5},{5,1},{9,13},{13,9},{2,6},{6,2},{1... | collective-permute-start | bytes 196616 | tf_op jit(solution)/shard_map/ppermute | solution.py:32
  8.9 8.4 %collective-permute-start.5 = (bf16[512,128]{1,0:T(8,128)(2,1)S(1)}, bf16[512,128]{1,0:T(8,128)(2,1)S(1)}, u32[]{:S(2)}, u32[]{:S(2)}) collective-permute-start(bf16[512,128]{1,0:T(8,128)(2,1)S(1)} %get-tuple-element.40.refs_5_), channel_id=1, source_target_pairs={{0,8},{4,12},{8,0},{12,4},{1,9},{5,13},{9,1},{13,5},{2,10},{6,14},... | collective-permute-start | bytes 393224 | tf_op jit(solution)/shard_map/ppermute | solution.py:32
  12.0 1.6 %collective-permute-start.3 = (bf16[128,896]{1,0:T(8,128)(2,1)S(1)}, bf16[128,896]{1,0:T(8,128)(2,1)S(1)}, u32[]{:S(2)}, u32[]{:S(2)}) collective-permute-start(bf16[128,896]{1,0:T(8,128)(2,1)S(1)} %get-tuple-element.43), channel_id=1, source_target_pairs={{0,1},{1,0},{2,3},{3,2},{4,5},{5,4},{6,7},{7,6},{8,9},{9,8},{10,11... | collective-permute-start | bytes 688136 | tf_op jit(solution)/shard_map/ppermute | solution.py:32
  12.5 9.4 %collective-permute-start.7 = (bf16[256,256]{1,0:T(8,128)(2,1)S(1)}, bf16[256,256]{1,0:T(8,128)(2,1)S(1)}, u32[]{:S(2)}, u32[]{:S(2)}) collective-permute-start(bf16[256,256]{1,0:T(8,128)(2,1)S(1)} %get-tuple-element.56), channel_id=1, source_target_pairs={{0,1},{1,0},{2,3},{3,2},{4,5},{5,4},{6,7},{7,6},{8,9},{9,8},{10,11... | collective-permute-start | bytes 393224 | tf_op jit(solution)/shard_map/ppermute | solution.py:32
  13.6 5.3 %collective-permute-start.4 = (bf16[64,896]{1,0:T(8,128)(2,1)S(1)}, bf16[64,896]{1,0:T(8,128)(2,1)S(1)}, u32[]{:S(2)}, u32[]{:S(2)}) collective-permute-start(bf16[64,896]{1,0:T(8,128)(2,1)S(1)} %get-tuple-element.46), channel_id=1, source_target_pairs={{0,2},{1,3},{2,0},{3,1},{4,6},{5,7},{6,4},{7,5},{8,10},{9,11},{10,... | collective-permute-start | bytes 344072 | tf_op jit(solution)/shard_map/ppermute | solution.py:32
  19.1 6.2 %collective-permute-start.6 = (bf16[272,128]{1,0:T(8,128)(2,1)S(1)}, bf16[272,128]{1,0:T(8,128)(2,1)S(1)}, u32[]{:S(2)}, u32[]{:S(2)}) collective-permute-start(bf16[272,128]{1,0:T(8,128)(2,1)S(1)} %get-tuple-element.51.refs_1_), channel_id=1, source_target_pairs={{0,12},{4,8},{8,4},{12,0},{1,13},{5,9},{9,5},{13,1},{2,14},{6,10},... | collective-permute-start | bytes 208904 | tf_op jit(solution)/shard_map/ppermute | solution.py:32
  21.9 6.3 %collective-permute-start.10 = (bf16[272,128]{1,0:T(8,128)(2,1)S(1)}, bf16[272,128]{1,0:T(8,128)(2,1)S(1)}, u32[]{:S(2)}, u32[]{:S(2)}) collective-permute-start(bf16[272,128]{1,0:T(8,128)(2,1)S(1)} %get-tuple-element.51.refs_1_), channel_id=1, source_target_pairs={{0,8},{4,12},{8,0},{12,4},{1,9},{5,13},{9,1},{13,5},{2,10},{6,14},... | collective-permute-start | bytes 208904 | tf_op jit(solution)/shard_map/ppermute | solution.py:32
  22.4 5.8 %collective-permute-start.9 = (bf16[272,128]{1,0:T(8,128)(2,1)S(1)}, bf16[272,128]{1,0:T(8,128)(2,1)S(1)}, u32[]{:S(2)}, u32[]{:S(2)}) collective-permute-start(bf16[272,128]{1,0:T(8,128)(2,1)S(1)} %get-tuple-element.51.refs_1_), channel_id=1, source_target_pairs={{0,4},{4,0},{8,12},{12,8},{1,5},{5,1},{9,13},{13,9},{2,6},{6,2},{1... | collective-permute-start | bytes 208904 | tf_op jit(solution)/shard_map/ppermute | solution.py:32
  23.6 9.1 %collective-permute-start.15 = (bf16[256,128]{1,0:T(8,128)(2,1)S(1)}, bf16[256,128]{1,0:T(8,128)(2,1)S(1)}, u32[]{:S(2)}, u32[]{:S(2)}) collective-permute-start(bf16[256,128]{1,0:T(8,128)(2,1)S(1)} %slice.16), channel_id=1, source_target_pairs={{0,4},{4,0},{8,12},{12,8},{1,5},{5,1},{9,13},{13,9},{2,6},{6,2},{1... | collective-permute-start | bytes 196616 | tf_op jit(solution)/shard_map/ppermute | solution.py:32
  25.3 4.5 %collective-permute-start.13 = (bf16[64,256]{1,0:T(8,128)(2,1)S(1)}, bf16[64,256]{1,0:T(8,128)(2,1)S(1)}, u32[]{:S(2)}, u32[]{:S(2)}) collective-permute-start(bf16[64,256]{1,0:T(8,128)(2,1)S(1)} %get-tuple-element.60), channel_id=1, source_target_pairs={{0,2},{1,3},{2,0},{3,1},{4,6},{5,7},{6,4},{7,5},{8,10},{9,11},{10,... | collective-permute-start | bytes 98312 | tf_op jit(solution)/shard_map/ppermute | solution.py:32
  26.9 5.8 %collective-permute-start.8 = (bf16[128,256]{1,0:T(8,128)(2,1)S(1)}, bf16[128,256]{1,0:T(8,128)(2,1)S(1)}, u32[]{:S(2)}, u32[]{:S(2)}) collective-permute-start(bf16[128,256]{1,0:T(8,128)(2,1)S(1)} %slice.20), channel_id=1, source_target_pairs={{0,2},{1,3},{2,0},{3,1},{4,6},{5,7},{6,4},{7,5},{8,10},{9,11},{10,... | collective-permute-start | bytes 196616 | tf_op jit(solution)/shard_map/ppermute | solution.py:32
  28.3 4.4 %collective-permute-start.11 = (bf16[272,128]{1,0:T(8,128)(2,1)S(1)}, bf16[272,128]{1,0:T(8,128)(2,1)S(1)}, u32[]{:S(2)}, u32[]{:S(2)}) collective-permute-start(bf16[272,128]{1,0:T(8,128)(2,1)S(1)} %shard_map.153), channel_id=1, source_target_pairs={{0,2},{1,3},{2,0},{3,1},{4,6},{5,7},{6,4},{7,5},{8,10},{9,11},{10,... | collective-permute-start | bytes 208904 | tf_op jit(solution)/shard_map/ppermute | solution.py:32
  29.8 3.8 %collective-permute-start.14 = (bf16[128,256]{1,0:T(8,128)(2,1)S(1)}, bf16[128,256]{1,0:T(8,128)(2,1)S(1)}, u32[]{:S(2)}, u32[]{:S(2)}) collective-permute-start(bf16[128,256]{1,0:T(8,128)(2,1)S(1)} %constant_dynamic-update-slice_fusion.refs_2_), channel_id=1, source_target_pairs={{0,1},{1,0},{2,3},{3,2},{4,5},{5,4},{6,7},{7,6},{8,9},{9,8},{10,11... | collective-permute-start | bytes 196616 | tf_op jit(solution)/shard_map/ppermute | solution.py:32
  32.6 1.4 %collective-permute-start.12 = (bf16[544,128]{1,0:T(8,128)(2,1)S(1)}, bf16[544,128]{1,0:T(8,128)(2,1)S(1)}, u32[]{:S(2)}, u32[]{:S(2)}) collective-permute-start(bf16[544,128]{1,0:T(8,128)(2,1)S(1)} %pad_maximum_fusion.refs_0_), channel_id=1, source_target_pairs={{0,1},{1,0},{2,3},{3,2},{4,5},{5,4},{6,7},{7,6},{8,9},{9,8},{10,11... | collective-permute-start | bytes 417800 | tf_op jit(solution)/shard_map/ppermute | solution.py:32
